TPU v7x, 256 devices: a whole 4x4x8 slice. The times are simulated.
256 devices in a mesh: row: 8 (over z), col: 32 (over y, x, core).
Axes of the slice: x: 4, y: 4, z: 8, core: 2. Of those that a mesh axis runs over, the one named last changes fastest.
Arguments:
- features: bfloat16 [65536, 128], P(('col', 'row')), may hold values from -6 to 6
- weight: bfloat16 [128, 256], replicated, may hold values from -0.5 to 0.5
- adj_tiles: bfloat16 [8, 32, 320, 128, 128], P('row', 'col'), may hold values from -0.078125 to 0.078125
- tile_rows: int32 [8, 32, 320], P('row', 'col'), may hold values from 0 to 63, as said below
- tile_cols: int32 [8, 32, 320], P('row', 'col'), may hold values from 0 to 15
- tile_count: int32 [8, 32], P('row', 'col'), may hold values from 20 to 320, as said below
- cotangent: bfloat16 [65536, 256], P(('row', 'col')), may hold values from -6 to 6
Outputs:
- hidden: bfloat16 [65536, 256], P(('row', 'col'))
- input_grad: bfloat16 [65536, 128], P(('col', 'row'))
- weight_grad: float32 [128, 256], replicated
Inputs may be any that keep to these rules, and one draw needn't show every extreme that they name: Within one block the 320 slots name distinct tile places (tile_rows, tile_cols). `tile_count`: in every draw some block uses all 320 slots.
All inputs are finite; a program needn't handle non-finite values.
Results may differ from a plain program's by a relative error of at most 0.027.
Values may be sent and summed in bfloat16 or wider, within the bound.
No kernel may reach another device: no remote copies, remote signals or barrier semaphores. Data moves between devices by JAX's collectives and lax.ppermute only.
A program may use at most 128 MiB of HBM per device.

v0:
```python
import jax
import jax.numpy as jnp
from jax import lax
from jax.sharding import PartitionSpec as P


def run_tiles(blocks, row_list, col_list, live_count, source, row_tiles, out_tiles, forward):
    slot_total = blocks.shape[0]
    groups = slot_total // row_tiles
    live_mask = (jnp.arange(slot_total, dtype=jnp.int32) < live_count).astype(jnp.float32)

    def advance(running, slot_group):
        first_slot = slot_group * row_tiles
        block_group = lax.dynamic_slice_in_dim(blocks, first_slot, row_tiles, 0)
        row_group = lax.dynamic_slice_in_dim(row_list, first_slot, row_tiles, 0)
        col_group = lax.dynamic_slice_in_dim(col_list, first_slot, row_tiles, 0)
        mask_group = lax.dynamic_slice_in_dim(live_mask, first_slot, row_tiles, 0)
        if forward:
            picked = jnp.take(source, col_group, axis=0)
            product = jnp.einsum(
                "kij,kjf->kif", block_group, picked, preferred_element_type=jnp.float32
            )
            target = row_group
        else:
            picked = jnp.take(source, row_group, axis=0)
            product = jnp.einsum(
                "kij,kif->kjf", block_group, picked, preferred_element_type=jnp.float32
            )
            target = col_group
        product = product * mask_group[:, None, None]
        return (running + jax.ops.segment_sum(product, target, num_segments=out_tiles), None)

    initial = jnp.zeros((out_tiles, blocks.shape[1], source.shape[2]), jnp.float32)
    running, _ = lax.scan(advance, initial, jnp.arange(groups, dtype=jnp.int32))
    return running


def gelu_parts(aggregated, weight, cotangent):
    pre_act = jnp.dot(aggregated, weight.astype(jnp.float32), precision=lax.Precision.HIGHEST)
    activated, pullback = jax.vjp(lambda values: jax.nn.gelu(values, approximate=True), pre_act)
    act_grad = pullback(cotangent.astype(jnp.float32))[0]
    return (activated, act_grad)


def per_device(features, weight, adj_tiles, tile_rows, tile_cols, tile_count, cotangent):
    own_rows, feat_width = features.shape
    row_count = lax.axis_size("row")
    col_count = lax.axis_size("col")
    tile_size = adj_tiles.shape[-1]
    row_tiles = own_rows * col_count // tile_size
    col_tiles = own_rows * row_count // tile_size
    blocks = adj_tiles[0, 0]
    row_list = tile_rows[0, 0]
    col_list = tile_cols[0, 0]
    live_count = tile_count[0, 0]
    node_total = own_rows * row_count * col_count
    x_panel = lax.all_gather(features, "row", axis=0, tiled=True).reshape(
        col_tiles, tile_size, feat_width
    )
    row_partial = run_tiles(
        blocks, row_list, col_list, live_count, x_panel, row_tiles, row_tiles, True
    )
    flat_partial = row_partial.reshape(row_tiles * tile_size, feat_width)
    block_agg = lax.psum(flat_partial.astype(jnp.bfloat16), "col").astype(jnp.float32)
    block_cot = lax.all_gather(cotangent, "col", axis=0, tiled=True)
    activated, block_act = gelu_parts(block_agg, weight, block_cot)
    first_row = lax.axis_index("col") * own_rows
    hidden = lax.dynamic_slice_in_dim(activated, first_row, own_rows, 0).astype(jnp.bfloat16)
    own_agg = lax.dynamic_slice_in_dim(block_agg, first_row, own_rows, 0)
    own_act = lax.dynamic_slice_in_dim(block_act, first_row, own_rows, 0)
    local_weight = jnp.dot(own_agg.T, own_act, precision=lax.Precision.HIGHEST)
    block_grad = jnp.dot(
        block_act.astype(jnp.bfloat16), weight.T, preferred_element_type=jnp.float32
    ).astype(jnp.bfloat16)
    weight_grad = lax.psum(local_weight, ("row", "col")) * node_total ** (-0.5)
    grad_panel = block_grad.reshape(row_tiles, tile_size, feat_width)
    col_partial = run_tiles(
        blocks, row_list, col_list, live_count, grad_panel, row_tiles, col_tiles, False
    )
    input_grad = lax.psum_scatter(
        col_partial.reshape(col_tiles * tile_size, feat_width).astype(jnp.bfloat16),
        "row",
        scatter_dimension=0,
        tiled=True,
    )
    return (hidden, input_grad, weight_grad)


def solution(mesh):
    placed = (
        P(("col", "row"), None),
        P(),
        P("row", "col", None, None, None),
        P("row", "col", None),
        P("row", "col", None),
        P("row", "col"),
        P(("row", "col"), None),
    )
    return jax.shard_map(
        per_device,
        mesh=mesh,
        in_specs=placed,
        out_specs=(P(("row", "col"), None), P(("col", "row"), None), P()),
        check_vma=False,
    )
```

profile of v0, /device:TPU:1, one launch (start us, length us, event | category | flops | bytes accessed | tf_op | source)
XLA Modules:
  0.0 613.4 jit_solution(7937668915316633790)
XLA Ops:
  7.2 0.7 reduce
  7.9 0.7 reduce.1
  8.6 24.0 %all_gather.6 = bf16[2048,128]{1,0:T(8,128)(2,1)S(1)} all-gather(bf16[256,128]{1,0:T(8,128)(2,1)} %param.11), channel_id=1, replica_groups=mesh['row'=8,'col'=32] {'row'}, dimensions={0}, use_global_device_ids=true | all-gather | bytes 589824 | tf_op jit(solution)/shard_map/all_gather | solution.py:57
  33.3 2.5 broadcast.29
  35.7 101.2 %while.20 = (s32[]{:T(128)}, f32[64,128,128]{2,1,0:T(8,128)}, s32[5]{0:T(128)S(1)}, s32[320]{0:T(512)S(1)}, bf16[320,128,128]{2,1,0:T(8,128)(2,1)}, /*index=5*/s...) while((s32[]{:T(128)}, f32[64,128,128]{2,1,0:T(8,128)}, ...), condition=%wide.region_2.3_spmd, body=%wide.region_0.2_spmd.sunk | while | flops 271582592 | bytes 25172808 | solution.py:34
  37.2 1.0 gather_fusion
  38.2 4.3 convolution_multiply_fusion.4
  42.5 13.4 %scatter_fusion = f32[64,128,128]{2,1,0:T(8,128)} fusion(f32[64,128,128]{2,1,0:T(8,128)} %get-tuple-element.255, s32[64]{0:T(128)S(1)} %dynamic_slice.71, f32[64,128,128]{2,1,0:T(8,128)} %convolution_multiply_fusion.4), kind=kCustom, calls=%fused_computation.2.clone.1 | custom fusion | flops 1048576 | bytes 12583168 | tf_op jit(solution)/shard_map/while/body/eval_jaxpr/scatter-add | solution.py:31
  57.4 1.0 gather_fusion
  58.4 4.3 convolution_multiply_fusion.4
  62.7 13.5 %scatter_fusion = f32[64,128,128]{2,1,0:T(8,128)} fusion(f32[64,128,128]{2,1,0:T(8,128)} %get-tuple-element.255, s32[64]{0:T(128)S(1)} %dynamic_slice.71, f32[64,128,128]{2,1,0:T(8,128)} %convolution_multiply_fusion.4), kind=kCustom, calls=%fused_computation.2.clone.1 | custom fusion | flops 1048576 | bytes 12583168 | tf_op jit(solution)/shard_map/while/body/eval_jaxpr/scatter-add | solution.py:31
  77.7 1.0 gather_fusion
  78.6 4.3 convolution_multiply_fusion.4
  82.9 13.4 %scatter_fusion = f32[64,128,128]{2,1,0:T(8,128)} fusion(f32[64,128,128]{2,1,0:T(8,128)} %get-tuple-element.255, s32[64]{0:T(128)S(1)} %dynamic_slice.71, f32[64,128,128]{2,1,0:T(8,128)} %convolution_multiply_fusion.4), kind=kCustom, calls=%fused_computation.2.clone.1 | custom fusion | flops 1048576 | bytes 12583168 | tf_op jit(solution)/shard_map/while/body/eval_jaxpr/scatter-add | solution.py:31
  97.9 1.0 gather_fusion
  98.8 4.3 convolution_multiply_fusion.4
  103.1 13.5 %scatter_fusion = f32[64,128,128]{2,1,0:T(8,128)} fusion(f32[64,128,128]{2,1,0:T(8,128)} %get-tuple-element.255, s32[64]{0:T(128)S(1)} %dynamic_slice.71, f32[64,128,128]{2,1,0:T(8,128)} %convolution_multiply_fusion.4), kind=kCustom, calls=%fused_computation.2.clone.1 | custom fusion | flops 1048576 | bytes 12583168 | tf_op jit(solution)/shard_map/while/body/eval_jaxpr/scatter-add | solution.py:31
  118.1 1.0 gather_fusion
  119.1 4.3 convolution_multiply_fusion.4
  123.4 13.5 %scatter_fusion = f32[64,128,128]{2,1,0:T(8,128)} fusion(f32[64,128,128]{2,1,0:T(8,128)} %get-tuple-element.255, s32[64]{0:T(128)S(1)} %dynamic_slice.71, f32[64,128,128]{2,1,0:T(8,128)} %convolution_multiply_fusion.4), kind=kCustom, calls=%fused_computation.2.clone.1 | custom fusion | flops 1048576 | bytes 12583168 | tf_op jit(solution)/shard_map/while/body/eval_jaxpr/scatter-add | solution.py:31
  136.9 3.9 convert_element_type.31
  141.6 14.4 %copy.10 = bf16[1,1,320,128,128]{3,4,2,1,0:T(8,128)(2,1)} copy(bf16[1,1,320,128,128]{4,3,2,1,0:T(8,128)(2,1)} %bitcast.20) | data formatting | bytes 20971520 | tf_op args[2]
  156.0 108.1 %all-reduce.3.cloned.1.call-done = bf16[8192,128]{1,0:T(8,128)(2,1)} async-done(((bf16[8192,128]{1,0:T(8,128)(2,1)}), bf16[8192,128]{1,0:T(8,128)(2,1)}) %all-reduce.3.cloned.1.call-update) | async-done | bytes 2097168 | tf_op jit(solution)/shard_map/psum | solution.py:64
  264.0 54.0 %all-gather.2.cloned.1.call-done = bf16[8192,256]{1,0:T(8,128)(2,1)} async-done(((bf16[256,256]{1,0:T(8,128)(2,1)}), bf16[8192,256]{1,0:T(8,128)(2,1)}) %all-gather.2.cloned.1.call-update) | async-done | bytes 4194320 | tf_op jit(solution)/shard_map/all_gather | solution.py:65
  318.0 11.5 %fusion.13 = (f32[8192,256]{1,0:T(8,128)S(1)}, f32[8192,256]{1,0:T(8,128)}, f32[8192,256]{1,0:T(8,128)}) fusion(bf16[8192,256]{1,0:T(8,128)(2,1)} %all-gather.2.cloned.1.call-done, bf16[8192,128]{1,0:T(8,128)(2,1)} %all-reduce.3.cloned.1.call-done, bf16[128,256]{1,0:T(8,128)(2,1)S(1)} %copy-done), kind=kOutput, calls=%fused_computation.30 | convolution fusion | flops 578813952 | bytes 31522816 | tf_op jit(solution)/shard_map/dot_general | solution.py:39
  329.5 2.6 convolution_convert_fusion
  332.1 1.8 fusion.23
  334.0 86.6 %while.21 = (s32[]{:T(128)}, f32[16,128,128]{2,1,0:T(8,128)S(1)}, s32[5]{0:T(128)S(1)}, s32[320]{0:T(512)S(1)}, bf16[320,128,128]{1,2,0:T(8,128)(2,1)}, /*index=...) while((s32[]{:T(128)}, f32[16,128,128]{2,1,0:T(8,128)S(1)}, ...), condition=%wide.region_6.7_spmd, body=%wide.region_4.6_spmd.sunk | while | flops 271582592 | bytes 25172808 | solution.py:34
  335.5 2.5 gather_fusion.1
  338.1 4.5 convolution_multiply_fusion.5
  342.5 8.8 %scatter_fusion.1 = f32[16,128,128]{2,1,0:T(8,128)S(1)} fusion(f32[16,128,128]{2,1,0:T(8,128)S(1)} %get-tuple-element.291, s32[64]{0:T(128)S(1)} %dynamic_slice.75, f32[64,128,128]{2,1,0:T(8,128)} %convolution_multiply_fusion.5), kind=kCustom, calls=%fused_computation.3.clone.1 | custom fusion | flops 1048576 | bytes 12583168 | tf_op jit(solution)/shard_map/while/body/eval_jaxpr/scatter-add | solution.py:31
  352.8 2.6 gather_fusion.1
  355.4 4.5 convolution_multiply_fusion.5
  359.9 8.8 %scatter_fusion.1 = f32[16,128,128]{2,1,0:T(8,128)S(1)} fusion(f32[16,128,128]{2,1,0:T(8,128)S(1)} %get-tuple-element.291, s32[64]{0:T(128)S(1)} %dynamic_slice.75, f32[64,128,128]{2,1,0:T(8,128)} %convolution_multiply_fusion.5), kind=kCustom, calls=%fused_computation.3.clone.1 | custom fusion | flops 1048576 | bytes 12583168 | tf_op jit(solution)/shard_map/while/body/eval_jaxpr/scatter-add | solution.py:31
  370.2 2.6 gather_fusion.1
  372.7 4.5 convolution_multiply_fusion.5
  377.2 8.8 %scatter_fusion.1 = f32[16,128,128]{2,1,0:T(8,128)S(1)} fusion(f32[16,128,128]{2,1,0:T(8,128)S(1)} %get-tuple-element.291, s32[64]{0:T(128)S(1)} %dynamic_slice.75, f32[64,128,128]{2,1,0:T(8,128)} %convolution_multiply_fusion.5), kind=kCustom, calls=%fused_computation.3.clone.1 | custom fusion | flops 1048576 | bytes 12583168 | tf_op jit(solution)/shard_map/while/body/eval_jaxpr/scatter-add | solution.py:31
  387.5 2.6 gather_fusion.1
  390.1 4.5 convolution_multiply_fusion.5
  394.6 8.8 %scatter_fusion.1 = f32[16,128,128]{2,1,0:T(8,128)S(1)} fusion(f32[16,128,128]{2,1,0:T(8,128)S(1)} %get-tuple-element.291, s32[64]{0:T(128)S(1)} %dynamic_slice.75, f32[64,128,128]{2,1,0:T(8,128)} %convolution_multiply_fusion.5), kind=kCustom, calls=%fused_computation.3.clone.1 | custom fusion | flops 1048576 | bytes 12583168 | tf_op jit(solution)/shard_map/while/body/eval_jaxpr/scatter-add | solution.py:31
  404.9 2.5 gather_fusion.1
  407.4 4.5 convolution_multiply_fusion.5
  411.9 8.8 %scatter_fusion.1 = f32[16,128,128]{2,1,0:T(8,128)S(1)} fusion(f32[16,128,128]{2,1,0:T(8,128)S(1)} %get-tuple-element.291, s32[64]{0:T(128)S(1)} %dynamic_slice.75, f32[64,128,128]{2,1,0:T(8,128)} %convolution_multiply_fusion.5), kind=kCustom, calls=%fused_computation.3.clone.1 | custom fusion | flops 1048576 | bytes 12583168 | tf_op jit(solution)/shard_map/while/body/eval_jaxpr/scatter-add | solution.py:31
  420.7 0.9 convert_element_type.37
  421.6 1.7 fusion.22
  423.3 150.4 %all-reduce.5.cloned.1.call-done = f32[128,256]{1,0:T(8,128)} async-done(((f32[128,256]{1,0:T(8,128)}), f32[128,256]{1,0:T(8,128)}) %all-reduce.5.cloned.1.call-update) | async-done | bytes 131088 | tf_op jit(solution)/shard_map/psum | solution.py:75
  573.8 1.6 broadcast_multiply_fusion
  575.3 31.6 %reduce-scatter.2.cloned.1.call-done = bf16[256,128]{1,0:T(8,128)(2,1)} async-done(((bf16[2048,128]{1,0:T(8,128)(2,1)}), bf16[256,128]{1,0:T(8,128)(2,1)}) %reduce-scatter.2.cloned.1.call-update) | async-done | bytes 65552 | tf_op jit(solution)/shard_map/reduce_scatter | solution.py:80
  (66 shorter events, 9.2 us)
Async XLA Ops:
  7.2 310.8 %copy-start = (bf16[128,256]{1,0:T(8,128)(2,1)S(1)}, bf16[128,256]{1,0:T(8,128)(2,1)}, u32[]{:S(2)}) copy-start(bf16[128,256]{1,0:T(8,128)(2,1)} %param.12) | copy-start | bytes 196612
  7.2 256.9 %all-reduce.3.cloned.1.call-start = ((), (), s32[]{:S(2)}) async-start(), calls=%async_computation.1 | async-start | bytes 4194304 | tf_op jit(solution)/shard_map/psum | solution.py:64
  140.8 177.2 %all-gather.2.cloned.1.call-start = ((), (), s32[]{:S(2)}) async-start(), calls=%async_computation.2 | async-start | bytes 4325376 | tf_op jit(solution)/shard_map/all_gather | solution.py:65
  141.5 432.2 %all-reduce.5.cloned.1.call-start = ((), (), s32[]{:S(2)}) async-start(), calls=%async_computation.4 | async-start | bytes 262144 | tf_op jit(solution)/shard_map/psum | solution.py:75
  333.9 273.0 %reduce-scatter.2.cloned.1.call-start = ((), (), s32[]{:S(2)}) async-start(), calls=%async_computation.3 | async-start | bytes 589824 | tf_op jit(solution)/shard_map/reduce_scatter | solution.py:80
  420.7 186.2 %copy-start.1 = (bf16[128,256]{1,0:T(8,128)(2,1)S(1)}, bf16[128,256]{1,0:T(8,128)(2,1)}, u32[]{:S(2)}) copy-start(bf16[128,256]{1,0:T(8,128)(2,1)} %param.12) | copy-start | bytes 196612
Sparse Core Ops, SparseCore 0:
  140.9 123.0 all-reduce.2
  266.6 51.3 all-gather.1
  334.0 239.7 all-reduce.4
  576.7 30.1 reduce-scatter.1
where the time goes:
time: 620 us; the launch traced here: 613 us
  waiting for transfers between devices  345 us (56%)
  other arithmetic  122 us (20%)
  matrix products  59.7 us (10%)
  local copies, waits for them, and re-layouts  41.8 us (7%)
  blocking collectives  24 us (4%)
  between operations  14.5 us (2%)
  loops' own time  6.8 us (1%)
    psum x1, waiting for transfers between devices, per_device(): weight_grad = lax.psum(local_weight, ('row', 'col')) * node_total ** (-0.5)  150 us
    scatter-add x10, other arithmetic, advance(): jax.ops.segment_sum(product, target, num_segments=out_tiles)  111 us
    psum x1, waiting for transfers between devices, per_device(): lax.psum(flat_partial.astype(jnp.bfloat16), 'col').astype(jnp.float32)  108 us
    all_gather x1, waiting for transfers between devices, per_device(): block_cot = lax.all_gather(cotangent, 'col', axis=0, tiled=True)  54 us
    reduce_scatter x1, waiting for transfers between devices, per_device(): lax.psum_scatter(col_partial.reshape(col_tiles * tile_size, feat_width).a...  31.6 us
    all_gather x1, blocking collectives, per_device(): lax.all_gather(features, 'row', axis=0, tiled=True)  24 us
    dot_general x5, matrix products, advance(): jnp.einsum('kij,kif->kjf', block_group, picked, preferred_element_type=jn...  22.3 us
    dot_general x5, matrix products, advance(): jnp.einsum('kij,kjf->kif', block_group, picked, preferred_element_type=jn...  21.5 us
  transfers between devices with their start and end apart: 4, of which 4 were waited for; matrix products, arithmetic and copies ran while one was open for 17% of the time, Pallas kernels for 0%

commit v1 on v0

v1 whole, which is shorter than its diff:
```python
import jax
import jax.numpy as jnp
from jax import lax
from jax.experimental import pallas as pl
from jax.experimental.pallas import tpu as pltpu
from jax.sharding import Mesh, PartitionSpec as P

F32, BF16 = jnp.float32, jnp.bfloat16
HIGHEST = lax.Precision.HIGHEST
UNROLL = 8
WROWS = 16
SMEM = pl.BlockSpec(memory_space=pltpu.SMEM)
VMEM = pl.BlockSpec(memory_space=pltpu.VMEM)


def in_vmem(value):
    return pltpu.with_memory_space_constraint(value, pltpu.VMEM)


def params(mebibytes):
    return pltpu.CompilerParams(vmem_limit_bytes=mebibytes * 2**20)


def forward_kernel(meta, rows, cols, tiles, panel, keep, send, acc):
    live, core = meta[0], meta[1]
    trash = acc.shape[0] - 1
    size = tiles.shape[-1]
    per_peer = keep.shape[1] // size
    acc[...] = jnp.zeros_like(acc)

    def group(step, carry):
        products, targets = [], []
        for offset in range(UNROLL):
            slot = step * UNROLL + offset
            targets.append(jnp.where(slot < live, rows[slot], trash))
            products.append(jnp.dot(tiles[slot], panel[cols[slot]], preferred_element_type=F32))
        for target, product in zip(targets, products):
            acc[target] += product
        return carry

    lax.fori_loop(0, pl.cdiv(live, UNROLL), group, 0)

    def emit(peer, carry):
        for part in range(per_peer):
            spot = pl.ds(part * size, size)
            keep[peer, spot] = acc[(2 * peer + core) * per_peer + part].astype(BF16)
            send[peer, spot] = acc[(2 * peer + 1 - core) * per_peer + part].astype(BF16)
        return carry

    lax.fori_loop(0, keep.shape[0], emit, 0)


def middle_kernel(parts, weight, cotangent, hidden, payload):
    own = hidden.shape[0]
    peers = parts.shape[0]
    feat = weight.shape[0]
    agg = parts[0].astype(F32)
    for peer in range(1, peers):
        agg += parts[peer].astype(F32)
    wide = weight[...].astype(F32)
    pre = jnp.dot(agg, wide, precision=HIGHEST, preferred_element_type=F32)
    slope, cubic = 0.7978845608028654, 0.044715
    square = pre * pre
    curve = jnp.tanh(slope * pre * (1.0 + cubic * square))
    cdf = 0.5 * (1.0 + curve)
    hidden[...] = (pre * cdf).astype(BF16)
    rate = cdf + 0.5 * pre * (1.0 - curve * curve) * (slope * (1.0 + 3.0 * cubic * square))
    act = cotangent[...].astype(F32) * rate
    local = lax.dot_general(
        agg, act, (((0,), (0,)), ((), ())), precision=HIGHEST, preferred_element_type=F32
    )
    grad = lax.dot_general(
        act.astype(BF16), weight[...], (((1,), (1,)), ((), ())), preferred_element_type=F32
    ).astype(BF16)
    per_half = feat // WROWS
    for peer in range(peers):
        payload[peer, :own] = grad
        half, chunk = divmod(peer, per_half)
        payload[peer, own:] = local[
            chunk * WROWS : (chunk + 1) * WROWS, half * feat : (half + 1) * feat
        ].astype(BF16)


def backward_kernel(meta, rows, cols, tiles, mine, other, out, grads, acc):
    live, core = meta[0], meta[1]
    size = tiles.shape[-1]
    trash = acc.shape[0] - 1
    peers = mine.shape[0]
    own = mine.shape[1] - WROWS
    per_peer = own // size
    acc[...] = jnp.zeros_like(acc)

    def place(peer, carry):
        for part in range(per_peer):
            spot = pl.ds(part * size, size)
            grads[(2 * peer + core) * per_peer + part] = mine[peer, spot]
            grads[(2 * peer + 1 - core) * per_peer + part] = other[peer, spot]
        return carry

    lax.fori_loop(0, peers, place, 0)

    def group(step, carry):
        products, targets = [], []
        for offset in range(UNROLL):
            slot = step * UNROLL + offset
            targets.append(jnp.where(slot < live, cols[slot], trash))
            products.append(
                lax.dot_general(
                    tiles[slot],
                    grads[rows[slot]],
                    (((0,), (0,)), ((), ())),
                    preferred_element_type=F32,
                )
            )
        for target, product in zip(targets, products):
            acc[target] += product
        return carry

    lax.fori_loop(0, pl.cdiv(live, UNROLL), group, 0)
    chunk = jnp.zeros((WROWS, size), F32)
    for peer in range(peers):
        chunk += mine[peer, own:].astype(F32) + other[peer, own:].astype(F32)
    for peer in range(out.shape[0]):
        for part in range(per_peer):
            out[peer, part * size : (part + 1) * size] = acc[peer * per_peer + part].astype(BF16)
        out[peer, own:] = chunk.astype(BF16)


def final_kernel(parts, grad, chunk, scale):
    total = parts[0].astype(F32)
    for peer in range(1, parts.shape[0]):
        total += parts[peer].astype(F32)
    own = grad.shape[0]
    grad[...] = total[:own].astype(BF16)
    chunk[...] = total[own:] * scale


def per_device(features, weight, adj_tiles, tile_rows, tile_cols, tile_count, cotangent):
    own, feat = features.shape
    n_row = lax.axis_size("row")
    peers = lax.axis_size("y") * lax.axis_size("x")
    slots, size = adj_tiles.shape[2], adj_tiles.shape[-1]
    row_tiles = own * peers * 2 // size
    col_tiles = own * n_row // size
    tiles = in_vmem(adj_tiles.reshape(slots, size, size))
    rows, cols = tile_rows.reshape(slots), tile_cols.reshape(slots)
    meta = jnp.stack([tile_count.reshape(()), lax.axis_index("core").astype(jnp.int32)])
    swap = [(0, 1), (1, 0)]
    yx = ("y", "x")

    spread = jnp.broadcast_to(features[None], (n_row, own, feat))
    panel = lax.all_to_all(spread, "row", 0, 0, tiled=True).reshape(col_tiles, size, feat)
    keep, send = pl.pallas_call(
        forward_kernel,
        out_shape=[jax.ShapeDtypeStruct((peers, own, feat), BF16)] * 2,
        in_specs=[SMEM, SMEM, SMEM, VMEM, VMEM],
        out_specs=[VMEM, VMEM],
        scratch_shapes=[pltpu.VMEM((row_tiles + 1, size, feat), F32)],
        compiler_params=params(24),
        name="forward",
    )(meta, rows, cols, tiles, panel)
    got = lax.ppermute(send, "core", swap)
    paired = (keep.astype(F32) + got.astype(F32)).astype(BF16)
    parts = lax.all_to_all(paired, yx, 0, 0, tiled=True)
    hidden, payload = pl.pallas_call(
        middle_kernel,
        out_shape=[
            jax.ShapeDtypeStruct(cotangent.shape, BF16),
            jax.ShapeDtypeStruct((peers, own + WROWS, feat), BF16),
        ],
        in_specs=[VMEM, VMEM, VMEM],
        out_specs=[VMEM, VMEM],
        compiler_params=params(24),
        name="middle",
    )(parts, weight, cotangent)
    mine = lax.all_to_all(payload, yx, 0, 0, tiled=True)
    other = lax.ppermute(mine, "core", swap)
    col_partial = pl.pallas_call(
        backward_kernel,
        out_shape=jax.ShapeDtypeStruct((n_row, own + WROWS, feat), BF16),
        in_specs=[SMEM, SMEM, SMEM, VMEM, VMEM, VMEM],
        out_specs=VMEM,
        scratch_shapes=[
            pltpu.VMEM((row_tiles, size, feat), BF16),
            pltpu.VMEM((col_tiles + 1, size, feat), F32),
        ],
        compiler_params=params(24),
        name="backward",
    )(meta, rows, cols, tiles, mine, other)
    shares = lax.all_to_all(col_partial, "row", 0, 0, tiled=True)
    scale = (own * n_row * peers * 2) ** -0.5

    def finish(parts_ref, grad_ref, chunk_ref):
        final_kernel(parts_ref, grad_ref, chunk_ref, scale)

    input_grad, chunk = pl.pallas_call(
        finish,
        out_shape=[
            jax.ShapeDtypeStruct((own, feat), BF16),
            jax.ShapeDtypeStruct((WROWS, feat), F32),
        ],
        in_specs=[VMEM],
        out_specs=[VMEM, VMEM],
        compiler_params=params(24),
        name="finish",
    )(shares)
    spread_chunk = jnp.broadcast_to(chunk[None], (peers, WROWS, feat))
    whole = lax.all_to_all(spread_chunk, yx, 0, 0, tiled=True).reshape(2, feat, feat)
    weight_grad = jnp.concatenate([whole[0], whole[1]], axis=1)
    return (hidden, input_grad, weight_grad)


def solution(mesh):
    side = 4
    fine = Mesh(
        mesh.devices.reshape(mesh.shape["row"], side, side, 2), ("row", "y", "x", "core")
    )
    col = ("y", "x", "core")
    placed = (
        P((*col, "row"), None),
        P(),
        P("row", col, None, None, None),
        P("row", col, None),
        P("row", col, None),
        P("row", col),
        P(("row", *col), None),
    )
    return jax.shard_map(
        per_device,
        mesh=fine,
        in_specs=placed,
        out_specs=(P(("row", *col), None), P((*col, "row"), None), P()),
        check_vma=False,
    )
```

time: 620 us -> 138 us (0.22)
  waiting for transfers between devices: 345 us -> 20.5 us
  other arithmetic: 122 us -> 2.42 us
  matrix products: 59.7 us -> 0 us
  blocking collectives: 24 us -> 81.2 us
  local copies, waits for them, and re-layouts: 41.8 us -> 5.71 us
  starting transfers between devices: 0.16 us -> 19.8 us
  between operations: 14.5 us -> 1.33 us
  loops' own time: 6.8 us -> 0 us
    psum x2 -> x0, waiting for transfers between devices: 259 us -> none  [the longest x1 150 us: per_device(): weight_grad = lax.psum(local_weight, ('row', 'col')) * node_total ** (-0.5)]
    scatter-add x10 -> x0, other arithmetic: 111 us -> none  [advance(): jax.ops.segment_sum(product, target, num_segments=out_tiles)]
    all_to_all x0 -> x4, blocking collectives: none -> 81.2 us  [the longest x1 23.6 us: per_device(): shares = lax.all_to_all(col_partial, 'row', 0, 0, tiled=True)]
    dot_general x13 -> x0, matrix products: 59.7 us -> none  [the longest x5 22.3 us: advance(): jnp.einsum('kij,kif->kjf', block_group, picked, preferred_element_type=jn...]
    all_gather x1 -> x0, waiting for transfers between devices: 54 us -> none  [per_device(): block_cot = lax.all_gather(cotangent, 'col', axis=0, tiled=True)]
    reduce_scatter x1 -> x0, waiting for transfers between devices: 31.6 us -> none  [per_device(): lax.psum_scatter(col_partial.reshape(col_tiles * tile_size, feat_width).a...]
    all_gather x1 -> x0, blocking collectives: 24 us -> none  [per_device(): lax.all_gather(features, 'row', axis=0, tiled=True)]
    gather x10 -> x0, local copies, waits for them, and re-layouts: 17.5 us -> none  [the longest x5 12.7 us: advance(): picked = jnp.take(source, row_group, axis=0)]
  transfers between devices with their start and end apart: 4 -> 3, of which waited for: 4 -> 3; matrix products, arithmetic and copies ran while one was open for 17% -> 1% of each run, Pallas kernels for 0% -> 0%
where the time goes in v1:
time: 138 us; the launch traced here: 137 us
  blocking collectives  81.2 us (59%)
  waiting for transfers between devices  20.5 us (15%)
  starting transfers between devices  19.8 us (14%)
  Pallas kernels  6.13 us (4%)
  local copies, waits for them, and re-layouts  5.71 us (4%)
  other arithmetic  2.42 us (2%)
    all_to_all x1, blocking collectives, per_device(): shares = lax.all_to_all(col_partial, 'row', 0, 0, tiled=True)  23.6 us
    all_to_all x1, blocking collectives, per_device(): parts = lax.all_to_all(paired, yx, 0, 0, tiled=True)  21 us
    all_to_all x1, blocking collectives, per_device(): mine = lax.all_to_all(payload, yx, 0, 0, tiled=True)  19.9 us
    all_to_all x1, blocking collectives, per_device(): lax.all_to_all(spread_chunk, yx, 0, 0, tiled=True).reshape(2, feat, feat)  16.6 us
    all_to_all x1, waiting for transfers between devices, per_device(): lax.all_to_all(spread, 'row', 0, 0, tiled=True)  15.8 us
    all_to_all x1, starting transfers between devices, per_device(): lax.all_to_all(spread, 'row', 0, 0, tiled=True)  9.01 us
    ppermute x1, starting transfers between devices, per_device(): got = lax.ppermute(send, 'core', swap)  8.6 us
    unnamed x12, local copies, waits for them, and re-layouts  4 us
  transfers between devices with their start and end apart: 3, of which 3 were waited for; matrix products, arithmetic and copies ran while one was open for 1% of the time, Pallas kernels for 0%

profile of v1, /device:TPU:1, one launch (start us, length us, event | category | flops | bytes accessed | tf_op | source)
XLA Modules:
  0.0 137.1 jit_solution(13187748940343317882)
XLA Ops:
  0.6 1.7 %broadcast_in_dim.4 = bf16[8,256,128]{2,1,0:T(8,128)(2,1)} broadcast(bf16[256,128]{1,0:T(8,128)(2,1)} %param.7), dimensions={1,2} | broadcast | bytes 589824 | tf_op jit(solution)/shard_map/broadcast_in_dim | solution.py:151
  2.3 9.0 %all-to-all-start = ((bf16[8,256,128]{2,1,0:T(8,128)(2,1)}), bf16[8,256,128]{2,1,0:T(8,128)(2,1)S(1)}, u32[]{:S(2)}, u32[]{:S(2)}) async-start(bf16[8,256,128]{2,1,0:T(8,128)(2,1)} %broadcast_in_dim.4), calls=%async_computation | async-start | bytes 1048576 | tf_op jit(solution)/shard_map/all_to_all | solution.py:152
  12.0 0.7 reduce.rows
  12.7 0.7 reduce.1.cols
  13.4 0.1 pad_add_fusion.meta
  13.5 15.8 %all-to-all-done = bf16[8,256,128]{2,1,0:T(8,128)(2,1)S(1)} async-done(((bf16[8,256,128]{2,1,0:T(8,128)(2,1)}), bf16[8,256,128]{2,1,0:T(8,128)(2,1)S(1)}, u32[]{:S(2)}, u32[]{:S(2)}) %all-to-all-start) | async-done | bytes 524320 | tf_op jit(solution)/shard_map/all_to_all | solution.py:152
  29.3 0.0 copy-start
  29.3 4.0 %copy-done = bf16[1,1,320,128,128]{4,3,2,1,0:T(8,128)(2,1)S(1)} copy-done((bf16[1,1,320,128,128]{4,3,2,1,0:T(8,128)(2,1)S(1)}, bf16[1,1,320,128,128]{4,3,2,1,0:T(8,128)(2,1)}, u32[]{:S(2)}) %copy-start) | copy-done | bytes 10485784
  33.3 0.0 slice-start
  33.3 0.0 slice-start.1
  33.3 2.1 %forward.1 = (bf16[16,256,128]{2,1,0:T(8,128)(2,1)S(1)}, bf16[16,256,128]{2,1,0:T(8,128)(2,1)S(1)}) custom-call(s32[2]{0:T(128)S(1)} %pad_add_fusion.meta, s32[320]{0:T(512)S(1)} %reduce.rows, s32[320]{0:T(512)S(1)} %reduce.1.cols, bf16[320,128,128]{2,1,0:T(8,128)(2,1)S(1)} %bitcast.7, bf16[16,128,128]{2,1,0:T(8,128)(2,1)S(1)} %bitcast.11), custom_call_target="tpu_custom_call" | custom-call | tf_op jit(solution)/shard_map/forward/pallas_call | solution.py:153
  35.4 8.6 %collective-permute-start = (bf16[16,256,128]{2,1,0:T(8,128)(2,1)S(1)}, bf16[16,256,128]{2,1,0:T(8,128)(2,1)S(1)}, u32[]{:S(2)}, u32[]{:S(2)}) collective-permute-start(bf16[16,256,128]{2,1,0:T(8,128)(2,1)S(1)} %get-tuple-element.10), channel_id=1, source_target_pairs={{0,1},{1,0},{2,3},{3,2},{4,5},{5,4},{6,7},{7,6},{8,9},{9,8},{10,11... | collective-permute-start | bytes 3145736 | tf_op jit(solution)/shard_map/ppermute | solution.py:162
  44.0 2.3 %collective-permute-done = bf16[16,256,128]{2,1,0:T(8,128)(2,1)S(1)} collective-permute-done((bf16[16,256,128]{2,1,0:T(8,128)(2,1)S(1)}, bf16[16,256,128]{2,1,0:T(8,128)(2,1)S(1)}, u32[]{:S(2)}, u32[]{:S(2)}) %collective-permute-start) | collective-permute-done | bytes 1048608 | tf_op jit(solution)/shard_map/ppermute | solution.py:162
  46.2 0.0 copy-start.1
  46.2 0.0 copy-start.2
  46.3 0.0 slice-start.2
  46.3 0.3 add_convert_fusion
  46.5 21.0 %all_to_all.25.parts = bf16[16,256,128]{2,1,0:T(8,128)(2,1)S(1)} all-to-all(bf16[16,256,128]{2,1,0:T(8,128)(2,1)S(1)} %add_convert_fusion), channel_id=1, replica_groups=mesh['row'=8,'y'=4,'x'=4,'core'=2] {'y','x'}, dimensions={0} | all-to-all | bytes 2097152 | tf_op jit(solution)/shard_map/all_to_all | solution.py:164
  67.5 0.0 copy-done.1
  67.5 0.0 copy-done.2
  67.5 1.3 middle.1
  68.9 19.9 %all_to_all.26.mine = bf16[16,272,128]{2,1,0:T(8,128)(2,1)S(1)} all-to-all(bf16[16,272,128]{2,1,0:T(8,128)(2,1)S(1)} %get-tuple-element.12), channel_id=1, replica_groups=mesh['row'=8,'y'=4,'x'=4,'core'=2] {'y','x'}, dimensions={0} | all-to-all | bytes 2228224 | tf_op jit(solution)/shard_map/all_to_all | solution.py:176
  88.8 2.2 %collective-permute-start.1 = (bf16[16,272,128]{2,1,0:T(8,128)(2,1)S(1)}, bf16[16,272,128]{2,1,0:T(8,128)(2,1)S(1)}, u32[]{:S(2)}, u32[]{:S(2)}) collective-permute-start(bf16[16,272,128]{2,1,0:T(8,128)(2,1)S(1)} %all_to_all.26.mine), channel_id=1, source_target_pairs={{0,1},{1,0},{2,3},{3,2},{4,5},{5,4},{6,7},{7,6},{8,9},{9,8},{10,11... | collective-permute-start | bytes 3342344 | tf_op jit(solution)/shard_map/ppermute | solution.py:177
  91.0 2.4 %collective-permute-done.1.other = bf16[16,272,128]{2,1,0:T(8,128)(2,1)S(1)} collective-permute-done((bf16[16,272,128]{2,1,0:T(8,128)(2,1)S(1)}, bf16[16,272,128]{2,1,0:T(8,128)(2,1)S(1)}, u32[]{:S(2)}, u32[]{:S(2)}) %collective-permute-start.1) | collective-permute-done | bytes 1114144 | tf_op jit(solution)/shard_map/ppermute | solution.py:177
  93.4 0.0 slice-done
  93.4 0.0 slice-done.1
  93.4 0.0 slice-done.2
  93.4 2.0 %backward.1 = bf16[8,272,128]{2,1,0:T(8,128)(2,1)S(1)} custom-call(s32[2]{0:T(128)S(1)} %pad_add_fusion.meta, s32[320]{0:T(512)S(1)} %reduce.rows, s32[320]{0:T(512)S(1)} %reduce.1.cols, bf16[320,128,128]{2,1,0:T(8,128)(2,1)S(1)} %bitcast.10, bf16[16,272,128]{2,1,0:T(8,128)(2,1)S(1)} %all_to_all.26.mine, bf16[16,272,128]{2,1,0:T(8,128)(2,1)S(1)} %collective-permute-done.1.other), custom_call_target="tpu_custom_call" | custom-call | tf_op jit(solution)/shard_map/backward/pallas_call | solution.py:178
  95.4 23.6 %all_to_all.27.parts_ref = bf16[8,272,128]{2,1,0:T(8,128)(2,1)S(1)} all-to-all(bf16[8,272,128]{2,1,0:T(8,128)(2,1)S(1)} %backward.1), channel_id=1, replica_groups=mesh['row'=8,'y'=4,'x'=4,'core'=2] {'row'}, dimensions={0} | all-to-all | bytes 1114112 | tf_op jit(solution)/shard_map/all_to_all | solution.py:190
  119.1 0.7 finish.1
  119.8 16.6 %all_to_all.28 = f32[16,16,128]{2,1,0:T(8,128)S(1)} all-to-all(f32[16,16,128]{2,1,0:T(8,128)S(1)} %broadcast_in_dim.5), channel_id=1, replica_groups=mesh['row'=8,'y'=4,'x'=4,'core'=2] {'y','x'}, dimensions={0} | all-to-all | bytes 262144 | tf_op jit(solution)/shard_map/all_to_all | solution.py:208
  136.4 0.7 pad_maximum_fusion
  (3 shorter events, 0.0 us)
Async XLA Ops:
  2.3 27.0 %all-to-all-start = ((bf16[8,256,128]{2,1,0:T(8,128)(2,1)}), bf16[8,256,128]{2,1,0:T(8,128)(2,1)S(1)}, u32[]{:S(2)}, u32[]{:S(2)}) async-start(bf16[8,256,128]{2,1,0:T(8,128)(2,1)} %broadcast_in_dim.4), calls=%async_computation | async-start | bytes 1048576 | tf_op jit(solution)/shard_map/all_to_all | solution.py:152
  29.3 4.0 %copy-start = (bf16[1,1,320,128,128]{4,3,2,1,0:T(8,128)(2,1)S(1)}, bf16[1,1,320,128,128]{4,3,2,1,0:T(8,128)(2,1)}, u32[]{:S(2)}) copy-start(bf16[1,1,320,128,128]{4,3,2,1,0:T(8,128)(2,1)} %param.9) | copy-start | bytes 31457284
  33.3 60.1 %slice-start = ((s8[10485760]{0:T(1024)(128)(4,1)}), s8[4194304]{0:T(1024)(128)(4,1)S(1)}, s32[]{:S(2)}) async-start(s8[10485760]{0:T(1024)(128)(4,1)} %bitcast.8), calls=%async_computation.5 | async-start | bytes 8388608
  33.3 60.1 %slice-start.1 = ((s8[10485760]{0:T(1024)(128)(4,1)}), s8[4194304]{0:T(1024)(128)(4,1)S(1)}, s32[]{:S(2)}) async-start(s8[10485760]{0:T(1024)(128)(4,1)} %bitcast.8), calls=%async_computation.6 | async-start | bytes 8388608
  35.4 10.9 %collective-permute-start = (bf16[16,256,128]{2,1,0:T(8,128)(2,1)S(1)}, bf16[16,256,128]{2,1,0:T(8,128)(2,1)S(1)}, u32[]{:S(2)}, u32[]{:S(2)}) collective-permute-start(bf16[16,256,128]{2,1,0:T(8,128)(2,1)S(1)} %get-tuple-element.10), channel_id=1, source_target_pairs={{0,1},{1,0},{2,3},{3,2},{4,5},{5,4},{6,7},{7,6},{8,9},{9,8},{10,11... | collective-permute-start | bytes 3145736 | tf_op jit(solution)/shard_map/ppermute | solution.py:162
  46.2 21.3 %copy-start.1 = (bf16[256,256]{1,0:T(8,128)(2,1)S(1)}, bf16[256,256]{1,0:T(8,128)(2,1)}, u32[]{:S(2)}) copy-start(bf16[256,256]{1,0:T(8,128)(2,1)} %cotangent.1) | copy-start | bytes 393220
  46.2 21.3 %copy-start.2 = (bf16[128,256]{1,0:T(8,128)(2,1)S(1)}, bf16[128,256]{1,0:T(8,128)(2,1)}, u32[]{:S(2)}) copy-start(bf16[128,256]{1,0:T(8,128)(2,1)} %weight.1) | copy-start | bytes 196612
  46.3 47.1 %slice-start.2 = ((s8[10485760]{0:T(1024)(128)(4,1)}), s8[2097152]{0:T(1024)(128)(4,1)S(1)}, s32[]{:S(2)}) async-start(s8[10485760]{0:T(1024)(128)(4,1)} %bitcast.8), calls=%async_computation.7 | async-start | bytes 4194304
  88.8 4.6 %collective-permute-start.1 = (bf16[16,272,128]{2,1,0:T(8,128)(2,1)S(1)}, bf16[16,272,128]{2,1,0:T(8,128)(2,1)S(1)}, u32[]{:S(2)}, u32[]{:S(2)}) collective-permute-start(bf16[16,272,128]{2,1,0:T(8,128)(2,1)S(1)} %all_to_all.26.mine), channel_id=1, source_target_pairs={{0,1},{1,0},{2,3},{3,2},{4,5},{5,4},{6,7},{7,6},{8,9},{9,8},{10,11... | collective-permute-start | bytes 3342344 | tf_op jit(solution)/shard_map/ppermute | solution.py:177

commit v2 on v1

v2 whole, which is shorter than its diff:
```python
import jax
import jax.numpy as jnp
from jax import lax
from jax.experimental import pallas as pl
from jax.experimental.pallas import tpu as pltpu
from jax.sharding import Mesh, PartitionSpec as P

F32, BF16, I32 = jnp.float32, jnp.bfloat16, jnp.int32
HIGHEST = lax.Precision.HIGHEST
UNROLL = 16
LIST = 208
CHUNKS = 8
PREPARE = 4
SMEM = pl.BlockSpec(memory_space=pltpu.SMEM)
VMEM = pl.BlockSpec(memory_space=pltpu.VMEM)
HBM = pl.BlockSpec(memory_space=pltpu.HBM)


def params(mebibytes):
    return pltpu.CompilerParams(vmem_limit_bytes=mebibytes * 2**20)


def prepare_kernel(rows, cols, count, words, pairs, open_row, open_col):
    live = count[0, 0]
    core = lax.axis_index("core")
    row_bins, col_bins = open_row.shape[0] - 1, open_col.shape[0] - 1

    for spot in range(row_bins + 1):
        open_row[spot] = -1
    for spot in range(col_bins + 1):
        open_col[spot] = -1

    def step(slot, ends):
        other, mine, first, second = ends
        valid = slot < live
        row, col = rows[0, 0, slot], cols[0, 0, slot]
        own = (((row >> 1) & 1) == core).astype(I32)
        local = ((row >> 2) << 1) + (row & 1)
        spot = jnp.where(valid, row, row_bins)
        waiting = open_row[spot]
        full = jnp.logical_and(waiting >= 0, valid).astype(I32)
        word = waiting + (slot << 9) + (local << 18) + (col << 27)
        words[jnp.where(own == 1, LIST + mine, other)] = word
        open_row[spot] = jnp.where(waiting >= 0, -1, slot + (col << 23))
        place = jnp.where(valid, (col << 1) + own, col_bins)
        paused = open_col[place]
        done = jnp.logical_and(paused >= 0, valid).astype(I32)
        word = paused + (slot << 9) + (col << 18) + (local << 27)
        words[jnp.where(own == 1, 2 * LIST + first, 3 * LIST + second)] = word
        open_col[place] = jnp.where(paused >= 0, -1, slot + (local << 22))
        return (
            other + full * (1 - own),
            mine + full * own,
            first + done * own,
            second + done * (1 - own),
        )

    def several(block, ends):
        for offset in range(PREPARE):
            ends = step(block * PREPARE + offset, ends)
        return ends

    ends = lax.fori_loop(0, pl.cdiv(live, PREPARE), several, (0, 0, 0, 0))

    def flush_row(row, ends):
        other, mine = ends
        own = (((row >> 1) & 1) == core).astype(I32)
        local = ((row >> 2) << 1) + (row & 1)
        waiting = open_row[row]
        full = (waiting >= 0).astype(I32)
        slot, col = waiting & 511, (waiting >> 23) & 15
        words[jnp.where(own == 1, LIST + mine, other)] = (
            waiting + (slot << 9) + (local << 18) + (col << 27)
        )
        return other + full * (1 - own), mine + full * own

    def flush_col(place, ends):
        first, second = ends
        own, col = place & 1, place >> 1
        paused = open_col[place]
        done = (paused >= 0).astype(I32)
        slot, local = paused & 511, (paused >> 22) & 31
        words[jnp.where(own == 1, 2 * LIST + first, 3 * LIST + second)] = (
            paused + (slot << 9) + (col << 18) + (local << 27)
        )
        return first + done * own, second + done * (1 - own)

    other, mine = lax.fori_loop(0, row_bins, flush_row, ends[:2])
    first, second = lax.fori_loop(0, col_bins, flush_col, ends[2:])
    for part, end in enumerate((other, mine, first, second)):
        pairs[part] = end
        for offset in range(UNROLL):
            words[part * LIST + end + offset] = 0


def weight_of(word, spot, total):
    alone = (word & 511) == ((word >> 9) & 511)
    return jnp.where(spot < total, jnp.where(alone, 0.5, 1.0), 0.0)


def start_tiles(live, stored, tiles, sems):
    for chunk in range(sems.shape[0]):
        span = tiles.shape[0] // sems.shape[0]

        @pl.when(chunk * span < live)
        def _():
            tile_copy(chunk, stored, tiles, sems).start()


def tile_copy(chunk, stored, tiles, sems):
    span = tiles.shape[0] // sems.shape[0]
    spot = pl.ds(chunk * span, span)
    return pltpu.make_async_copy(stored.at[0, 0, spot], tiles.at[spot], sems.at[chunk])


def await_tiles(first, last, stored, tiles, sems):
    def body(chunk, carry):
        tile_copy(chunk, stored, tiles, sems).wait()
        return carry

    lax.fori_loop(first, last, body, 0)


def tile_pass(part, words, pairs, tiles, multiply, acc, count=None, stored=None, sems=None):
    total = pairs[part]

    def group(step, loaded):
        listed = [words[part * LIST + step * UNROLL + offset] for offset in range(UNROLL)]
        if stored is not None:
            span = tiles.shape[0] // sems.shape[0]
            needed = loaded
            for word in listed:
                needed = jnp.maximum(needed, ((word >> 9) & 511) // span + 1)
            await_tiles(loaded, needed, stored, tiles, sems)
            loaded = needed
        results = []
        for offset, word in enumerate(listed):
            target, product = multiply(word, tiles)
            weight = weight_of(word, step * UNROLL + offset, total)
            results.append((target, product * weight))
        for target, product in results:
            acc[target] += product
        return loaded

    loaded = lax.fori_loop(0, pl.cdiv(total, UNROLL), group, 0)
    if stored is not None:
        span = tiles.shape[0] // sems.shape[0]
        await_tiles(loaded, pl.cdiv(count[0, 0], span), stored, tiles, sems)


def forward_product(panel):
    def multiply(word, tiles):
        pair = jnp.concatenate([tiles[word & 511], tiles[(word >> 9) & 511]], axis=1)
        source = jnp.concatenate([panel[(word >> 23) & 15], panel[(word >> 27) & 15]], axis=0)
        return (word >> 18) & 31, jnp.dot(pair, source, preferred_element_type=F32)

    return multiply


def backward_product(grads):
    def multiply(word, tiles):
        pair = jnp.concatenate([tiles[word & 511], tiles[(word >> 9) & 511]], axis=0)
        source = jnp.concatenate([grads[(word >> 22) & 31], grads[(word >> 27) & 31]], axis=0)
        product = lax.dot_general(
            pair, source, (((0,), (0,)), ((), ())), preferred_element_type=F32
        )
        return (word >> 18) & 15, product

    return multiply


def forward_send_kernel(words, pairs, count, stored, panel, send, tiles, acc, sems):
    start_tiles(count[0, 0], stored, tiles, sems)
    acc[...] = jnp.zeros_like(acc)
    tile_pass(0, words, pairs, tiles, forward_product(panel), acc, count, stored, sems)
    send[...] = acc[...].astype(BF16)


def forward_keep_kernel(words, pairs, tiles, panel, keep):
    keep[...] = jnp.zeros_like(keep)
    tile_pass(1, words, pairs, tiles, forward_product(panel), keep)


def middle_kernel(parts, weight, cotangent, hidden, payload, local):
    peers = parts.shape[0]
    feat = weight.shape[0]
    agg = parts[0].astype(F32)
    for peer in range(1, peers):
        agg += parts[peer].astype(F32)
    wide = weight[...].astype(F32)
    pre = jnp.dot(agg, wide, precision=HIGHEST, preferred_element_type=F32)
    slope, cubic = 0.7978845608028654, 0.044715
    square = pre * pre
    curve = jnp.tanh(slope * pre * (1.0 + cubic * square))
    cdf = 0.5 * (1.0 + curve)
    hidden[...] = (pre * cdf).astype(BF16)
    rate = cdf + 0.5 * pre * (1.0 - curve * curve) * (slope * (1.0 + 3.0 * cubic * square))
    act = cotangent[...].astype(F32) * rate
    grad = lax.dot_general(
        act.astype(BF16), weight[...], (((1,), (1,)), ((), ())), preferred_element_type=F32
    ).astype(BF16)
    for peer in range(peers):
        payload[peer] = grad
    share = lax.dot_general(
        agg, act, (((0,), (0,)), ((), ())), precision=HIGHEST, preferred_element_type=F32
    ).astype(BF16)
    local[:feat] = share[:, :feat]
    local[feat:] = share[:, feat:]


def backward_first_kernel(words, pairs, count, stored, grads, acc, tiles, sems):
    start_tiles(count[0, 0], stored, tiles, sems)
    acc[...] = jnp.zeros_like(acc)
    tile_pass(2, words, pairs, tiles, backward_product(grads), acc, count, stored, sems)


def backward_second_kernel(words, pairs, tiles, grads, start, out, acc):
    acc[...] = start[...]
    tile_pass(3, words, pairs, tiles, backward_product(grads), acc)
    out[...] = acc[...].astype(BF16)


def finish_kernel(parts, grad):
    total = parts[0].astype(F32)
    for peer in range(1, parts.shape[0]):
        total += parts[peer].astype(F32)
    grad[...] = total.astype(BF16)


def add_kernel(left, right, total):
    total[...] = (left[...].astype(F32) + right[...].astype(F32)).astype(BF16)


def added(*terms):
    terms = [term.astype(F32) for term in terms]
    while len(terms) > 1:
        terms = [left + right for left, right in zip(terms[::2], terms[1::2])]
    return terms[0]


def swapped(value, axis, step):
    return lax.ppermute(value, axis, [(i, i ^ step) for i in range(lax.axis_size(axis))])


def shifted(value, axis, step):
    size = lax.axis_size(axis)
    return lax.ppermute(value, axis, [(i, (i + step) % size) for i in range(size)])


def per_device(features, weight, adj_tiles, tile_rows, tile_cols, tile_count, cotangent):
    own, feat = features.shape
    hid = weight.shape[1]
    n_row = lax.axis_size("row")
    peers = lax.axis_size("y") * lax.axis_size("x")
    slots, size = adj_tiles.shape[2], adj_tiles.shape[-1]
    half_rows = own * peers // size
    col_tiles = own * n_row // size
    yx = ("y", "x")

    stored = pltpu.with_memory_space_constraint(adj_tiles, pltpu.HBM)
    words, pairs = pl.pallas_call(
        prepare_kernel,
        out_shape=[
            jax.ShapeDtypeStruct((4 * LIST,), I32),
            jax.ShapeDtypeStruct((4,), I32),
        ],
        in_specs=[SMEM, SMEM, SMEM],
        out_specs=[SMEM, SMEM],
        scratch_shapes=[
            pltpu.SMEM((2 * half_rows + 1,), I32),
            pltpu.SMEM((2 * col_tiles + 1,), I32),
        ],
        compiler_params=params(4),
        name="prepare",
    )(tile_rows, tile_cols, tile_count)

    spread = jnp.broadcast_to(features[None], (n_row, own, feat))
    panel = lax.all_to_all(spread, "row", 0, 0, tiled=True).reshape(col_tiles, size, feat)
    flops = slots * size * size * feat
    tile_cost = pl.CostEstimate(flops=flops, bytes_accessed=adj_tiles.size, transcendentals=0)
    held = pltpu.VMEM((slots, size, size), BF16)
    sems = pltpu.SemaphoreType.DMA((CHUNKS,))
    send, tiles = pl.pallas_call(
        forward_send_kernel,
        out_shape=[jax.ShapeDtypeStruct((half_rows, size, feat), BF16), held],
        in_specs=[SMEM, SMEM, SMEM, HBM, VMEM],
        out_specs=[VMEM, VMEM],
        scratch_shapes=[pltpu.VMEM((half_rows, size, feat), F32), sems],
        compiler_params=params(16),
        cost_estimate=tile_cost,
        name="forward_send",
    )(words, pairs, tile_count, stored, panel)
    got = swapped(send, "core", 1)
    keep = pl.pallas_call(
        forward_keep_kernel,
        out_shape=jax.ShapeDtypeStruct((half_rows, size, feat), F32),
        in_specs=[SMEM, SMEM, VMEM, VMEM],
        out_specs=VMEM,
        compiler_params=params(16),
        cost_estimate=tile_cost,
        name="forward_keep",
    )(words, pairs, tiles, panel)
    paired = (keep + got.astype(F32)).astype(BF16).reshape(peers, own, feat)
    parts = lax.all_to_all(paired, yx, 0, 0, tiled=True)
    hidden, payload, local = pl.pallas_call(
        middle_kernel,
        out_shape=[
            jax.ShapeDtypeStruct(cotangent.shape, BF16),
            jax.ShapeDtypeStruct((peers, own, feat), BF16),
            jax.ShapeDtypeStruct((hid, feat), BF16),
        ],
        in_specs=[VMEM, VMEM, VMEM],
        out_specs=[VMEM, VMEM, VMEM],
        compiler_params=params(16),
        name="middle",
    )(parts, weight, cotangent)

    step = 1
    while step < n_row:
        local = added(local, swapped(local, "row", step)).astype(BF16)
        step *= 2
    mine = lax.all_to_all(payload, yx, 0, 0, tiled=True).reshape(half_rows, size, feat)
    mine, local = lax.optimization_barrier((mine, local))
    other = swapped(mine, "core", 1)
    paired_local = swapped(local, "core", 1)
    started, tiles = pl.pallas_call(
        backward_first_kernel,
        out_shape=[jax.ShapeDtypeStruct((col_tiles, size, feat), F32), held],
        in_specs=[SMEM, SMEM, SMEM, HBM, VMEM],
        out_specs=[VMEM, VMEM],
        scratch_shapes=[sems],
        compiler_params=params(16),
        cost_estimate=tile_cost,
        name="backward_first",
    )(words, pairs, tile_count, stored, mine)
    col_partial = pl.pallas_call(
        backward_second_kernel,
        out_shape=jax.ShapeDtypeStruct((col_tiles, size, feat), BF16),
        in_specs=[SMEM, SMEM, VMEM, VMEM, VMEM],
        out_specs=VMEM,
        scratch_shapes=[pltpu.VMEM((col_tiles, size, feat), F32)],
        compiler_params=params(16),
        cost_estimate=tile_cost,
        name="backward_second",
    )(words, pairs, tiles, other, started)
    col_partial, local, paired_local = lax.optimization_barrier((col_partial, local, paired_local))
    local = pl.pallas_call(
        add_kernel,
        out_shape=jax.ShapeDtypeStruct(local.shape, BF16),
        in_specs=[VMEM, VMEM],
        out_specs=VMEM,
        compiler_params=params(4),
        cost_estimate=tile_cost,
        name="add_core",
    )(local, paired_local)
    shares = lax.all_to_all(col_partial.reshape(n_row, own, feat), "row", 0, 0, tiled=True)
    local = added(local, *[shifted(local, "x", step) for step in (2, 1, 3)]).astype(BF16)
    total = added(local, *[shifted(local, "y", step) for step in (2, 1, 3)])
    total = total * (own * n_row * peers * 2) ** -0.5
    weight_grad = jnp.concatenate([total[:feat], total[feat:]], axis=1)
    input_grad = pl.pallas_call(
        finish_kernel,
        out_shape=jax.ShapeDtypeStruct((own, feat), BF16),
        in_specs=[VMEM],
        out_specs=VMEM,
        compiler_params=params(16),
        name="finish",
    )(shares)
    return (hidden, input_grad, weight_grad)


def solution(mesh):
    side = 4
    fine = Mesh(
        mesh.devices.reshape(mesh.shape["row"], side, side, 2), ("row", "y", "x", "core")
    )
    col = ("y", "x", "core")
    placed = (
        P((*col, "row"), None),
        P(),
        P("row", col, None, None, None),
        P("row", col, None),
        P("row", col, None),
        P("row", col),
        P(("row", *col), None),
    )
    return jax.shard_map(
        per_device,
        mesh=fine,
        in_specs=placed,
        out_specs=(P(("row", *col), None), P((*col, "row"), None), P()),
        check_vma=False,
    )
```

time: 138 us -> 124 us (0.90)
  blocking collectives: 81.2 us -> 24.9 us
  waiting for transfers between devices: 20.5 us -> 40.1 us
  starting transfers between devices: 19.8 us -> 37.6 us
  Pallas kernels: 6.13 us -> 16.1 us
  local copies, waits for them, and re-layouts: 5.71 us -> 3.09 us
    all_to_all x3 -> x0, blocking collectives: 60.2 us -> none  [the longest x1 23.6 us: per_device(): shares = lax.all_to_all(col_partial, 'row', 0, 0, tiled=True)]
    ppermute x2 -> x12, waiting for transfers between devices: 4.67 us -> 18.4 us  [the longest x6 14.1 us: swapped(): lax.ppermute(value, axis, [(i, i ^ step) for i in range(lax.axis_size(axi...]
    ppermute x2 -> x12, starting transfers between devices: 10.8 us -> 21.5 us  [the longest x6 13.2 us: shifted(): lax.ppermute(value, axis, [(i, (i + step) % size) for i in range(size)])]
    pallas_call x3 -> x7, Pallas kernels: 4.78 us -> 14.2 us  [the longest x1 3.5 us: per_device(): pl.pallas_call(forward_send_kernel, out_shape=[jax.ShapeDtypeStruct((half...]
    all_to_all x0 -> x2, waiting for transfers between devices: none -> 9.2 us  [the longest x1 9.2 us: per_device(): lax.all_to_all(col_partial.reshape(n_row, own, feat), 'row', 0, 0, tiled=...]
    all_to_all x0 -> x2, starting transfers between devices: none -> 7.14 us  [the longest x1 3.65 us: per_device(): lax.all_to_all(payload, yx, 0, 0, tiled=True).reshape(half_rows, size, feat)]
    all_to_all x1, blocking collectives: 21 us -> 24.9 us  [per_device(): parts = lax.all_to_all(paired, yx, 0, 0, tiled=True)]
    all_to_all x1, waiting for transfers between devices: 15.8 us -> 12.5 us  [per_device(): lax.all_to_all(spread, 'row', 0, 0, tiled=True)]
  transfers between devices with their start and end apart: 3 -> 15, of which waited for: 3 -> 10; matrix products, arithmetic and copies ran while one was open for 1% -> 1% of each run, Pallas kernels for 0% -> 8%
where the time goes in v2:
time: 124 us
  waiting for transfers between devices  40.1 us (32%)
  starting transfers between devices  37.6 us (30%)
  blocking collectives  24.9 us (20%)
  Pallas kernels  16.1 us (13%)
  local copies, waits for them, and re-layouts  3.09 us (2%)
  between operations  1.44 us (1%)
    all_to_all x1, blocking collectives, per_device(): parts = lax.all_to_all(paired, yx, 0, 0, tiled=True)  24.9 us
    ppermute x6, waiting for transfers between devices, swapped(): lax.ppermute(value, axis, [(i, i ^ step) for i in range(lax.axis_size(axi...  14.1 us
    ppermute x6, starting transfers between devices, shifted(): lax.ppermute(value, axis, [(i, (i + step) % size) for i in range(size)])  13.2 us
    all_to_all x1, waiting for transfers between devices, per_device(): lax.all_to_all(spread, 'row', 0, 0, tiled=True)  12.5 us
    all_to_all x1, waiting for transfers between devices, per_device(): lax.all_to_all(col_partial.reshape(n_row, own, feat), 'row', 0, 0, tiled=...  9.2 us
    all_to_all x1, starting transfers between devices, per_device(): lax.all_to_all(spread, 'row', 0, 0, tiled=True)  9.01 us
    ppermute x6, starting transfers between devices, swapped(): lax.ppermute(value, axis, [(i, i ^ step) for i in range(lax.axis_size(axi...  8.21 us
    ppermute x6, waiting for transfers between devices, shifted(): lax.ppermute(value, axis, [(i, (i + step) % size) for i in range(size)])  4.29 us
  transfers between devices with their start and end apart: 15, of which 10 were waited for; matrix products, arithmetic and copies ran while one was open for 1% of the time, Pallas kernels for 8%

profile of v2, /device:TPU:1, one launch (start us, length us, event | category | flops | bytes accessed | tf_op | source)
XLA Modules:
  0.0 124.4 jit_solution(2384079004603063861)
XLA Ops:
  0.6 1.7 %broadcast_in_dim.2 = bf16[8,256,128]{2,1,0:T(8,128)(2,1)} broadcast(bf16[256,128]{1,0:T(8,128)(2,1)} %param.7), dimensions={1,2} | broadcast | bytes 589824 | tf_op jit(solution)/shard_map/broadcast_in_dim | solution.py:277
  2.3 9.0 %all-to-all-start = ((bf16[8,256,128]{2,1,0:T(8,128)(2,1)}), bf16[8,256,128]{2,1,0:T(8,128)(2,1)S(1)}, u32[]{:S(2)}, u32[]{:S(2)}) async-start(bf16[8,256,128]{2,1,0:T(8,128)(2,1)} %broadcast_in_dim.2), calls=%async_computation | async-start | bytes 1048576 | tf_op jit(solution)/shard_map/all_to_all | solution.py:278
  12.0 0.0 copy-start.2
  12.0 0.7 copy-done.2
  12.7 0.7 copy-done.3
  13.4 3.4 %prepare.1 = (s32[832]{0:T(1024)S(1)}, s32[4]{0:T(128)S(1)}) custom-call(s32[1,1,320]{2,1,0:T(1,128)S(1)} %copy-done.2, s32[1,1,320]{2,1,0:T(1,128)S(1)} %copy-done.3, s32[1,1]{1,0:T(1,128)S(6)} %copy.10.count), custom_call_target="tpu_custom_call" | custom-call | tf_op jit(solution)/shard_map/prepare/pallas_call | solution.py:261
  16.8 12.5 %all-to-all-done = bf16[8,256,128]{2,1,0:T(8,128)(2,1)S(1)} async-done(((bf16[8,256,128]{2,1,0:T(8,128)(2,1)}), bf16[8,256,128]{2,1,0:T(8,128)(2,1)S(1)}, u32[]{:S(2)}, u32[]{:S(2)}) %all-to-all-start) | async-done | bytes 524320 | tf_op jit(solution)/shard_map/all_to_all | solution.py:278
  29.3 3.5 %forward_send.1 = (bf16[32,128,128]{2,1,0:T(8,128)(2,1)S(1)}, bf16[320,128,128]{2,1,0:T(8,128)(2,1)S(1)}) custom-call(s32[832]{0:T(1024)S(1)} %get-tuple-element.17.words, s32[4]{0:T(128)S(1)} %get-tuple-element.18.pairs, s32[1,1]{1,0:T(1,128)S(6)} %copy.10.count, bf16[1,1,320,128,128]{4,3,2,1,0:T(8,128)(2,1)} %stored.3, bf16[16,128,128]{2,1,0:T(8,128)(2,1)S(1)} %bitcast.4), custom_call_target="tpu_custom_call" | custom-call | flops 671088640 | bytes 5242880 | tf_op jit(solution)/shard_map/forward_send/pallas_call | solution.py:283
  32.8 0.6 collective-permute-start
  33.4 1.2 forward_keep.1
  34.6 1.1 collective-permute-done
  35.7 0.3 add_convert_fusion
  36.0 0.0 copy-start
  36.0 0.0 copy-start.1
  36.0 24.9 %all_to_all.20.parts = bf16[16,256,128]{2,1,0:T(8,128)(2,1)S(1)} all-to-all(bf16[16,256,128]{2,1,0:T(8,128)(2,1)S(1)} %bitcast.8), channel_id=1, replica_groups=mesh['row'=8,'y'=4,'x'=4,'core'=2] {'y','x'}, dimensions={0} | all-to-all | bytes 2097152 | tf_op jit(solution)/shard_map/all_to_all | solution.py:304
  61.0 0.0 copy-done
  61.0 0.0 copy-done.1
  61.0 1.9 %middle.1 = (bf16[256,256]{1,0:T(8,128)(2,1)}, bf16[16,256,128]{2,1,0:T(8,128)(2,1)}, bf16[256,128]{1,0:T(8,128)(2,1)S(1)}) custom-call(bf16[16,256,128]{2,1,0:T(8,128)(2,1)S(1)} %all_to_all.20.parts, bf16[128,256]{1,0:T(8,128)(2,1)S(1)} %copy-done.1, bf16[256,256]{1,0:T(8,128)(2,1)S(1)} %copy-done), custom_call_target="tpu_custom_call" | custom-call | tf_op jit(solution)/shard_map/middle/pallas_call | solution.py:305
  62.9 3.7 %all-to-all-start.2 = ((bf16[16,256,128]{2,1,0:T(8,128)(2,1)}), bf16[16,256,128]{2,1,0:T(8,128)(2,1)S(1)}, u32[]{:S(2)}, u32[]{:S(2)}) async-start(bf16[16,256,128]{2,1,0:T(8,128)(2,1)} %get-tuple-element.22), calls=%async_computation.2 | async-start | bytes 2097152 | tf_op jit(solution)/shard_map/all_to_all | solution.py:322
  66.5 0.4 collective-permute-start.1
  66.9 2.8 %collective-permute-done.1 = bf16[256,128]{1,0:T(8,128)(2,1)S(1)} collective-permute-done((bf16[256,128]{1,0:T(8,128)(2,1)S(1)}, bf16[256,128]{1,0:T(8,128)(2,1)S(1)}, u32[]{:S(2)}, u32[]{:S(2)}) %collective-permute-start.1) | collective-permute-done | bytes 65568 | tf_op jit(solution)/shard_map/ppermute | solution.py:242
  69.7 0.1 collective-permute-start.2
  69.8 5.0 %collective-permute-done.2 = bf16[256,128]{1,0:T(8,128)(2,1)S(1)} collective-permute-done((bf16[256,128]{1,0:T(8,128)(2,1)S(1)}, bf16[256,128]{1,0:T(8,128)(2,1)S(1)}, u32[]{:S(2)}, u32[]{:S(2)}) %collective-permute-start.2) | collective-permute-done | bytes 65568 | tf_op jit(solution)/shard_map/ppermute | solution.py:242
  74.9 1.9 %collective-permute-start.3 = (bf16[256,128]{1,0:T(8,128)(2,1)S(1)}, bf16[256,128]{1,0:T(8,128)(2,1)S(1)}, u32[]{:S(2)}, u32[]{:S(2)}) collective-permute-start(bf16[256,128]{1,0:T(8,128)(2,1)S(1)} %add_convert_fusion.3), channel_id=1, source_target_pairs={{0,128},{32,160},{64,192},{96,224},{128,0},{160,32},{192,64},{224,... | collective-permute-start | bytes 196616 | tf_op jit(solution)/shard_map/ppermute | solution.py:242
  76.8 5.2 %collective-permute-done.3 = bf16[256,128]{1,0:T(8,128)(2,1)S(1)} collective-permute-done((bf16[256,128]{1,0:T(8,128)(2,1)S(1)}, bf16[256,128]{1,0:T(8,128)(2,1)S(1)}, u32[]{:S(2)}, u32[]{:S(2)}) %collective-permute-start.3) | collective-permute-done | bytes 65568 | tf_op jit(solution)/shard_map/ppermute | solution.py:242
  82.0 0.0 all-to-all-done.2
  82.0 5.1 %collective-permute-start.4 = (bf16[32,128,128]{2,1,0:T(8,128)(2,1)S(1)}, bf16[32,128,128]{2,1,0:T(8,128)(2,1)S(1)}, u32[]{:S(2)}, u32[]{:S(2)}) collective-permute-start(bf16[32,128,128]{2,1,0:T(8,128)(2,1)S(1)} %bitcast.6), channel_id=1, source_target_pairs={{0,1},{1,0},{2,3},{3,2},{4,5},{5,4},{6,7},{7,6},{8,9},{9,8},{10,11... | collective-permute-start | bytes 3145736 | tf_op jit(solution)/shard_map/ppermute | solution.py:242
  87.2 0.1 collective-permute-start.5
  87.3 2.9 %backward_first.1 = (f32[16,128,128]{2,1,0:T(8,128)S(1)}, bf16[320,128,128]{2,1,0:T(8,128)(2,1)S(1)}) custom-call(s32[832]{0:T(1024)S(1)} %get-tuple-element.17.words, s32[4]{0:T(128)S(1)} %get-tuple-element.18.pairs, s32[1,1]{1,0:T(1,128)S(6)} %copy.10.count, bf16[1,1,320,128,128]{4,3,2,1,0:T(8,128)(2,1)} %stored.3, bf16[32,128,128]{2,1,0:T(8,128)(2,1)S(1)} %bitcast.7), custom_call_target="tpu_custom_call" | custom-call | flops 671088640 | bytes 5242880 | tf_op jit(solution)/shard_map/backward_first/pallas_call | solution.py:326
  90.1 0.0 collective-permute-done.4.grads
  90.2 2.5 %backward_second.1 = bf16[16,128,128]{2,1,0:T(8,128)(2,1)} custom-call(s32[832]{0:T(1024)S(1)} %get-tuple-element.17.words, s32[4]{0:T(128)S(1)} %get-tuple-element.18.pairs, bf16[320,128,128]{2,1,0:T(8,128)(2,1)S(1)} %get-tuple-element.25.tiles, bf16[32,128,128]{2,1,0:T(8,128)(2,1)S(1)} %collective-permute-done.4.grads, ...), custom_call_target="tpu_custom_call" | custom-call | flops 671088640 | bytes 5242880 | tf_op jit(solution)/shard_map/backward_second/pallas_call | solution.py:336
  92.6 0.0 collective-permute-done.5.right
  92.7 8.4 %collective-permute-start.8 = (bf16[256,128]{1,0:T(8,128)(2,1)S(1)}, bf16[256,128]{1,0:T(8,128)(2,1)S(1)}, u32[]{:S(2)}, u32[]{:S(2)}) collective-permute-start(bf16[256,128]{1,0:T(8,128)(2,1)S(1)} %add_core.1), channel_id=1, source_target_pairs={{0,6},{2,0},{4,2},{6,4},{1,7},{3,1},{5,3},{7,5},{8,14},{10,8},{12,... | collective-permute-start | bytes 196616 | tf_op jit(solution)/shard_map/ppermute | solution.py:247
  101.1 0.0 collective-permute-start.7
  101.1 1.3 %collective-permute-start.6 = (bf16[256,128]{1,0:T(8,128)(2,1)S(1)}, bf16[256,128]{1,0:T(8,128)(2,1)S(1)}, u32[]{:S(2)}, u32[]{:S(2)}) collective-permute-start(bf16[256,128]{1,0:T(8,128)(2,1)S(1)} %add_core.1), channel_id=1, source_target_pairs={{0,4},{2,6},{4,0},{6,2},{1,5},{3,7},{5,1},{7,3},{8,12},{10,14},{12... | collective-permute-start | bytes 196616 | tf_op jit(solution)/shard_map/ppermute | solution.py:247
  102.3 3.5 %all-to-all-start.3 = ((bf16[8,256,128]{2,1,0:T(8,128)(2,1)}), bf16[8,256,128]{2,1,0:T(8,128)(2,1)S(1)}, u32[]{:S(2)}, u32[]{:S(2)}) async-start(bf16[8,256,128]{2,1,0:T(8,128)(2,1)} %bitcast.3), calls=%async_computation.3 | async-start | bytes 1048576 | tf_op jit(solution)/shard_map/all_to_all | solution.py:356
  105.8 0.0 collective-permute-done.8
  105.8 0.9 collective-permute-done.7
  106.8 0.0 collective-permute-done.6
  106.8 0.1 collective-permute-start.11
  106.9 1.5 %collective-permute-start.10 = (bf16[256,128]{1,0:T(8,128)(2,1)S(1)}, bf16[256,128]{1,0:T(8,128)(2,1)S(1)}, u32[]{:S(2)}, u32[]{:S(2)}) collective-permute-start(bf16[256,128]{1,0:T(8,128)(2,1)S(1)} %add_convert_fusion.1), channel_id=1, source_target_pairs={{0,8},{8,16},{16,24},{24,0},{1,9},{9,17},{17,25},{25,1},{2,10},{10... | collective-permute-start | bytes 196616 | tf_op jit(solution)/shard_map/ppermute | solution.py:247
  108.4 2.1 %collective-permute-start.9 = (bf16[256,128]{1,0:T(8,128)(2,1)S(1)}, bf16[256,128]{1,0:T(8,128)(2,1)S(1)}, u32[]{:S(2)}, u32[]{:S(2)}) collective-permute-start(bf16[256,128]{1,0:T(8,128)(2,1)S(1)} %add_convert_fusion.1), channel_id=1, source_target_pairs={{0,16},{8,24},{16,0},{24,8},{1,17},{9,25},{17,1},{25,9},{2,18},{10... | collective-permute-start | bytes 196616 | tf_op jit(solution)/shard_map/ppermute | solution.py:247
  110.4 0.3 collective-permute-done.11
  110.8 0.6 collective-permute-done.10
  111.3 2.4 %collective-permute-done.9 = bf16[256,128]{1,0:T(8,128)(2,1)S(1)} collective-permute-done((bf16[256,128]{1,0:T(8,128)(2,1)S(1)}, bf16[256,128]{1,0:T(8,128)(2,1)S(1)}, u32[]{:S(2)}, u32[]{:S(2)}) %collective-permute-start.9) | collective-permute-done | bytes 65568 | tf_op jit(solution)/shard_map/ppermute | solution.py:247
  113.8 0.7 pad_maximum_fusion
  114.5 9.2 %all-to-all-done.3.parts = bf16[8,256,128]{2,1,0:T(8,128)(2,1)S(1)} async-done(((bf16[8,256,128]{2,1,0:T(8,128)(2,1)}), bf16[8,256,128]{2,1,0:T(8,128)(2,1)S(1)}, u32[]{:S(2)}, u32[]{:S(2)}) %all-to-all-start.3) | async-done | bytes 524320 | tf_op jit(solution)/shard_map/all_to_all | solution.py:356
  123.7 0.7 finish.1
  (8 shorter events, 0.2 us)
Async XLA Ops:
  2.3 27.0 %all-to-all-start = ((bf16[8,256,128]{2,1,0:T(8,128)(2,1)}), bf16[8,256,128]{2,1,0:T(8,128)(2,1)S(1)}, u32[]{:S(2)}, u32[]{:S(2)}) async-start(bf16[8,256,128]{2,1,0:T(8,128)(2,1)} %broadcast_in_dim.2), calls=%async_computation | async-start | bytes 1048576 | tf_op jit(solution)/shard_map/all_to_all | solution.py:278
  12.0 0.7 copy-start.2
  12.7 0.7 copy-start.3
  32.8 2.9 %collective-permute-start = (bf16[32,128,128]{2,1,0:T(8,128)(2,1)S(1)}, bf16[32,128,128]{2,1,0:T(8,128)(2,1)S(1)}, u32[]{:S(2)}, u32[]{:S(2)}) collective-permute-start(bf16[32,128,128]{2,1,0:T(8,128)(2,1)S(1)} %get-tuple-element.20), channel_id=1, source_target_pairs={{0,1},{1,0},{2,3},{3,2},{4,5},{5,4},{6,7},{7,6},{8,9},{9,8},{10,11... | collective-permute-start | bytes 3145736 | tf_op jit(solution)/shard_map/ppermute | solution.py:242
  36.0 24.9 %copy-start = (bf16[256,256]{1,0:T(8,128)(2,1)S(1)}, bf16[256,256]{1,0:T(8,128)(2,1)}, u32[]{:S(2)}) copy-start(bf16[256,256]{1,0:T(8,128)(2,1)} %cotangent.1) | copy-start | bytes 393220
  36.0 24.9 %copy-start.1 = (bf16[128,256]{1,0:T(8,128)(2,1)S(1)}, bf16[128,256]{1,0:T(8,128)(2,1)}, u32[]{:S(2)}) copy-start(bf16[128,256]{1,0:T(8,128)(2,1)} %weight.1) | copy-start | bytes 196612
  62.9 19.1 %all-to-all-start.2 = ((bf16[16,256,128]{2,1,0:T(8,128)(2,1)}), bf16[16,256,128]{2,1,0:T(8,128)(2,1)S(1)}, u32[]{:S(2)}, u32[]{:S(2)}) async-start(bf16[16,256,128]{2,1,0:T(8,128)(2,1)} %get-tuple-element.22), calls=%async_computation.2 | async-start | bytes 2097152 | tf_op jit(solution)/shard_map/all_to_all | solution.py:322
  66.5 3.2 %collective-permute-start.1 = (bf16[256,128]{1,0:T(8,128)(2,1)S(1)}, bf16[256,128]{1,0:T(8,128)(2,1)S(1)}, u32[]{:S(2)}, u32[]{:S(2)}) collective-permute-start(bf16[256,128]{1,0:T(8,128)(2,1)S(1)} %get-tuple-element.23), channel_id=1, source_target_pairs={{0,32},{32,0},{64,96},{96,64},{128,160},{160,128},{192,224},{224,1... | collective-permute-start | bytes 196616 | tf_op jit(solution)/shard_map/ppermute | solution.py:242
  69.7 5.1 %collective-permute-start.2 = (bf16[256,128]{1,0:T(8,128)(2,1)S(1)}, bf16[256,128]{1,0:T(8,128)(2,1)S(1)}, u32[]{:S(2)}, u32[]{:S(2)}) collective-permute-start(bf16[256,128]{1,0:T(8,128)(2,1)S(1)} %add_convert_fusion.4), channel_id=1, source_target_pairs={{0,64},{32,96},{64,0},{96,32},{128,192},{160,224},{192,128},{224,1... | collective-permute-start | bytes 196616 | tf_op jit(solution)/shard_map/ppermute | solution.py:242
  74.9 7.1 %collective-permute-start.3 = (bf16[256,128]{1,0:T(8,128)(2,1)S(1)}, bf16[256,128]{1,0:T(8,128)(2,1)S(1)}, u32[]{:S(2)}, u32[]{:S(2)}) collective-permute-start(bf16[256,128]{1,0:T(8,128)(2,1)S(1)} %add_convert_fusion.3), channel_id=1, source_target_pairs={{0,128},{32,160},{64,192},{96,224},{128,0},{160,32},{192,64},{224,... | collective-permute-start | bytes 196616 | tf_op jit(solution)/shard_map/ppermute | solution.py:242
  82.0 8.1 %collective-permute-start.4 = (bf16[32,128,128]{2,1,0:T(8,128)(2,1)S(1)}, bf16[32,128,128]{2,1,0:T(8,128)(2,1)S(1)}, u32[]{:S(2)}, u32[]{:S(2)}) collective-permute-start(bf16[32,128,128]{2,1,0:T(8,128)(2,1)S(1)} %bitcast.6), channel_id=1, source_target_pairs={{0,1},{1,0},{2,3},{3,2},{4,5},{5,4},{6,7},{7,6},{8,9},{9,8},{10,11... | collective-permute-start | bytes 3145736 | tf_op jit(solution)/shard_map/ppermute | solution.py:242
  87.2 5.5 %collective-permute-start.5 = (bf16[256,128]{1,0:T(8,128)(2,1)S(1)}, bf16[256,128]{1,0:T(8,128)(2,1)S(1)}, u32[]{:S(2)}, u32[]{:S(2)}) collective-permute-start(bf16[256,128]{1,0:T(8,128)(2,1)S(1)} %add_convert_fusion.2.left), channel_id=1, source_target_pairs={{0,1},{1,0},{2,3},{3,2},{4,5},{5,4},{6,7},{7,6},{8,9},{9,8},{10,11... | collective-permute-start | bytes 196616 | tf_op jit(solution)/shard_map/ppermute | solution.py:242
  92.7 13.2 %collective-permute-start.8 = (bf16[256,128]{1,0:T(8,128)(2,1)S(1)}, bf16[256,128]{1,0:T(8,128)(2,1)S(1)}, u32[]{:S(2)}, u32[]{:S(2)}) collective-permute-start(bf16[256,128]{1,0:T(8,128)(2,1)S(1)} %add_core.1), channel_id=1, source_target_pairs={{0,6},{2,0},{4,2},{6,4},{1,7},{3,1},{5,3},{7,5},{8,14},{10,8},{12,... | collective-permute-start | bytes 196616 | tf_op jit(solution)/shard_map/ppermute | solution.py:247
  101.1 5.7 %collective-permute-start.7 = (bf16[256,128]{1,0:T(8,128)(2,1)S(1)}, bf16[256,128]{1,0:T(8,128)(2,1)S(1)}, u32[]{:S(2)}, u32[]{:S(2)}) collective-permute-start(bf16[256,128]{1,0:T(8,128)(2,1)S(1)} %add_core.1), channel_id=1, source_target_pairs={{0,2},{2,4},{4,6},{6,0},{1,3},{3,5},{5,7},{7,1},{8,10},{10,12},{12... | collective-permute-start | bytes 196616 | tf_op jit(solution)/shard_map/ppermute | solution.py:247
  101.1 5.7 %collective-permute-start.6 = (bf16[256,128]{1,0:T(8,128)(2,1)S(1)}, bf16[256,128]{1,0:T(8,128)(2,1)S(1)}, u32[]{:S(2)}, u32[]{:S(2)}) collective-permute-start(bf16[256,128]{1,0:T(8,128)(2,1)S(1)} %add_core.1), channel_id=1, source_target_pairs={{0,4},{2,6},{4,0},{6,2},{1,5},{3,7},{5,1},{7,3},{8,12},{10,14},{12... | collective-permute-start | bytes 196616 | tf_op jit(solution)/shard_map/ppermute | solution.py:247
  102.3 21.4 %all-to-all-start.3 = ((bf16[8,256,128]{2,1,0:T(8,128)(2,1)}), bf16[8,256,128]{2,1,0:T(8,128)(2,1)S(1)}, u32[]{:S(2)}, u32[]{:S(2)}) async-start(bf16[8,256,128]{2,1,0:T(8,128)(2,1)} %bitcast.3), calls=%async_computation.3 | async-start | bytes 1048576 | tf_op jit(solution)/shard_map/all_to_all | solution.py:356
  106.8 3.9 %collective-permute-start.11 = (bf16[256,128]{1,0:T(8,128)(2,1)S(1)}, bf16[256,128]{1,0:T(8,128)(2,1)S(1)}, u32[]{:S(2)}, u32[]{:S(2)}) collective-permute-start(bf16[256,128]{1,0:T(8,128)(2,1)S(1)} %add_convert_fusion.1), channel_id=1, source_target_pairs={{0,24},{8,0},{16,8},{24,16},{1,25},{9,1},{17,9},{25,17},{2,26},{10... | collective-permute-start | bytes 196616 | tf_op jit(solution)/shard_map/ppermute | solution.py:247
  106.9 4.4 %collective-permute-start.10 = (bf16[256,128]{1,0:T(8,128)(2,1)S(1)}, bf16[256,128]{1,0:T(8,128)(2,1)S(1)}, u32[]{:S(2)}, u32[]{:S(2)}) collective-permute-start(bf16[256,128]{1,0:T(8,128)(2,1)S(1)} %add_convert_fusion.1), channel_id=1, source_target_pairs={{0,8},{8,16},{16,24},{24,0},{1,9},{9,17},{17,25},{25,1},{2,10},{10... | collective-permute-start | bytes 196616 | tf_op jit(solution)/shard_map/ppermute | solution.py:247
  108.4 5.4 %collective-permute-start.9 = (bf16[256,128]{1,0:T(8,128)(2,1)S(1)}, bf16[256,128]{1,0:T(8,128)(2,1)S(1)}, u32[]{:S(2)}, u32[]{:S(2)}) collective-permute-start(bf16[256,128]{1,0:T(8,128)(2,1)S(1)} %add_convert_fusion.1), channel_id=1, source_target_pairs={{0,16},{8,24},{16,0},{24,8},{1,17},{9,25},{17,1},{25,9},{2,18},{10... | collective-permute-start | bytes 196616 | tf_op jit(solution)/shard_map/ppermute | solution.py:247

commit v3 on v2

v3 whole, which is shorter than its diff:
```python
import jax
import jax.numpy as jnp
from jax import lax
from jax.experimental import pallas as pl
from jax.experimental.pallas import tpu as pltpu
from jax.sharding import Mesh, PartitionSpec as P

F32, BF16, I32 = jnp.float32, jnp.bfloat16, jnp.int32
HIGHEST = lax.Precision.HIGHEST
UNROLL = 16
LIST = 208
CHUNKS = 8
AHEAD = 8
PREPARE = 4
SMEM = pl.BlockSpec(memory_space=pltpu.SMEM)
VMEM = pl.BlockSpec(memory_space=pltpu.VMEM)
HBM = pl.BlockSpec(memory_space=pltpu.HBM)


def params(mebibytes):
    return pltpu.CompilerParams(vmem_limit_bytes=mebibytes * 2**20)


def prepare_kernel(forward, rows, cols, count, *refs):
    if forward:
        stored, words, pairs, tiles, waiting, sem = refs
        load = pltpu.make_async_copy(stored.at[0, 0], tiles, sem)
        load.start()
    else:
        words, pairs, waiting = refs
    live = count[0, 0]
    core = lax.axis_index("core")
    bins = waiting.shape[0] - 1
    target_at, source_at, partner_at = (18, 23, 27) if forward else (18, 22, 27)

    for spot in range(bins + 1):
        waiting[spot] = -1

    def enter(ends, here, open_word, closing, valid):
        first, second = ends
        full = jnp.logical_and(open_word >= 0, valid).astype(I32)
        words[jnp.where(here == 1, LIST + second, first)] = open_word + closing
        return first + full * (1 - here), second + full * here

    def step(slot, ends):
        valid = slot < live
        row, col = rows[0, 0, slot], cols[0, 0, slot]
        own = (((row >> 1) & 1) == core).astype(I32)
        local = ((row >> 2) << 1) + (row & 1)
        if forward:
            place, target, source, here = row, local, col, own
        else:
            place, target, source, here = (col << 1) + own, col, local, 1 - own
        place = jnp.where(valid, place, bins)
        held = waiting[place]
        waiting[place] = jnp.where(held >= 0, -1, slot + (source << source_at))
        closing = (slot << 9) + (target << target_at) + (source << partner_at)
        return enter(ends, here, held, closing, valid)

    def several(block, ends):
        for offset in range(PREPARE):
            ends = step(block * PREPARE + offset, ends)
        return ends

    def flush(block, ends):
        for offset in range(PREPARE):
            place = block * PREPARE + offset
            held = waiting[place]
            if forward:
                here = (((place >> 1) & 1) == core).astype(I32)
                target = ((place >> 2) << 1) + (place & 1)
                source = (held >> source_at) & 15
            else:
                here, target = 1 - (place & 1), place >> 1
                source = (held >> source_at) & 31
            closing = ((held & 511) << 9) + (target << target_at) + (source << partner_at)
            ends = enter(ends, here, held, closing, True)
        return ends

    ends = lax.fori_loop(0, pl.cdiv(live, PREPARE), several, (0, 0))
    ends = lax.fori_loop(0, bins // PREPARE, flush, ends)
    for part, end in enumerate(ends):
        pairs[part] = end
        for offset in range(UNROLL):
            words[part * LIST + end + offset] = 0
    if forward:
        load.wait()


def weight_of(word, spot, total):
    alone = (word & 511) == ((word >> 9) & 511)
    return jnp.where(spot < total, jnp.where(alone, 0.5, 1.0), 0.0)


def tile_copy(chunk, stored, tiles, sems):
    span = tiles.shape[0] // CHUNKS
    spot = pl.ds(chunk * span, span)
    return pltpu.make_async_copy(stored.at[0, 0, spot], tiles.at[spot], sems.at[chunk])


def start_tiles(chunk, live, stored, tiles, sems):
    span = tiles.shape[0] // CHUNKS

    @pl.when(chunk * span < live)
    def _():
        tile_copy(chunk, stored, tiles, sems).start()


def await_tiles(first, last, live, stored, tiles, sems):
    def body(chunk, carry):
        tile_copy(chunk, stored, tiles, sems).wait()
        start_tiles(chunk + AHEAD, live, stored, tiles, sems)
        return carry

    lax.fori_loop(first, last, body, 0)


def tile_pass(part, words, pairs, tiles, multiply, acc, count=None, stored=None, sems=None):
    total = pairs[part]

    def group(step, loaded):
        listed = [words[part * LIST + step * UNROLL + offset] for offset in range(UNROLL)]
        if stored is not None:
            span = tiles.shape[0] // CHUNKS
            highest = 0
            for word in listed:
                highest = jnp.maximum(highest, (word >> 9) & 511)
            needed = jnp.maximum(loaded, highest // span + 1)
            await_tiles(loaded, needed, count[0, 0], stored, tiles, sems)
            loaded = needed
        results = []
        for offset, word in enumerate(listed):
            target, product = multiply(word, tiles)
            weight = weight_of(word, step * UNROLL + offset, total)
            results.append((target, product * weight))
        for target, product in results:
            acc[target] += product
        return loaded

    loaded = lax.fori_loop(0, pl.cdiv(total, UNROLL), group, 0)
    if stored is not None:
        span = tiles.shape[0] // CHUNKS
        await_tiles(loaded, pl.cdiv(count[0, 0], span), count[0, 0], stored, tiles, sems)


def forward_product(panel):
    def multiply(word, tiles):
        pair = jnp.concatenate([tiles[word & 511], tiles[(word >> 9) & 511]], axis=1)
        source = jnp.concatenate([panel[(word >> 23) & 15], panel[(word >> 27) & 15]], axis=0)
        return (word >> 18) & 31, jnp.dot(pair, source, preferred_element_type=F32)

    return multiply


def backward_product(grads):
    def multiply(word, tiles):
        pair = jnp.concatenate([tiles[word & 511], tiles[(word >> 9) & 511]], axis=0)
        source = jnp.concatenate([grads[(word >> 22) & 31], grads[(word >> 27) & 31]], axis=0)
        product = lax.dot_general(
            pair, source, (((0,), (0,)), ((), ())), preferred_element_type=F32
        )
        return (word >> 18) & 15, product

    return multiply


def forward_send_kernel(words, pairs, tiles, *refs):
    *blocks, send, panel, acc = refs
    here = lax.axis_index("row")
    per_block = panel.shape[0] // len(blocks)
    for step, block in enumerate(blocks):
        owner = lax.rem(here - step + len(blocks), len(blocks))
        for part in range(per_block):
            spot = pl.ds(part * panel.shape[1], panel.shape[1])
            panel[owner * per_block + part] = block[spot]
    acc[...] = jnp.zeros_like(acc)
    tile_pass(0, words, pairs, tiles, forward_product(panel), acc)
    send[...] = acc[...].astype(BF16)


def forward_keep_kernel(words, pairs, tiles, panel, keep):
    keep[...] = jnp.zeros_like(keep)
    tile_pass(1, words, pairs, tiles, forward_product(panel), keep)


def middle_kernel(parts, weight, cotangent, hidden, payload, local):
    peers = parts.shape[0]
    feat = weight.shape[0]
    agg = parts[0].astype(F32)
    for peer in range(1, peers):
        agg += parts[peer].astype(F32)
    wide = weight[...].astype(F32)
    pre = jnp.dot(agg, wide, precision=HIGHEST, preferred_element_type=F32)
    slope, cubic = 0.7978845608028654, 0.044715
    square = pre * pre
    curve = jnp.tanh(slope * pre * (1.0 + cubic * square))
    cdf = 0.5 * (1.0 + curve)
    hidden[...] = (pre * cdf).astype(BF16)
    rate = cdf + 0.5 * pre * (1.0 - curve * curve) * (slope * (1.0 + 3.0 * cubic * square))
    act = cotangent[...].astype(F32) * rate
    grad = lax.dot_general(
        act.astype(BF16), weight[...], (((1,), (1,)), ((), ())), preferred_element_type=F32
    ).astype(BF16)
    for peer in range(peers):
        payload[peer] = grad
    share = lax.dot_general(
        agg, act, (((0,), (0,)), ((), ())), precision=HIGHEST, preferred_element_type=F32
    ).astype(BF16)
    local[:feat] = share[:, :feat]
    local[feat:] = share[:, feat:]


def backward_first_kernel(words, pairs, count, stored, grads, acc, tiles, sems):
    for chunk in range(AHEAD):
        start_tiles(chunk, count[0, 0], stored, tiles, sems)
    acc[...] = jnp.zeros_like(acc)
    tile_pass(0, words, pairs, tiles, backward_product(grads), acc, count, stored, sems)


def backward_second_kernel(words, pairs, tiles, grads, start, out, acc):
    acc[...] = start[...]
    tile_pass(1, words, pairs, tiles, backward_product(grads), acc)
    per_peer = out.shape[1] // acc.shape[1]
    for peer in range(out.shape[0]):
        for part in range(per_peer):
            spot = pl.ds(part * acc.shape[1], acc.shape[1])
            out[peer, spot] = acc[peer * per_peer + part].astype(BF16)


def finish_kernel(scale, parts, first, second, third, fourth, grad, weight_grad):
    total = parts[0].astype(F32)
    for peer in range(1, parts.shape[0]):
        total += parts[peer].astype(F32)
    grad[...] = total.astype(BF16)
    feat = grad.shape[1]
    total = added(first[...], second[...], third[...], fourth[...]) * scale
    weight_grad[:, :feat] = total[:feat]
    weight_grad[:, feat:] = total[feat:]


def add_kernel(*refs):
    *terms, total = refs
    total[...] = added(*[term[...] for term in terms]).astype(BF16)


def summed(*terms):
    return pl.pallas_call(
        add_kernel,
        out_shape=jax.ShapeDtypeStruct(terms[0].shape, BF16),
        in_specs=[VMEM] * len(terms),
        out_specs=VMEM,
        compiler_params=params(4),
        name="add",
    )(*terms)


def added(*terms):
    terms = [term.astype(F32) for term in terms]
    while len(terms) > 1:
        terms = [left + right for left, right in zip(terms[::2], terms[1::2])]
    return terms[0]


def swapped(value, axis, step):
    return lax.ppermute(value, axis, [(i, i ^ step) for i in range(lax.axis_size(axis))])


def shifted(value, axis, step):
    size = lax.axis_size(axis)
    return lax.ppermute(value, axis, [(i, (i + step) % size) for i in range(size)])


def per_device(features, weight, adj_tiles, tile_rows, tile_cols, tile_count, cotangent):
    own, feat = features.shape
    hid = weight.shape[1]
    n_row = lax.axis_size("row")
    peers = lax.axis_size("y") * lax.axis_size("x")
    slots, size = adj_tiles.shape[2], adj_tiles.shape[-1]
    half_rows = own * peers // size
    col_tiles = own * n_row // size
    yx = ("y", "x")

    stored = pltpu.with_memory_space_constraint(adj_tiles, pltpu.HBM)
    rows, cols = [pltpu.with_memory_space_constraint(v, pltpu.HBM) for v in (tile_rows, tile_cols)]
    places = (rows, cols, tile_count)
    held = pltpu.VMEM((slots, size, size), BF16)
    lists = [jax.ShapeDtypeStruct((2 * LIST,), I32), jax.ShapeDtypeStruct((2,), I32)]

    def prepare(forward, bins, operands):
        def kernel(*refs):
            prepare_kernel(forward, *refs)

        sem = pltpu.SemaphoreType.DMA(())
        return pl.pallas_call(
            kernel,
            out_shape=[*lists, *([held] if forward else [])],
            in_specs=[SMEM, SMEM, SMEM, *([HBM] if forward else [])],
            out_specs=[SMEM, SMEM, *([VMEM] if forward else [])],
            scratch_shapes=[pltpu.SMEM((bins + 1,), I32), *([sem] if forward else [])],
            compiler_params=params(4),
            name="prepare_forward" if forward else "prepare_backward",
        )(*operands)

    arrived = {way: shifted(features, "row", way) for way in (4, 3, 5, 2, 6, 1, 7)}
    words, pairs, resident = prepare(True, 2 * half_rows, (*places, stored))
    flops = slots * size * size * feat
    tile_cost = pl.CostEstimate(flops=flops, bytes_accessed=adj_tiles.size, transcendentals=0)
    send, panel = pl.pallas_call(
        forward_send_kernel,
        out_shape=[
            jax.ShapeDtypeStruct((half_rows, size, feat), BF16),
            jax.ShapeDtypeStruct((col_tiles, size, feat), BF16),
        ],
        in_specs=[SMEM, SMEM, VMEM, *([VMEM] * n_row)],
        out_specs=[VMEM, VMEM],
        scratch_shapes=[pltpu.VMEM((half_rows, size, feat), F32)],
        compiler_params=params(16),
        cost_estimate=tile_cost,
        name="forward_send",
    )(words, pairs, resident, features, *[arrived[way] for way in range(1, n_row)])
    got = swapped(send, "core", 1)
    keep = pl.pallas_call(
        forward_keep_kernel,
        out_shape=jax.ShapeDtypeStruct((half_rows, size, feat), F32),
        in_specs=[SMEM, SMEM, VMEM, VMEM],
        out_specs=VMEM,
        compiler_params=params(16),
        cost_estimate=tile_cost,
        name="forward_keep",
    )(words, pairs, resident, panel)
    paired = (keep + got.astype(F32)).astype(BF16).reshape(peers, own, feat)
    paired, words, pairs = lax.optimization_barrier((paired, words, pairs))
    words, pairs = prepare(False, 2 * col_tiles, (rows, cols, tile_count + 0 * pairs[:1, None]))
    parts = lax.all_to_all(paired, yx, 0, 0, tiled=True)
    parts, words, pairs = lax.optimization_barrier((parts, words, pairs))
    hidden, payload, local = pl.pallas_call(
        middle_kernel,
        out_shape=[
            jax.ShapeDtypeStruct(cotangent.shape, BF16),
            jax.ShapeDtypeStruct((peers, own, feat), BF16),
            jax.ShapeDtypeStruct((hid, feat), BF16),
        ],
        in_specs=[VMEM, VMEM, VMEM],
        out_specs=[VMEM, VMEM, VMEM],
        compiler_params=params(16),
        name="middle",
    )(parts, weight, cotangent)

    local = added(local, swapped(local, "row", 1)).astype(BF16)
    local = added(local, *[shifted(local, "row", step) for step in (4, 2, 6)]).astype(BF16)
    mine = lax.all_to_all(payload, yx, 0, 0, tiled=True).reshape(half_rows, size, feat)
    mine, local = lax.optimization_barrier((mine, local))
    other = swapped(mine, "core", 1)
    paired_local = swapped(local, "core", 1)
    started, tiles = pl.pallas_call(
        backward_first_kernel,
        out_shape=[jax.ShapeDtypeStruct((col_tiles, size, feat), F32), held],
        in_specs=[SMEM, SMEM, SMEM, HBM, VMEM],
        out_specs=[VMEM, VMEM],
        scratch_shapes=[pltpu.SemaphoreType.DMA((CHUNKS,))],
        compiler_params=params(16),
        cost_estimate=tile_cost,
        name="backward_first",
    )(words, pairs, tile_count, stored, mine)
    col_partial = pl.pallas_call(
        backward_second_kernel,
        out_shape=jax.ShapeDtypeStruct((n_row, own, feat), BF16),
        in_specs=[SMEM, SMEM, VMEM, VMEM, VMEM],
        out_specs=VMEM,
        scratch_shapes=[pltpu.VMEM((col_tiles, size, feat), F32)],
        compiler_params=params(16),
        cost_estimate=tile_cost,
        name="backward_second",
    )(words, pairs, tiles, other, started)
    col_partial, local, paired_local = lax.optimization_barrier((col_partial, local, paired_local))
    shares = lax.all_to_all(col_partial, "row", 0, 0, tiled=True)
    local = summed(local, paired_local)
    local = summed(local, *[shifted(local, "x", step) for step in (2, 1, 3)])
    last = [local, *[shifted(local, "y", step) for step in (2, 1, 3)]]
    scale = (own * n_row * peers * 2) ** -0.5

    def finish(*refs):
        finish_kernel(scale, *refs)

    input_grad, weight_grad = pl.pallas_call(
        finish,
        out_shape=[
            jax.ShapeDtypeStruct((own, feat), BF16),
            jax.ShapeDtypeStruct((feat, hid), F32),
        ],
        in_specs=[VMEM] * 5,
        out_specs=[VMEM, VMEM],
        compiler_params=params(16),
        name="finish",
    )(shares, *last)
    return (hidden, input_grad, weight_grad)


def solution(mesh):
    side = 4
    fine = Mesh(
        mesh.devices.reshape(mesh.shape["row"], side, side, 2), ("row", "y", "x", "core")
    )
    col = ("y", "x", "core")
    placed = (
        P((*col, "row"), None),
        P(),
        P("row", col, None, None, None),
        P("row", col, None),
        P("row", col, None),
        P("row", col),
        P(("row", *col), None),
    )
    return jax.shard_map(
        per_device,
        mesh=fine,
        in_specs=placed,
        out_specs=(P(("row", *col), None), P((*col, "row"), None), P()),
        check_vma=False,
    )
```

time: 124 us -> 114 us (0.919)
  starting transfers between devices: 37.6 us -> 67.1 us
  blocking collectives: 24.9 us -> 0 us
  waiting for transfers between devices: 40.1 us -> 26.4 us
  local copies, waits for them, and re-layouts: 3.09 us -> 0.01 us
    ppermute x6 -> x16, starting transfers between devices: 13.2 us -> 40.9 us  [shifted(): lax.ppermute(value, axis, [(i, (i + step) % size) for i in range(size)])]
    all_to_all x1 -> x0, blocking collectives: 24.9 us -> none  [per_device(): parts = lax.all_to_all(paired, yx, 0, 0, tiled=True)]
    ppermute x6 -> x4, waiting for transfers between devices: 14.1 us -> 3.51 us  [swapped(): lax.ppermute(value, axis, [(i, i ^ step) for i in range(lax.axis_size(axi...]
    all_to_all x2, waiting for transfers between devices: 21.7 us -> 14.3 us  [the longest x1 14.3 us: per_device(): parts = lax.all_to_all(paired, yx, 0, 0, tiled=True)]
    pallas_call x4 -> x6, Pallas kernels: 6.66 us -> 10.3 us  [the longest x2 7.51 us: prepare(): pl.pallas_call(kernel, out_shape=[*lists, *([held] if forward else [])],...]
    ppermute x6 -> x16, waiting for transfers between devices: 4.29 us -> 7.68 us  [shifted(): lax.ppermute(value, axis, [(i, (i + step) % size) for i in range(size)])]
    pallas_call x1, Pallas kernels: 3.5 us -> 1.3 us  [per_device(): pl.pallas_call(forward_send_kernel, out_shape=[jax.ShapeDtypeStruct((half...]
    all_to_all x2, starting transfers between devices: 12.5 us -> 14.5 us  [the longest x1 7.58 us: per_device(): shares = lax.all_to_all(col_partial, 'row', 0, 0, tiled=True)]
  transfers between devices with their start and end apart: 15 -> 23, of which waited for: 10 -> 8; matrix products, arithmetic and copies ran while one was open for 1% -> 0% of each run, Pallas kernels for 8% -> 12%
where the time goes in v3:
time: 114 us; the launch traced here: 113 us
  starting transfers between devices  67.1 us (59%)
  waiting for transfers between devices  26.4 us (23%)
  Pallas kernels  17.1 us (15%)
  between operations  1.41 us (1%)
  other arithmetic  1.34 us (1%)
    ppermute x16, starting transfers between devices, shifted(): lax.ppermute(value, axis, [(i, (i + step) % size) for i in range(size)])  40.9 us
    all_to_all x1, waiting for transfers between devices, per_device(): parts = lax.all_to_all(paired, yx, 0, 0, tiled=True)  14.3 us
    ppermute x16, waiting for transfers between devices, shifted(): lax.ppermute(value, axis, [(i, (i + step) % size) for i in range(size)])  7.68 us
    all_to_all x1, starting transfers between devices, per_device(): shares = lax.all_to_all(col_partial, 'row', 0, 0, tiled=True)  7.58 us
    pallas_call x2, Pallas kernels, prepare(): pl.pallas_call(kernel, out_shape=[*lists, *([held] if forward else [])],...  7.51 us
    ppermute x4, starting transfers between devices, swapped(): lax.ppermute(value, axis, [(i, i ^ step) for i in range(lax.axis_size(axi...  7.25 us
    all_to_all x1, starting transfers between devices, per_device(): parts = lax.all_to_all(paired, yx, 0, 0, tiled=True)  6.88 us
    all_to_all x1, starting transfers between devices, per_device(): lax.all_to_all(payload, yx, 0, 0, tiled=True).reshape(half_rows, size, feat)  4.51 us
  transfers between devices with their start and end apart: 23, of which 8 were waited for; matrix products, arithmetic and copies ran while one was open for 0% of the time, Pallas kernels for 12%

profile of v3, /device:TPU:1, one launch (start us, length us, event | category | flops | bytes accessed | tf_op | source)
XLA Modules:
  0.0 113.3 jit_solution(6034083351346427739)
XLA Ops:
  0.6 2.5 %collective-permute-start = (bf16[256,128]{1,0:T(8,128)(2,1)}, bf16[256,128]{1,0:T(8,128)(2,1)S(1)}, u32[]{:S(2)}, u32[]{:S(2)}) collective-permute-start(bf16[256,128]{1,0:T(8,128)(2,1)} %refs_0_.4), channel_id=1, source_target_pairs={{0,32},{32,64},{64,96},{96,128},{128,160},{160,192},{192,224},{224... | collective-permute-start | bytes 196616 | tf_op jit(solution)/shard_map/ppermute | solution.py:270
  3.2 3.0 %collective-permute-start.1 = (bf16[256,128]{1,0:T(8,128)(2,1)}, bf16[256,128]{1,0:T(8,128)(2,1)S(1)}, u32[]{:S(2)}, u32[]{:S(2)}) collective-permute-start(bf16[256,128]{1,0:T(8,128)(2,1)} %refs_0_.4), channel_id=1, source_target_pairs={{0,64},{32,96},{64,128},{96,160},{128,192},{160,224},{192,0},{224,... | collective-permute-start | bytes 196616 | tf_op jit(solution)/shard_map/ppermute | solution.py:270
  6.2 3.8 %collective-permute-start.2 = (bf16[256,128]{1,0:T(8,128)(2,1)}, bf16[256,128]{1,0:T(8,128)(2,1)S(1)}, u32[]{:S(2)}, u32[]{:S(2)}) collective-permute-start(bf16[256,128]{1,0:T(8,128)(2,1)} %refs_0_.4), channel_id=1, source_target_pairs={{0,96},{32,128},{64,160},{96,192},{128,224},{160,0},{192,32},{224,... | collective-permute-start | bytes 196616 | tf_op jit(solution)/shard_map/ppermute | solution.py:270
  9.9 0.5 collective-permute-start.3
  10.4 4.5 %collective-permute-start.4 = (bf16[256,128]{1,0:T(8,128)(2,1)}, bf16[256,128]{1,0:T(8,128)(2,1)S(1)}, u32[]{:S(2)}, u32[]{:S(2)}) collective-permute-start(bf16[256,128]{1,0:T(8,128)(2,1)} %refs_0_.4), channel_id=1, source_target_pairs={{0,160},{32,192},{64,224},{96,0},{128,32},{160,64},{192,96},{224,1... | collective-permute-start | bytes 196616 | tf_op jit(solution)/shard_map/ppermute | solution.py:270
  14.9 0.0 collective-permute-done.refs_1_
  14.9 2.4 %collective-permute-start.5 = (bf16[256,128]{1,0:T(8,128)(2,1)}, bf16[256,128]{1,0:T(8,128)(2,1)S(1)}, u32[]{:S(2)}, u32[]{:S(2)}) collective-permute-start(bf16[256,128]{1,0:T(8,128)(2,1)} %refs_0_.4), channel_id=1, source_target_pairs={{0,192},{32,224},{64,0},{96,32},{128,64},{160,96},{192,128},{224,1... | collective-permute-start | bytes 196616 | tf_op jit(solution)/shard_map/ppermute | solution.py:270
  17.2 0.0 collective-permute-done.1.refs_2_
  17.2 0.7 collective-permute-start.6
  18.6 5.5 %prepare_forward.1 = (s32[416]{0:T(512)S(1)}, s32[2]{0:T(128)S(1)}, bf16[320,128,128]{2,1,0:T(8,128)(2,1)S(1)}) custom-call(s32[1,1,320]{2,1,0:T(1,128)} %refs_0_.5, s32[1,1,320]{2,1,0:T(1,128)} %refs_1_.3, s32[1,1]{1,0:T(1,128)S(6)} %copy.10.refs_2_.count, bf16[1,1,320,128,128]{4,3,2,1,0:T(8,128)(2,1)} %stored.1), custom_call_target="tpu_custom_call" | custom-call | tf_op jit(solution)/shard_map/prepare_forward/pallas_call | solution.py:294
  24.1 0.0 collective-permute-done.2.refs_3_
  24.1 0.0 collective-permute-done.3.refs_4_
  24.1 0.0 collective-permute-done.4.refs_5_
  24.1 1.0 collective-permute-done.5.refs_6_
  25.2 1.3 %forward_send.1 = (bf16[32,128,128]{2,1,0:T(8,128)(2,1)S(1)}, bf16[16,128,128]{2,1,0:T(8,128)(2,1)S(1)}) custom-call(s32[416]{0:T(512)S(1)} %get-tuple-element.26.words, s32[2]{0:T(128)S(1)} %get-tuple-element.27.pairs, bf16[320,128,128]{2,1,0:T(8,128)(2,1)S(1)} %get-tuple-element.28.tiles, bf16[256,128]{1,0:T(8,128)(2,1)S(1)} %copy-done.1, ...), custom_call_target="tpu_custom_call" | custom-call | flops 671088640 | bytes 5242880 | tf_op jit(solution)/shard_map/forward_send/pallas_call | solution.py:308
  26.5 3.5 %collective-permute-start.7 = (bf16[32,128,128]{2,1,0:T(8,128)(2,1)S(1)}, bf16[32,128,128]{2,1,0:T(8,128)(2,1)S(1)}, u32[]{:S(2)}, u32[]{:S(2)}) collective-permute-start(bf16[32,128,128]{2,1,0:T(8,128)(2,1)S(1)} %get-tuple-element.30), channel_id=1, source_target_pairs={{0,1},{1,0},{2,3},{3,2},{4,5},{5,4},{6,7},{7,6},{8,9},{9,8},{10,11... | collective-permute-start | bytes 3145736 | tf_op jit(solution)/shard_map/ppermute | solution.py:265
  30.0 1.1 %forward_keep.1 = f32[32,128,128]{2,1,0:T(8,128)S(1)} custom-call(s32[416]{0:T(512)S(1)} %get-tuple-element.26.words, s32[2]{0:T(128)S(1)} %get-tuple-element.27.pairs, bf16[320,128,128]{2,1,0:T(8,128)(2,1)S(1)} %get-tuple-element.28.tiles, bf16[16,128,128]{2,1,0:T(8,128)(2,1)S(1)} %get-tuple-element.29.panel), custom_call_target="tpu_custom_call" | custom-call | flops 671088640 | bytes 5242880 | tf_op jit(solution)/shard_map/forward_keep/pallas_call | solution.py:322
  31.2 1.1 collective-permute-done.7
  32.3 1.3 %add_convert_fusion = bf16[32,128,128]{2,1,0:T(8,128)(2,1)} fusion(f32[32,128,128]{2,1,0:T(8,128)S(1)} %forward_keep.1, bf16[32,128,128]{2,1,0:T(8,128)(2,1)S(1)} %collective-permute-done.7), kind=kLoop, calls=%fused_computation | loop fusion | flops 1572864 | bytes 4194304 | tf_op jit(solution)/shard_map/convert_element_type | solution.py:331
  33.6 6.9 %all-to-all-start = ((bf16[16,256,128]{2,1,0:T(8,128)(2,1)}), bf16[16,256,128]{2,1,0:T(8,128)(2,1)S(1)}, u32[]{:S(2)}, u32[]{:S(2)}) async-start(bf16[16,256,128]{2,1,0:T(8,128)(2,1)} %bitcast), calls=%async_computation | async-start | bytes 2097152 | tf_op jit(solution)/shard_map/all_to_all | solution.py:334
  40.5 2.0 %prepare_backward.1 = (s32[416]{0:T(512)S(1)}, s32[2]{0:T(128)S(1)}) custom-call(s32[1,1,320]{2,1,0:T(1,128)} %refs_0_.5, s32[1,1,320]{2,1,0:T(1,128)} %refs_1_.3, s32[1,1]{1,0:T(1,128)S(6)} %copy.10.refs_2_.count), custom_call_target="tpu_custom_call" | custom-call | tf_op jit(solution)/shard_map/prepare_backward/pallas_call | solution.py:294
  42.5 14.3 %all-to-all-done.parts = bf16[16,256,128]{2,1,0:T(8,128)(2,1)S(1)} async-done(((bf16[16,256,128]{2,1,0:T(8,128)(2,1)}), bf16[16,256,128]{2,1,0:T(8,128)(2,1)S(1)}, u32[]{:S(2)}, u32[]{:S(2)}) %all-to-all-start) | async-done | bytes 1048608 | tf_op jit(solution)/shard_map/all_to_all | solution.py:334
  56.8 1.9 %middle.1 = (bf16[256,256]{1,0:T(8,128)(2,1)}, bf16[16,256,128]{2,1,0:T(8,128)(2,1)}, bf16[256,128]{1,0:T(8,128)(2,1)S(1)}) custom-call(bf16[16,256,128]{2,1,0:T(8,128)(2,1)S(1)} %all-to-all-done.parts, bf16[128,256]{1,0:T(8,128)(2,1)S(1)} %copy-done.2, bf16[256,256]{1,0:T(8,128)(2,1)S(1)} %copy-done), custom_call_target="tpu_custom_call" | custom-call | tf_op jit(solution)/shard_map/middle/pallas_call | solution.py:336
  58.7 4.5 %all-to-all-start.1 = ((bf16[16,256,128]{2,1,0:T(8,128)(2,1)}), bf16[16,256,128]{2,1,0:T(8,128)(2,1)S(1)}, u32[]{:S(2)}, u32[]{:S(2)}) async-start(bf16[16,256,128]{2,1,0:T(8,128)(2,1)} %get-tuple-element.38), calls=%async_computation.1 | async-start | bytes 2097152 | tf_op jit(solution)/shard_map/all_to_all | solution.py:351
  63.2 0.8 collective-permute-start.8
  64.0 2.4 %collective-permute-done.8 = bf16[256,128]{1,0:T(8,128)(2,1)S(1)} collective-permute-done((bf16[256,128]{1,0:T(8,128)(2,1)S(1)}, bf16[256,128]{1,0:T(8,128)(2,1)S(1)}, u32[]{:S(2)}, u32[]{:S(2)}) %collective-permute-start.8) | collective-permute-done | bytes 65568 | tf_op jit(solution)/shard_map/ppermute | solution.py:265
  66.4 2.5 %collective-permute-start.10 = (bf16[256,128]{1,0:T(8,128)(2,1)S(1)}, bf16[256,128]{1,0:T(8,128)(2,1)S(1)}, u32[]{:S(2)}, u32[]{:S(2)}) collective-permute-start(bf16[256,128]{1,0:T(8,128)(2,1)S(1)} %add_convert_fusion.2), channel_id=1, source_target_pairs={{0,64},{32,96},{64,128},{96,160},{128,192},{160,224},{192,0},{224,... | collective-permute-start | bytes 196616 | tf_op jit(solution)/shard_map/ppermute | solution.py:270
  68.9 1.2 %collective-permute-start.11 = (bf16[256,128]{1,0:T(8,128)(2,1)S(1)}, bf16[256,128]{1,0:T(8,128)(2,1)S(1)}, u32[]{:S(2)}, u32[]{:S(2)}) collective-permute-start(bf16[256,128]{1,0:T(8,128)(2,1)S(1)} %add_convert_fusion.2), channel_id=1, source_target_pairs={{0,192},{32,224},{64,0},{96,32},{128,64},{160,96},{192,128},{224,1... | collective-permute-start | bytes 196616 | tf_op jit(solution)/shard_map/ppermute | solution.py:270
  70.1 5.5 %collective-permute-start.9 = (bf16[256,128]{1,0:T(8,128)(2,1)S(1)}, bf16[256,128]{1,0:T(8,128)(2,1)S(1)}, u32[]{:S(2)}, u32[]{:S(2)}) collective-permute-start(bf16[256,128]{1,0:T(8,128)(2,1)S(1)} %add_convert_fusion.2), channel_id=1, source_target_pairs={{0,128},{32,160},{64,192},{96,224},{128,0},{160,32},{192,64},{224,... | collective-permute-start | bytes 196616 | tf_op jit(solution)/shard_map/ppermute | solution.py:270
  75.6 2.3 %collective-permute-done.9 = bf16[256,128]{1,0:T(8,128)(2,1)S(1)} collective-permute-done((bf16[256,128]{1,0:T(8,128)(2,1)S(1)}, bf16[256,128]{1,0:T(8,128)(2,1)S(1)}, u32[]{:S(2)}, u32[]{:S(2)}) %collective-permute-start.9) | collective-permute-done | bytes 65568 | tf_op jit(solution)/shard_map/ppermute | solution.py:270
  78.0 0.9 all-to-all-done.1
  78.9 2.9 %collective-permute-start.12 = (bf16[32,128,128]{2,1,0:T(8,128)(2,1)S(1)}, bf16[32,128,128]{2,1,0:T(8,128)(2,1)S(1)}, u32[]{:S(2)}, u32[]{:S(2)}) collective-permute-start(bf16[32,128,128]{2,1,0:T(8,128)(2,1)S(1)} %bitcast.2), channel_id=1, source_target_pairs={{0,1},{1,0},{2,3},{3,2},{4,5},{5,4},{6,7},{7,6},{8,9},{9,8},{10,11... | collective-permute-start | bytes 3145736 | tf_op jit(solution)/shard_map/ppermute | solution.py:265
  81.8 0.0 collective-permute-start.13
  81.8 2.5 %backward_first.1 = (f32[16,128,128]{2,1,0:T(8,128)S(1)}, bf16[320,128,128]{2,1,0:T(8,128)(2,1)S(1)}) custom-call(s32[416]{0:T(512)S(1)} %get-tuple-element.36.words, s32[2]{0:T(128)S(1)} %get-tuple-element.37.pairs, s32[1,1]{1,0:T(1,128)S(6)} %copy.10.refs_2_.count, bf16[1,1,320,128,128]{4,3,2,1,0:T(8,128)(2,1)} %stored.1, bf16[32,128,128]{2,1,0:T(8,128)(2,1)S(1)} %bitcast.3), custom_call_target="tpu_custom_call" | custom-call | flops 671088640 | bytes 5242880 | tf_op jit(solution)/shard_map/backward_first/pallas_call | solution.py:355
  84.2 0.0 collective-permute-done.12.grads
  84.3 2.0 %backward_second.1 = bf16[8,256,128]{2,1,0:T(8,128)(2,1)} custom-call(s32[416]{0:T(512)S(1)} %get-tuple-element.36.words, s32[2]{0:T(128)S(1)} %get-tuple-element.37.pairs, bf16[320,128,128]{2,1,0:T(8,128)(2,1)S(1)} %get-tuple-element.41.tiles, bf16[32,128,128]{2,1,0:T(8,128)(2,1)S(1)} %collective-permute-done.12.grads, ...), custom_call_target="tpu_custom_call" | custom-call | flops 671088640 | bytes 5242880 | tf_op jit(solution)/shard_map/backward_second/pallas_call | solution.py:365
  86.2 7.6 %all-to-all-start.2 = ((bf16[8,256,128]{2,1,0:T(8,128)(2,1)}), bf16[8,256,128]{2,1,0:T(8,128)(2,1)S(1)}, u32[]{:S(2)}, u32[]{:S(2)}) async-start(bf16[8,256,128]{2,1,0:T(8,128)(2,1)} %backward_second.1), calls=%async_computation.2 | async-start | bytes 1048576 | tf_op jit(solution)/shard_map/all_to_all | solution.py:376
  93.8 4.2 %collective-permute-start.14 = (bf16[256,128]{1,0:T(8,128)(2,1)S(1)}, bf16[256,128]{1,0:T(8,128)(2,1)S(1)}, u32[]{:S(2)}, u32[]{:S(2)}) collective-permute-start(bf16[256,128]{1,0:T(8,128)(2,1)S(1)} %add.27.refs_0_), channel_id=1, source_target_pairs={{0,4},{2,6},{4,0},{6,2},{1,5},{3,7},{5,1},{7,3},{8,12},{10,14},{12... | collective-permute-start | bytes 196616 | tf_op jit(solution)/shard_map/ppermute | solution.py:270
  98.1 2.7 %collective-permute-start.16 = (bf16[256,128]{1,0:T(8,128)(2,1)S(1)}, bf16[256,128]{1,0:T(8,128)(2,1)S(1)}, u32[]{:S(2)}, u32[]{:S(2)}) collective-permute-start(bf16[256,128]{1,0:T(8,128)(2,1)S(1)} %add.27.refs_0_), channel_id=1, source_target_pairs={{0,6},{2,0},{4,2},{6,4},{1,7},{3,1},{5,3},{7,5},{8,14},{10,8},{12,... | collective-permute-start | bytes 196616 | tf_op jit(solution)/shard_map/ppermute | solution.py:270
  100.7 0.0 collective-permute-done.14.refs_1_
  100.7 1.9 %collective-permute-done.15.refs_2_ = bf16[256,128]{1,0:T(8,128)(2,1)S(1)} collective-permute-done((bf16[256,128]{1,0:T(8,128)(2,1)S(1)}, bf16[256,128]{1,0:T(8,128)(2,1)S(1)}, u32[]{:S(2)}, u32[]{:S(2)}) %collective-permute-start.15) | collective-permute-done | bytes 65568 | tf_op jit(solution)/shard_map/ppermute | solution.py:270
  102.7 0.0 collective-permute-done.16.refs_3_
  102.7 4.8 %collective-permute-start.17 = (bf16[256,128]{1,0:T(8,128)(2,1)S(1)}, bf16[256,128]{1,0:T(8,128)(2,1)S(1)}, u32[]{:S(2)}, u32[]{:S(2)}) collective-permute-start(bf16[256,128]{1,0:T(8,128)(2,1)S(1)} %add.28.refs_1_), channel_id=1, source_target_pairs={{0,16},{8,24},{16,0},{24,8},{1,17},{9,25},{17,1},{25,9},{2,18},{10... | collective-permute-start | bytes 196616 | tf_op jit(solution)/shard_map/ppermute | solution.py:270
  107.5 0.7 collective-permute-start.18
  108.3 1.9 %collective-permute-start.19 = (bf16[256,128]{1,0:T(8,128)(2,1)S(1)}, bf16[256,128]{1,0:T(8,128)(2,1)S(1)}, u32[]{:S(2)}, u32[]{:S(2)}) collective-permute-start(bf16[256,128]{1,0:T(8,128)(2,1)S(1)} %add.28.refs_1_), channel_id=1, source_target_pairs={{0,24},{8,0},{16,8},{24,16},{1,25},{9,1},{17,9},{25,17},{2,26},{10... | collective-permute-start | bytes 196616 | tf_op jit(solution)/shard_map/ppermute | solution.py:270
  110.2 0.0 collective-permute-done.17.refs_2_
  110.2 2.4 %collective-permute-done.18.refs_3_ = bf16[256,128]{1,0:T(8,128)(2,1)S(1)} collective-permute-done((bf16[256,128]{1,0:T(8,128)(2,1)S(1)}, bf16[256,128]{1,0:T(8,128)(2,1)S(1)}, u32[]{:S(2)}, u32[]{:S(2)}) %collective-permute-start.18) | collective-permute-done | bytes 65568 | tf_op jit(solution)/shard_map/ppermute | solution.py:270
  112.6 0.8 finish.1
  (17 shorter events, 0.1 us)
Async XLA Ops:
  0.6 14.2 %collective-permute-start = (bf16[256,128]{1,0:T(8,128)(2,1)}, bf16[256,128]{1,0:T(8,128)(2,1)S(1)}, u32[]{:S(2)}, u32[]{:S(2)}) collective-permute-start(bf16[256,128]{1,0:T(8,128)(2,1)} %refs_0_.4), channel_id=1, source_target_pairs={{0,32},{32,64},{64,96},{96,128},{128,160},{160,192},{192,224},{224... | collective-permute-start | bytes 196616 | tf_op jit(solution)/shard_map/ppermute | solution.py:270
  3.2 14.1 %collective-permute-start.1 = (bf16[256,128]{1,0:T(8,128)(2,1)}, bf16[256,128]{1,0:T(8,128)(2,1)S(1)}, u32[]{:S(2)}, u32[]{:S(2)}) collective-permute-start(bf16[256,128]{1,0:T(8,128)(2,1)} %refs_0_.4), channel_id=1, source_target_pairs={{0,64},{32,96},{64,128},{96,160},{128,192},{160,224},{192,0},{224,... | collective-permute-start | bytes 196616 | tf_op jit(solution)/shard_map/ppermute | solution.py:270
  6.2 17.9 %collective-permute-start.2 = (bf16[256,128]{1,0:T(8,128)(2,1)}, bf16[256,128]{1,0:T(8,128)(2,1)S(1)}, u32[]{:S(2)}, u32[]{:S(2)}) collective-permute-start(bf16[256,128]{1,0:T(8,128)(2,1)} %refs_0_.4), channel_id=1, source_target_pairs={{0,96},{32,128},{64,160},{96,192},{128,224},{160,0},{192,32},{224,... | collective-permute-start | bytes 196616 | tf_op jit(solution)/shard_map/ppermute | solution.py:270
  9.9 14.2 %collective-permute-start.3 = (bf16[256,128]{1,0:T(8,128)(2,1)}, bf16[256,128]{1,0:T(8,128)(2,1)S(1)}, u32[]{:S(2)}, u32[]{:S(2)}) collective-permute-start(bf16[256,128]{1,0:T(8,128)(2,1)} %refs_0_.4), channel_id=1, source_target_pairs={{0,128},{32,160},{64,192},{96,224},{128,0},{160,32},{192,64},{224,... | collective-permute-start | bytes 196616 | tf_op jit(solution)/shard_map/ppermute | solution.py:270
  10.4 13.7 %collective-permute-start.4 = (bf16[256,128]{1,0:T(8,128)(2,1)}, bf16[256,128]{1,0:T(8,128)(2,1)S(1)}, u32[]{:S(2)}, u32[]{:S(2)}) collective-permute-start(bf16[256,128]{1,0:T(8,128)(2,1)} %refs_0_.4), channel_id=1, source_target_pairs={{0,160},{32,192},{64,224},{96,0},{128,32},{160,64},{192,96},{224,1... | collective-permute-start | bytes 196616 | tf_op jit(solution)/shard_map/ppermute | solution.py:270
  14.9 10.3 %collective-permute-start.5 = (bf16[256,128]{1,0:T(8,128)(2,1)}, bf16[256,128]{1,0:T(8,128)(2,1)S(1)}, u32[]{:S(2)}, u32[]{:S(2)}) collective-permute-start(bf16[256,128]{1,0:T(8,128)(2,1)} %refs_0_.4), channel_id=1, source_target_pairs={{0,192},{32,224},{64,0},{96,32},{128,64},{160,96},{192,128},{224,1... | collective-permute-start | bytes 196616 | tf_op jit(solution)/shard_map/ppermute | solution.py:270
  17.2 7.9 %collective-permute-start.6 = (bf16[256,128]{1,0:T(8,128)(2,1)}, bf16[256,128]{1,0:T(8,128)(2,1)S(1)}, u32[]{:S(2)}, u32[]{:S(2)}) collective-permute-start(bf16[256,128]{1,0:T(8,128)(2,1)} %refs_0_.4), channel_id=1, source_target_pairs={{0,224},{32,0},{64,32},{96,64},{128,96},{160,128},{192,160},{224,1... | collective-permute-start | bytes 196616 | tf_op jit(solution)/shard_map/ppermute | solution.py:270
  18.6 6.5 %copy-start.1 = (bf16[256,128]{1,0:T(8,128)(2,1)S(1)}, bf16[256,128]{1,0:T(8,128)(2,1)}, u32[]{:S(2)}) copy-start(bf16[256,128]{1,0:T(8,128)(2,1)} %refs_0_.4) | copy-start | bytes 196612
  26.5 5.8 %collective-permute-start.7 = (bf16[32,128,128]{2,1,0:T(8,128)(2,1)S(1)}, bf16[32,128,128]{2,1,0:T(8,128)(2,1)S(1)}, u32[]{:S(2)}, u32[]{:S(2)}) collective-permute-start(bf16[32,128,128]{2,1,0:T(8,128)(2,1)S(1)} %get-tuple-element.30), channel_id=1, source_target_pairs={{0,1},{1,0},{2,3},{3,2},{4,5},{5,4},{6,7},{7,6},{8,9},{9,8},{10,11... | collective-permute-start | bytes 3145736 | tf_op jit(solution)/shard_map/ppermute | solution.py:265
  33.6 23.2 %copy-start = (bf16[256,256]{1,0:T(8,128)(2,1)S(1)}, bf16[256,256]{1,0:T(8,128)(2,1)}, u32[]{:S(2)}) copy-start(bf16[256,256]{1,0:T(8,128)(2,1)} %cotangent.1) | copy-start | bytes 393220
  33.6 23.2 %copy-start.2 = (bf16[128,256]{1,0:T(8,128)(2,1)S(1)}, bf16[128,256]{1,0:T(8,128)(2,1)}, u32[]{:S(2)}) copy-start(bf16[128,256]{1,0:T(8,128)(2,1)} %weight.1) | copy-start | bytes 196612
  33.6 23.2 %all-to-all-start = ((bf16[16,256,128]{2,1,0:T(8,128)(2,1)}), bf16[16,256,128]{2,1,0:T(8,128)(2,1)S(1)}, u32[]{:S(2)}, u32[]{:S(2)}) async-start(bf16[16,256,128]{2,1,0:T(8,128)(2,1)} %bitcast), calls=%async_computation | async-start | bytes 2097152 | tf_op jit(solution)/shard_map/all_to_all | solution.py:334
  58.7 20.2 %all-to-all-start.1 = ((bf16[16,256,128]{2,1,0:T(8,128)(2,1)}), bf16[16,256,128]{2,1,0:T(8,128)(2,1)S(1)}, u32[]{:S(2)}, u32[]{:S(2)}) async-start(bf16[16,256,128]{2,1,0:T(8,128)(2,1)} %get-tuple-element.38), calls=%async_computation.1 | async-start | bytes 2097152 | tf_op jit(solution)/shard_map/all_to_all | solution.py:351
  63.2 3.2 %collective-permute-start.8 = (bf16[256,128]{1,0:T(8,128)(2,1)S(1)}, bf16[256,128]{1,0:T(8,128)(2,1)S(1)}, u32[]{:S(2)}, u32[]{:S(2)}) collective-permute-start(bf16[256,128]{1,0:T(8,128)(2,1)S(1)} %get-tuple-element.39), channel_id=1, source_target_pairs={{0,32},{32,0},{64,96},{96,64},{128,160},{160,128},{192,224},{224,1... | collective-permute-start | bytes 196616 | tf_op jit(solution)/shard_map/ppermute | solution.py:265
  66.4 9.2 %collective-permute-start.10 = (bf16[256,128]{1,0:T(8,128)(2,1)S(1)}, bf16[256,128]{1,0:T(8,128)(2,1)S(1)}, u32[]{:S(2)}, u32[]{:S(2)}) collective-permute-start(bf16[256,128]{1,0:T(8,128)(2,1)S(1)} %add_convert_fusion.2), channel_id=1, source_target_pairs={{0,64},{32,96},{64,128},{96,160},{128,192},{160,224},{192,0},{224,... | collective-permute-start | bytes 196616 | tf_op jit(solution)/shard_map/ppermute | solution.py:270
  68.9 6.7 %collective-permute-start.11 = (bf16[256,128]{1,0:T(8,128)(2,1)S(1)}, bf16[256,128]{1,0:T(8,128)(2,1)S(1)}, u32[]{:S(2)}, u32[]{:S(2)}) collective-permute-start(bf16[256,128]{1,0:T(8,128)(2,1)S(1)} %add_convert_fusion.2), channel_id=1, source_target_pairs={{0,192},{32,224},{64,0},{96,32},{128,64},{160,96},{192,128},{224,1... | collective-permute-start | bytes 196616 | tf_op jit(solution)/shard_map/ppermute | solution.py:270
  70.1 7.9 %collective-permute-start.9 = (bf16[256,128]{1,0:T(8,128)(2,1)S(1)}, bf16[256,128]{1,0:T(8,128)(2,1)S(1)}, u32[]{:S(2)}, u32[]{:S(2)}) collective-permute-start(bf16[256,128]{1,0:T(8,128)(2,1)S(1)} %add_convert_fusion.2), channel_id=1, source_target_pairs={{0,128},{32,160},{64,192},{96,224},{128,0},{160,32},{192,64},{224,... | collective-permute-start | bytes 196616 | tf_op jit(solution)/shard_map/ppermute | solution.py:270
  78.9 5.3 %collective-permute-start.12 = (bf16[32,128,128]{2,1,0:T(8,128)(2,1)S(1)}, bf16[32,128,128]{2,1,0:T(8,128)(2,1)S(1)}, u32[]{:S(2)}, u32[]{:S(2)}) collective-permute-start(bf16[32,128,128]{2,1,0:T(8,128)(2,1)S(1)} %bitcast.2), channel_id=1, source_target_pairs={{0,1},{1,0},{2,3},{3,2},{4,5},{5,4},{6,7},{7,6},{8,9},{9,8},{10,11... | collective-permute-start | bytes 3145736 | tf_op jit(solution)/shard_map/ppermute | solution.py:265
  81.8 4.5 %collective-permute-start.13 = (bf16[256,128]{1,0:T(8,128)(2,1)S(1)}, bf16[256,128]{1,0:T(8,128)(2,1)S(1)}, u32[]{:S(2)}, u32[]{:S(2)}) collective-permute-start(bf16[256,128]{1,0:T(8,128)(2,1)S(1)} %add_convert_fusion.1.refs_0_), channel_id=1, source_target_pairs={{0,1},{1,0},{2,3},{3,2},{4,5},{5,4},{6,7},{7,6},{8,9},{9,8},{10,11... | collective-permute-start | bytes 196616 | tf_op jit(solution)/shard_map/ppermute | solution.py:265
  86.2 26.3 %all-to-all-start.2 = ((bf16[8,256,128]{2,1,0:T(8,128)(2,1)}), bf16[8,256,128]{2,1,0:T(8,128)(2,1)S(1)}, u32[]{:S(2)}, u32[]{:S(2)}) async-start(bf16[8,256,128]{2,1,0:T(8,128)(2,1)} %backward_second.1), calls=%async_computation.2 | async-start | bytes 1048576 | tf_op jit(solution)/shard_map/all_to_all | solution.py:376
  93.8 6.9 %collective-permute-start.14 = (bf16[256,128]{1,0:T(8,128)(2,1)S(1)}, bf16[256,128]{1,0:T(8,128)(2,1)S(1)}, u32[]{:S(2)}, u32[]{:S(2)}) collective-permute-start(bf16[256,128]{1,0:T(8,128)(2,1)S(1)} %add.27.refs_0_), channel_id=1, source_target_pairs={{0,4},{2,6},{4,0},{6,2},{1,5},{3,7},{5,1},{7,3},{8,12},{10,14},{12... | collective-permute-start | bytes 196616 | tf_op jit(solution)/shard_map/ppermute | solution.py:270
  98.1 4.6 %collective-permute-start.15 = (bf16[256,128]{1,0:T(8,128)(2,1)S(1)}, bf16[256,128]{1,0:T(8,128)(2,1)S(1)}, u32[]{:S(2)}, u32[]{:S(2)}) collective-permute-start(bf16[256,128]{1,0:T(8,128)(2,1)S(1)} %add.27.refs_0_), channel_id=1, source_target_pairs={{0,2},{2,4},{4,6},{6,0},{1,3},{3,5},{5,7},{7,1},{8,10},{10,12},{12... | collective-permute-start | bytes 196616 | tf_op jit(solution)/shard_map/ppermute | solution.py:270
  98.1 4.6 %collective-permute-start.16 = (bf16[256,128]{1,0:T(8,128)(2,1)S(1)}, bf16[256,128]{1,0:T(8,128)(2,1)S(1)}, u32[]{:S(2)}, u32[]{:S(2)}) collective-permute-start(bf16[256,128]{1,0:T(8,128)(2,1)S(1)} %add.27.refs_0_), channel_id=1, source_target_pairs={{0,6},{2,0},{4,2},{6,4},{1,7},{3,1},{5,3},{7,5},{8,14},{10,8},{12,... | collective-permute-start | bytes 196616 | tf_op jit(solution)/shard_map/ppermute | solution.py:270
  102.7 7.5 %collective-permute-start.17 = (bf16[256,128]{1,0:T(8,128)(2,1)S(1)}, bf16[256,128]{1,0:T(8,128)(2,1)S(1)}, u32[]{:S(2)}, u32[]{:S(2)}) collective-permute-start(bf16[256,128]{1,0:T(8,128)(2,1)S(1)} %add.28.refs_1_), channel_id=1, source_target_pairs={{0,16},{8,24},{16,0},{24,8},{1,17},{9,25},{17,1},{25,9},{2,18},{10... | collective-permute-start | bytes 196616 | tf_op jit(solution)/shard_map/ppermute | solution.py:270
  107.5 5.0 %collective-permute-start.18 = (bf16[256,128]{1,0:T(8,128)(2,1)S(1)}, bf16[256,128]{1,0:T(8,128)(2,1)S(1)}, u32[]{:S(2)}, u32[]{:S(2)}) collective-permute-start(bf16[256,128]{1,0:T(8,128)(2,1)S(1)} %add.28.refs_1_), channel_id=1, source_target_pairs={{0,8},{8,16},{16,24},{24,0},{1,9},{9,17},{17,25},{25,1},{2,10},{10... | collective-permute-start | bytes 196616 | tf_op jit(solution)/shard_map/ppermute | solution.py:270
  108.3 4.3 %collective-permute-start.19 = (bf16[256,128]{1,0:T(8,128)(2,1)S(1)}, bf16[256,128]{1,0:T(8,128)(2,1)S(1)}, u32[]{:S(2)}, u32[]{:S(2)}) collective-permute-start(bf16[256,128]{1,0:T(8,128)(2,1)S(1)} %add.28.refs_1_), channel_id=1, source_target_pairs={{0,24},{8,0},{16,8},{24,16},{1,25},{9,1},{17,9},{25,17},{2,26},{10... | collective-permute-start | bytes 196616 | tf_op jit(solution)/shard_map/ppermute | solution.py:270

commit v4 on v3

v4 whole, which is shorter than its diff:
```python
import jax
import jax.numpy as jnp
from jax import lax
from jax.experimental import pallas as pl
from jax.experimental.pallas import tpu as pltpu
from jax.sharding import Mesh, PartitionSpec as P

F32, BF16, I32 = jnp.float32, jnp.bfloat16, jnp.int32
HIGHEST = lax.Precision.HIGHEST
UNROLL = 16
LIST = 240
WORDS = 512
CHUNKS = 8
AHEAD = 8
NEAR = (1, 7, 2, 6, 3, 5)
SMEM = pl.BlockSpec(memory_space=pltpu.SMEM)
VMEM = pl.BlockSpec(memory_space=pltpu.VMEM)
HBM = pl.BlockSpec(memory_space=pltpu.HBM)


def params(mebibytes):
    return pltpu.CompilerParams(vmem_limit_bytes=mebibytes * 2**20)


def stacked(shape, *rows):
    spot = lax.broadcasted_iota(I32, shape, 0)
    out = jnp.zeros(shape, F32)
    for index, row in enumerate(rows):
        out = jnp.where(spot == index, row.astype(F32), out)
    return out.astype(BF16)


def ones_where(mask):
    return jnp.where(mask, 1.0, 0.0).astype(BF16)


def over_lanes(left, right):
    return lax.dot_general(left, right, (((1,), (1,)), ((), ())), preferred_element_type=F32)


def write_list(key, own, bins, part_of_bin, target, source, source_at, slot, valid, earlier, words):
    slots, width = slot.shape[1], words.shape[1]
    member = jnp.logical_and(lax.broadcasted_iota(I32, (bins, slots), 0) == key, valid)
    before = jnp.dot(
        ones_where(member), earlier[:slots, :slots], preferred_element_type=F32
    )
    rank = jnp.sum(jnp.where(member, before, 0.0), axis=0, keepdims=True).astype(I32)
    name = jnp.where(valid, (rank >> 1) * bins + key, -1)
    named = lax.broadcasted_iota(I32, (width, slots), 0) == name
    closes = (rank & 1) == 1
    closing = [jnp.logical_and(jnp.logical_and(closes, valid), own == index) for index in range(2)]
    marks = stacked((8, slots), *[jnp.where(mask, 1.0, 0.0) for mask in closing])
    ahead = jnp.dot(marks, earlier[:slots, :slots], preferred_element_type=F32)
    turn = jnp.where(own == 1, ahead[1:2], ahead[0:1])
    fields = stacked(
        (8, slots), slot >> 1, slot & 1, source, target, jnp.ones_like(slot), turn
    )
    opened = over_lanes(fields, ones_where(jnp.logical_and(named, jnp.logical_not(closes))))
    closed = over_lanes(fields, ones_where(jnp.logical_and(named, closes)))
    lane = lax.broadcasted_iota(I32, (1, width), 1)
    part = part_of_bin(lane & (bins - 1))
    used, paired = opened[4:5] > 0.5, closed[4:5] > 0.5
    masks = [jnp.logical_and(used, part == index) for index in range(2)]
    singles = [jnp.logical_and(mask, jnp.logical_not(paired)) for mask in masks]
    marks = stacked((8, width), *[jnp.where(mask, 1.0, 0.0) for mask in singles])
    ahead = jnp.dot(marks, earlier, preferred_element_type=F32)
    place = jnp.full((1, width), -1, I32)
    for index, (mask, single) in enumerate(zip(masks, singles)):
        couples = jnp.where(jnp.logical_and(mask, paired), 1.0, 0.0)
        alone = jnp.sum(couples, axis=1, keepdims=True) + ahead[index : index + 1]
        spot = jnp.where(single, alone, closed[5:6]).astype(I32) + index * LIST
        place = jnp.where(mask, spot, place)
    other = [jnp.where(paired, closed[index : index + 1], opened[index : index + 1]) for index in range(3)]
    fields = stacked((8, width), *[opened[index : index + 1] for index in range(4)], *other)
    moved = over_lanes(
        fields, ones_where(lax.broadcasted_iota(I32, (width, width), 0) == place)
    ).astype(I32)
    high, low, source_a, target, high_b, low_b, source_b = [moved[k : k + 1] for k in range(7)]
    word = 2 * high + low + ((2 * high_b + low_b) << 9)
    word = word + (target << 18) + (source_a << source_at) + (source_b << 27)
    for index, mask in enumerate(masks):
        length = jnp.sum(jnp.where(mask, 1.0, 0.0), axis=1, keepdims=True).astype(I32)
        word = jnp.where(lane == width - 2 + index, length, word)
    words[...] = word


def prepare_kernel(rows, cols, count, forward_words, backward_words, padded):
    core = lax.axis_index("core")
    padded[...] = jnp.zeros_like(padded)
    padded[0:1, : rows.shape[2]] = rows[0]
    padded[1:2, : rows.shape[2]] = cols[0]
    row, col = padded[0:1], padded[1:2]
    slot = lax.broadcasted_iota(I32, row.shape, 1)
    valid = slot < count[0, 0]
    width = forward_words.shape[1]
    earlier = ones_where(
        lax.broadcasted_iota(I32, (width, width), 0) < lax.broadcasted_iota(I32, (width, width), 1)
    )
    own = jnp.where(((row >> 1) & 1) == core, 1, 0)
    local = ((row >> 2) << 1) + (row & 1)
    shared = (slot, valid, earlier)

    def forward_part(row):
        return jnp.where(((row >> 1) & 1) == core, 1, 0)

    def backward_part(place):
        return 1 - (place & 1)

    write_list(row, own, 64, forward_part, local, col, 23, *shared, forward_words)
    write_list((col << 1) + own, 1 - own, 32, backward_part, col, local, 22, *shared, backward_words)


def weight_of(word, spot, total):
    alone = (word & 511) == ((word >> 9) & 511)
    return jnp.where(spot < total, jnp.where(alone, 0.5, 1.0), 0.0)


def tile_copy(chunk, stored, tiles, sems):
    span = tiles.shape[0] // CHUNKS
    spot = pl.ds(chunk * span, span)
    return pltpu.make_async_copy(stored.at[0, 0, spot], tiles.at[spot], sems.at[chunk])


def start_tiles(chunk, live, stored, tiles, sems):
    span = tiles.shape[0] // CHUNKS

    @pl.when(chunk * span < live)
    def _():
        tile_copy(chunk, stored, tiles, sems).start()


def await_tiles(first, last, live, stored, tiles, sems):
    def body(chunk, carry):
        tile_copy(chunk, stored, tiles, sems).wait()
        start_tiles(chunk + AHEAD, live, stored, tiles, sems)
        return carry

    lax.fori_loop(first, last, body, 0)


def tile_pass(part, words, tiles, multiply, acc, count=None, stored=None, sems=None):
    total = words[0, words.shape[1] - 2 + part]

    def group(step, loaded):
        listed = [words[0, part * LIST + step * UNROLL + offset] for offset in range(UNROLL)]
        if stored is not None:
            span = tiles.shape[0] // CHUNKS
            highest = 0
            for word in listed:
                highest = jnp.maximum(highest, (word >> 9) & 511)
            needed = jnp.maximum(loaded, highest // span + 1)
            await_tiles(loaded, needed, count[0, 0], stored, tiles, sems)
            loaded = needed
        results = []
        for offset, word in enumerate(listed):
            target, product = multiply(word, tiles)
            weight = weight_of(word, step * UNROLL + offset, total)
            results.append((target, product * weight))
        for target, product in results:
            acc[target] += product
        return loaded

    loaded = lax.fori_loop(0, pl.cdiv(total, UNROLL), group, 0)
    if stored is not None:
        span = tiles.shape[0] // CHUNKS
        await_tiles(loaded, pl.cdiv(count[0, 0], span), count[0, 0], stored, tiles, sems)


def forward_product(panel):
    def multiply(word, tiles):
        pair = jnp.concatenate([tiles[word & 511], tiles[(word >> 9) & 511]], axis=1)
        source = jnp.concatenate([panel[(word >> 23) & 15], panel[(word >> 27) & 15]], axis=0)
        return (word >> 18) & 31, jnp.dot(pair, source, preferred_element_type=F32)

    return multiply


def backward_product(grads):
    def multiply(word, tiles):
        pair = jnp.concatenate([tiles[word & 511], tiles[(word >> 9) & 511]], axis=0)
        source = jnp.concatenate([grads[(word >> 22) & 31], grads[(word >> 27) & 31]], axis=0)
        product = lax.dot_general(
            pair, source, (((0,), (0,)), ((), ())), preferred_element_type=F32
        )
        return (word >> 18) & 15, product

    return multiply


def forward_send_kernel(words, tiles, *refs):
    *blocks, low, high, send, panel, acc = refs
    here, rows = lax.axis_index("row"), lax.axis_size("row")
    size = panel.shape[1]
    for distance, block in zip((0, *NEAR), blocks):
        owner = lax.rem(here - distance + rows, rows)
        for part in range(block.shape[0] // size):
            panel[2 * owner + part] = block[pl.ds(part * size, size)]
    opposite = lax.rem(here + rows // 2, rows)
    panel[2 * opposite] = low[...]
    panel[2 * opposite + 1] = high[...]
    acc[...] = jnp.zeros_like(acc)
    tile_pass(0, words, tiles, forward_product(panel), acc)
    send[...] = acc[...].astype(BF16)


def forward_keep_kernel(words, tiles, panel, keep):
    keep[...] = jnp.zeros_like(keep)
    tile_pass(1, words, tiles, forward_product(panel), keep)


def middle_kernel(parts, weight, cotangent, hidden, payload, keep, send):
    peers = parts.shape[0]
    feat = weight.shape[0]
    agg = parts[0].astype(F32)
    for peer in range(1, peers):
        agg += parts[peer].astype(F32)
    wide = weight[...].astype(F32)
    pre = jnp.dot(agg, wide, precision=HIGHEST, preferred_element_type=F32)
    slope, cubic = 0.7978845608028654, 0.044715
    square = pre * pre
    curve = jnp.tanh(slope * pre * (1.0 + cubic * square))
    cdf = 0.5 * (1.0 + curve)
    hidden[...] = (pre * cdf).astype(BF16)
    rate = cdf + 0.5 * pre * (1.0 - curve * curve) * (slope * (1.0 + 3.0 * cubic * square))
    act = cotangent[...].astype(F32) * rate
    grad = lax.dot_general(
        act.astype(BF16), weight[...], (((1,), (1,)), ((), ())), preferred_element_type=F32
    ).astype(BF16)
    for peer in range(peers):
        payload[peer] = grad
    share = lax.dot_general(
        agg, act, (((0,), (0,)), ((), ())), precision=HIGHEST, preferred_element_type=F32
    ).astype(BF16)
    first = lax.axis_index("core") == 0
    keep[...] = jnp.where(first, share[:, :feat], share[:, feat:])
    send[...] = jnp.where(first, share[:, feat:], share[:, :feat])


def backward_first_kernel(words, count, stored, grads, acc, tiles, sems):
    for chunk in range(AHEAD):
        start_tiles(chunk, count[0, 0], stored, tiles, sems)
    acc[...] = jnp.zeros_like(acc)
    tile_pass(0, words, tiles, backward_product(grads), acc, count, stored, sems)


def backward_second_kernel(words, tiles, grads, start, out, acc):
    acc[...] = start[...]
    tile_pass(1, words, tiles, backward_product(grads), acc)
    per_peer = out.shape[1] // acc.shape[1]
    for peer in range(out.shape[0]):
        for part in range(per_peer):
            spot = pl.ds(part * acc.shape[1], acc.shape[1])
            out[peer, spot] = acc[peer * per_peer + part].astype(BF16)


def finish_kernel(scale, parts, mine, other, grad, weight_grad):
    total = parts[0].astype(F32)
    for peer in range(1, parts.shape[0]):
        total += parts[peer].astype(F32)
    grad[...] = total.astype(BF16)
    feat = grad.shape[1]
    left = lax.axis_index("core") == 0
    weight_grad[:, :feat] = jnp.where(left, mine[...], other[...]).astype(F32) * scale
    weight_grad[:, feat:] = jnp.where(left, other[...], mine[...]).astype(F32) * scale


def add_kernel(*refs):
    *terms, total = refs
    total[...] = added(*[term[...] for term in terms]).astype(BF16)


def summed(*terms):
    return pl.pallas_call(
        add_kernel,
        out_shape=jax.ShapeDtypeStruct(terms[0].shape, BF16),
        in_specs=[VMEM] * len(terms),
        out_specs=VMEM,
        compiler_params=params(4),
        name="add",
    )(*terms)


def added(*terms):
    terms = [term.astype(F32) for term in terms]
    while len(terms) > 1:
        terms = [left + right for left, right in zip(terms[::2], terms[1::2])]
    return terms[0]


def swapped(value, axis, step):
    return lax.ppermute(value, axis, [(i, i ^ step) for i in range(lax.axis_size(axis))])


def shifted(value, axis, step):
    size = lax.axis_size(axis)
    return lax.ppermute(value, axis, [(i, (i + step) % size) for i in range(size)])


def per_device(features, weight, adj_tiles, tile_rows, tile_cols, tile_count, cotangent):
    own, feat = features.shape
    hid = weight.shape[1]
    n_row = lax.axis_size("row")
    peers = lax.axis_size("y") * lax.axis_size("x")
    slots, size = adj_tiles.shape[2], adj_tiles.shape[-1]
    half_rows = own * peers // size
    col_tiles = own * n_row // size
    yx = ("y", "x")

    stored = pltpu.with_memory_space_constraint(adj_tiles, pltpu.HBM)
    held = pltpu.VMEM((slots, size, size), BF16)
    list_shape = jax.ShapeDtypeStruct((1, WORDS), I32)
    forward_words, backward_words = pl.pallas_call(
        prepare_kernel,
        out_shape=[list_shape, list_shape],
        in_specs=[VMEM, VMEM, SMEM],
        out_specs=[VMEM, VMEM],
        scratch_shapes=[pltpu.VMEM((8, -(-slots // 128) * 128), I32)],
        compiler_params=params(16),
        cost_estimate=pl.CostEstimate(flops=10**10, bytes_accessed=0, transcendentals=0),
        name="prepare",
    )(
        *[pltpu.with_memory_space_constraint(v, pltpu.HBM) for v in (tile_rows, tile_cols)],
        tile_count,
    )
    resident = pltpu.with_memory_space_constraint(
        adj_tiles.reshape(slots, size, size), pltpu.VMEM
    )
    after, before, after2, before2 = [shifted(features, "row", way) for way in NEAR[:4]]
    after3, before3 = shifted(after2, "row", 1), shifted(before2, "row", 7)
    low, high = shifted(after2[:size], "row", 2), shifted(before2[size:], "row", 6)
    blocks = (features, after, before, after2, before2, after3, before3)
    flops = slots * size * size * feat
    tile_cost = pl.CostEstimate(flops=flops, bytes_accessed=adj_tiles.size, transcendentals=0)
    send, panel = pl.pallas_call(
        forward_send_kernel,
        out_shape=[
            jax.ShapeDtypeStruct((half_rows, size, feat), BF16),
            jax.ShapeDtypeStruct((col_tiles, size, feat), BF16),
        ],
        in_specs=[SMEM, VMEM, *([VMEM] * (n_row + 1))],
        out_specs=[VMEM, VMEM],
        scratch_shapes=[pltpu.VMEM((half_rows, size, feat), F32)],
        compiler_params=params(16),
        cost_estimate=tile_cost,
        name="forward_send",
    )(forward_words, resident, *blocks, low, high)
    got = swapped(send, "core", 1)
    keep = pl.pallas_call(
        forward_keep_kernel,
        out_shape=jax.ShapeDtypeStruct((half_rows, size, feat), F32),
        in_specs=[SMEM, VMEM, VMEM],
        out_specs=VMEM,
        compiler_params=params(16),
        cost_estimate=tile_cost,
        name="forward_keep",
    )(forward_words, resident, panel)
    paired = (keep + got.astype(F32)).astype(BF16).reshape(peers, own, feat)
    parts = lax.all_to_all(paired, yx, 0, 0, tiled=True)
    hidden, payload, local, given = pl.pallas_call(
        middle_kernel,
        out_shape=[
            jax.ShapeDtypeStruct(cotangent.shape, BF16),
            jax.ShapeDtypeStruct((peers, own, feat), BF16),
            jax.ShapeDtypeStruct((feat, hid // 2), BF16),
            jax.ShapeDtypeStruct((feat, hid // 2), BF16),
        ],
        in_specs=[VMEM, VMEM, VMEM],
        out_specs=[VMEM, VMEM, VMEM, VMEM],
        compiler_params=params(16),
        name="middle",
    )(parts, weight, cotangent)

    local = added(local, swapped(given, "core", 1)).astype(BF16)
    local = added(local, swapped(local, "row", 1)).astype(BF16)
    local = added(local, *[shifted(local, "row", step) for step in (4, 2, 6)]).astype(BF16)
    mine = lax.all_to_all(payload, yx, 0, 0, tiled=True).reshape(half_rows, size, feat)
    mine, local = lax.optimization_barrier((mine, local))
    other = swapped(mine, "core", 1)
    beside = swapped(local, "x", 1)
    started, tiles = pl.pallas_call(
        backward_first_kernel,
        out_shape=[jax.ShapeDtypeStruct((col_tiles, size, feat), F32), held],
        in_specs=[SMEM, SMEM, HBM, VMEM],
        out_specs=[VMEM, VMEM],
        scratch_shapes=[pltpu.SemaphoreType.DMA((CHUNKS,))],
        compiler_params=params(16),
        cost_estimate=tile_cost,
        name="backward_first",
    )(backward_words, tile_count, stored, mine)
    col_partial = pl.pallas_call(
        backward_second_kernel,
        out_shape=jax.ShapeDtypeStruct((n_row, own, feat), BF16),
        in_specs=[SMEM, VMEM, VMEM, VMEM],
        out_specs=VMEM,
        scratch_shapes=[pltpu.VMEM((col_tiles, size, feat), F32)],
        compiler_params=params(16),
        cost_estimate=tile_cost,
        name="backward_second",
    )(backward_words, tiles, other, started)
    col_partial, local, beside = lax.optimization_barrier((col_partial, local, beside))
    shares = lax.all_to_all(col_partial, "row", 0, 0, tiled=True)
    local = summed(local, beside)
    local = summed(local, swapped(local, "x", 2))
    local = summed(local, *[shifted(local, "y", step) for step in (2, 1, 3)])
    last = [local, swapped(local, "core", 1)]
    scale = (own * n_row * peers * 2) ** -0.5

    def finish(*refs):
        finish_kernel(scale, *refs)

    input_grad, weight_grad = pl.pallas_call(
        finish,
        out_shape=[
            jax.ShapeDtypeStruct((own, feat), BF16),
            jax.ShapeDtypeStruct((feat, hid), F32),
        ],
        in_specs=[VMEM] * 3,
        out_specs=[VMEM, VMEM],
        compiler_params=params(16),
        name="finish",
    )(shares, *last)
    return (hidden, input_grad, weight_grad)


def solution(mesh):
    side = 4
    fine = Mesh(
        mesh.devices.reshape(mesh.shape["row"], side, side, 2), ("row", "y", "x", "core")
    )
    col = ("y", "x", "core")
    placed = (
        P((*col, "row"), None),
        P(),
        P("row", col, None, None, None),
        P("row", col, None),
        P("row", col, None),
        P("row", col),
        P(("row", *col), None),
    )
    return jax.shard_map(
        per_device,
        mesh=fine,
        in_specs=placed,
        out_specs=(P(("row", *col), None), P((*col, "row"), None), P()),
        check_vma=False,
    )
```

time: 114 us -> 110 us (0.965)
  blocking collectives: 0 us -> 23.9 us
  starting transfers between devices: 67.1 us -> 52 us
  waiting for transfers between devices: 26.4 us -> 12.9 us
    all_to_all x0 -> x1, blocking collectives: none -> 23.9 us  [per_device(): parts = lax.all_to_all(paired, yx, 0, 0, tiled=True)]
    all_to_all x1 -> x0, waiting for transfers between devices: 14.3 us -> none  [per_device(): parts = lax.all_to_all(paired, yx, 0, 0, tiled=True)]
    ppermute x16 -> x14, starting transfers between devices: 40.9 us -> 29.4 us  [shifted(): lax.ppermute(value, axis, [(i, (i + step) % size) for i in range(size)])]
    all_to_all x1 -> x0, starting transfers between devices: 6.88 us -> none  [per_device(): parts = lax.all_to_all(paired, yx, 0, 0, tiled=True)]
    ppermute x4 -> x7, starting transfers between devices: 7.25 us -> 12.3 us  [swapped(): lax.ppermute(value, axis, [(i, i ^ step) for i in range(lax.axis_size(axi...]
    pallas_call x2 -> x1, Pallas kernels: 7.51 us -> 2.55 us  [per_device(): pl.pallas_call(prepare_kernel, out_shape=[list_shape, list_shape], in_spe...]
    ppermute x4 -> x7, waiting for transfers between devices: 3.51 us -> 7.39 us  [swapped(): lax.ppermute(value, axis, [(i, i ^ step) for i in range(lax.axis_size(axi...]
    ppermute x16 -> x14, waiting for transfers between devices: 7.68 us -> 4.07 us  [shifted(): lax.ppermute(value, axis, [(i, (i + step) % size) for i in range(size)])]
  transfers between devices with their start and end apart: 23 -> 23, of which waited for: 8 -> 9; matrix products, arithmetic and copies ran while one was open for 0% -> 0% of each run, Pallas kernels for 12% -> 12%
where the time goes in v4:
time: 110 us; the launch traced here: 109 us
  starting transfers between devices  52 us (47%)
  blocking collectives  23.9 us (22%)
  Pallas kernels  18 us (16%)
  waiting for transfers between devices  12.9 us (12%)
  between operations  1.52 us (1%)
    ppermute x14, starting transfers between devices, shifted(): lax.ppermute(value, axis, [(i, (i + step) % size) for i in range(size)])  29.4 us
    all_to_all x1, blocking collectives, per_device(): parts = lax.all_to_all(paired, yx, 0, 0, tiled=True)  23.9 us
    ppermute x7, starting transfers between devices, swapped(): lax.ppermute(value, axis, [(i, i ^ step) for i in range(lax.axis_size(axi...  12.3 us
    ppermute x7, waiting for transfers between devices, swapped(): lax.ppermute(value, axis, [(i, i ^ step) for i in range(lax.axis_size(axi...  7.39 us
    all_to_all x1, starting transfers between devices, per_device(): shares = lax.all_to_all(col_partial, 'row', 0, 0, tiled=True)  6.59 us
    pallas_call x1, Pallas kernels, per_device(): pl.pallas_call(backward_first_kernel, out_shape=[jax.ShapeDtypeStruct((co...  4.72 us
    ppermute x14, waiting for transfers between devices, shifted(): lax.ppermute(value, axis, [(i, (i + step) % size) for i in range(size)])  4.07 us
    all_to_all x1, starting transfers between devices, per_device(): lax.all_to_all(payload, yx, 0, 0, tiled=True).reshape(half_rows, size, feat)  3.65 us
  transfers between devices with their start and end apart: 23, of which 9 were waited for; matrix products, arithmetic and copies ran while one was open for 0% of the time, Pallas kernels for 12%

profile of v4, /device:TPU:1, one launch (start us, length us, event | category | flops | bytes accessed | tf_op | source)
XLA Modules:
  0.0 108.7 jit_solution(9805324526608316789)
XLA Ops:
  0.6 3.9 %collective-permute-start.2 = (bf16[256,128]{1,0:T(8,128)(2,1)}, bf16[256,128]{1,0:T(8,128)(2,1)S(1)}, u32[]{:S(2)}, u32[]{:S(2)}) collective-permute-start(bf16[256,128]{1,0:T(8,128)(2,1)} %refs_0_.1), channel_id=1, source_target_pairs={{0,64},{32,96},{64,128},{96,160},{128,192},{160,224},{192,0},{224,... | collective-permute-start | bytes 196616 | tf_op jit(solution)/shard_map/ppermute | solution.py:296
  4.5 3.1 %collective-permute-start.3 = (bf16[256,128]{1,0:T(8,128)(2,1)}, bf16[256,128]{1,0:T(8,128)(2,1)S(1)}, u32[]{:S(2)}, u32[]{:S(2)}) collective-permute-start(bf16[256,128]{1,0:T(8,128)(2,1)} %refs_0_.1), channel_id=1, source_target_pairs={{0,192},{32,224},{64,0},{96,32},{128,64},{160,96},{192,128},{224,1... | collective-permute-start | bytes 196616 | tf_op jit(solution)/shard_map/ppermute | solution.py:296
  7.6 0.7 collective-permute-start
  8.4 1.9 %collective-permute-start.1 = (bf16[256,128]{1,0:T(8,128)(2,1)}, bf16[256,128]{1,0:T(8,128)(2,1)S(1)}, u32[]{:S(2)}, u32[]{:S(2)}) collective-permute-start(bf16[256,128]{1,0:T(8,128)(2,1)} %refs_0_.1), channel_id=1, source_target_pairs={{0,224},{32,0},{64,32},{96,64},{128,96},{160,128},{192,160},{224,1... | collective-permute-start | bytes 196616 | tf_op jit(solution)/shard_map/ppermute | solution.py:296
  11.0 0.0 collective-permute-done.2.refs_3_
  11.0 0.2 collective-permute-start.6
  11.2 0.6 collective-permute-done.3.refs_4_
  11.8 0.0 copy-start.1
  11.8 3.0 %collective-permute-start.7 = (bf16[128,128]{1,0:T(8,128)(2,1)S(1)}, bf16[128,128]{1,0:T(8,128)(2,1)S(1)}, u32[]{:S(2)}, u32[]{:S(2)}) collective-permute-start(bf16[128,128]{1,0:T(8,128)(2,1)S(1)} %slice.9), channel_id=1, source_target_pairs={{0,192},{32,224},{64,0},{96,32},{128,64},{160,96},{192,128},{224,1... | collective-permute-start | bytes 98312 | tf_op jit(solution)/shard_map/ppermute | solution.py:296
  14.8 1.0 collective-permute-start.4
  15.8 1.7 %collective-permute-start.5 = (bf16[256,128]{1,0:T(8,128)(2,1)S(1)}, bf16[256,128]{1,0:T(8,128)(2,1)S(1)}, u32[]{:S(2)}, u32[]{:S(2)}) collective-permute-start(bf16[256,128]{1,0:T(8,128)(2,1)S(1)} %collective-permute-done.3.refs_4_), channel_id=1, source_target_pairs={{0,224},{32,0},{64,32},{96,64},{128,96},{160,128},{192,160},{224,1... | collective-permute-start | bytes 196616 | tf_op jit(solution)/shard_map/ppermute | solution.py:296
  17.5 2.6 %prepare.1 = (s32[1,512]{1,0:T(1,128)S(1)}, s32[1,512]{1,0:T(1,128)S(1)}) custom-call(s32[1,1,320]{2,1,0:T(1,128)} %rows.1, s32[1,1,320]{2,1,0:T(1,128)} %cols.1, s32[1,1]{1,0:T(1,128)S(6)} %copy.10.count), custom_call_target="tpu_custom_call" | custom-call | flops 10000000000 | tf_op jit(solution)/shard_map/prepare/pallas_call | solution.py:312
  20.0 0.0 collective-permute-done.6.refs_7_
  20.0 0.0 collective-permute-done.7.refs_8_
  20.1 0.0 collective-permute-done.5.refs_6_
  20.1 2.7 %forward_send.1 = (bf16[32,128,128]{2,1,0:T(8,128)(2,1)S(1)}, bf16[16,128,128]{2,1,0:T(8,128)(2,1)S(1)}) custom-call(s32[1,512]{1,0:T(1,128)S(1)} %get-tuple-element.20.words, bf16[320,128,128]{2,1,0:T(8,128)(2,1)S(1)} %bitcast.5, bf16[256,128]{1,0:T(8,128)(2,1)S(1)} %copy-done.1, bf16[256,128]{1,0:T(8,128)(2,1)S(1)} %collective-permute-done.refs_1_, ...), custom_call_target="tpu_custom_call" | custom-call | flops 671088640 | bytes 5242880 | tf_op jit(solution)/shard_map/forward_send/pallas_call | solution.py:334
  22.8 1.8 %collective-permute-start.8 = (bf16[32,128,128]{2,1,0:T(8,128)(2,1)S(1)}, bf16[32,128,128]{2,1,0:T(8,128)(2,1)S(1)}, u32[]{:S(2)}, u32[]{:S(2)}) collective-permute-start(bf16[32,128,128]{2,1,0:T(8,128)(2,1)S(1)} %get-tuple-element.22), channel_id=1, source_target_pairs={{0,1},{1,0},{2,3},{3,2},{4,5},{5,4},{6,7},{7,6},{8,9},{9,8},{10,11... | collective-permute-start | bytes 3145736 | tf_op jit(solution)/shard_map/ppermute | solution.py:291
  24.6 2.5 %forward_keep.1 = f32[32,128,128]{2,1,0:T(8,128)S(1)} custom-call(s32[1,512]{1,0:T(1,128)S(1)} %get-tuple-element.20.words, bf16[320,128,128]{2,1,0:T(8,128)(2,1)S(1)} %bitcast.6, bf16[16,128,128]{2,1,0:T(8,128)(2,1)S(1)} %get-tuple-element.21.panel), custom_call_target="tpu_custom_call" | custom-call | flops 671088640 | bytes 5242880 | tf_op jit(solution)/shard_map/forward_keep/pallas_call | solution.py:348
  27.1 0.3 add_convert_fusion
  27.5 0.0 copy-start
  27.5 0.0 copy-start.2
  27.5 23.9 %all_to_all.15.parts = bf16[16,256,128]{2,1,0:T(8,128)(2,1)S(1)} all-to-all(bf16[16,256,128]{2,1,0:T(8,128)(2,1)S(1)} %bitcast.9), channel_id=1, replica_groups=mesh['row'=8,'y'=4,'x'=4,'core'=2] {'y','x'}, dimensions={0} | all-to-all | bytes 2097152 | tf_op jit(solution)/shard_map/all_to_all | solution.py:358
  51.4 1.9 %middle.1 = (bf16[256,256]{1,0:T(8,128)(2,1)}, bf16[16,256,128]{2,1,0:T(8,128)(2,1)}, bf16[128,128]{1,0:T(8,128)(2,1)S(1)}, bf16[128,128]{1,0:T(8,128)(2,1)S(1)}) custom-call(bf16[16,256,128]{2,1,0:T(8,128)(2,1)S(1)} %all_to_all.15.parts, bf16[128,256]{1,0:T(8,128)(2,1)S(1)} %copy-done.2, bf16[256,256]{1,0:T(8,128)(2,1)S(1)} %copy-done), custom_call_target="tpu_custom_call" | custom-call | tf_op jit(solution)/shard_map/middle/pallas_call | solution.py:359
  53.2 3.7 %all-to-all-start.1 = ((bf16[16,256,128]{2,1,0:T(8,128)(2,1)}), bf16[16,256,128]{2,1,0:T(8,128)(2,1)S(1)}, u32[]{:S(2)}, u32[]{:S(2)}) async-start(bf16[16,256,128]{2,1,0:T(8,128)(2,1)} %get-tuple-element.25), calls=%async_computation.1 | async-start | bytes 2097152 | tf_op jit(solution)/shard_map/all_to_all | solution.py:376
  56.9 1.9 %collective-permute-start.9 = (bf16[128,128]{1,0:T(8,128)(2,1)S(1)}, bf16[128,128]{1,0:T(8,128)(2,1)S(1)}, u32[]{:S(2)}, u32[]{:S(2)}) collective-permute-start(bf16[128,128]{1,0:T(8,128)(2,1)S(1)} %get-tuple-element.27), channel_id=1, source_target_pairs={{0,1},{1,0},{2,3},{3,2},{4,5},{5,4},{6,7},{7,6},{8,9},{9,8},{10,11... | collective-permute-start | bytes 98312 | tf_op jit(solution)/shard_map/ppermute | solution.py:291
  58.8 0.9 collective-permute-done.9
  59.6 0.5 collective-permute-start.10
  60.1 2.4 %collective-permute-done.10 = bf16[128,128]{1,0:T(8,128)(2,1)S(1)} collective-permute-done((bf16[128,128]{1,0:T(8,128)(2,1)S(1)}, bf16[128,128]{1,0:T(8,128)(2,1)S(1)}, u32[]{:S(2)}, u32[]{:S(2)}) %collective-permute-start.10) | collective-permute-done | bytes 32800 | tf_op jit(solution)/shard_map/ppermute | solution.py:291
  62.5 6.0 %collective-permute-start.11 = (bf16[128,128]{1,0:T(8,128)(2,1)S(1)}, bf16[128,128]{1,0:T(8,128)(2,1)S(1)}, u32[]{:S(2)}, u32[]{:S(2)}) collective-permute-start(bf16[128,128]{1,0:T(8,128)(2,1)S(1)} %add_convert_fusion.2), channel_id=1, source_target_pairs={{0,128},{32,160},{64,192},{96,224},{128,0},{160,32},{192,64},{224,... | collective-permute-start | bytes 98312 | tf_op jit(solution)/shard_map/ppermute | solution.py:296
  68.5 3.6 %collective-permute-start.13 = (bf16[128,128]{1,0:T(8,128)(2,1)S(1)}, bf16[128,128]{1,0:T(8,128)(2,1)S(1)}, u32[]{:S(2)}, u32[]{:S(2)}) collective-permute-start(bf16[128,128]{1,0:T(8,128)(2,1)S(1)} %add_convert_fusion.2), channel_id=1, source_target_pairs={{0,192},{32,224},{64,0},{96,32},{128,64},{160,96},{192,128},{224,1... | collective-permute-start | bytes 98312 | tf_op jit(solution)/shard_map/ppermute | solution.py:296
  72.1 1.9 %collective-permute-done.12 = bf16[128,128]{1,0:T(8,128)(2,1)S(1)} collective-permute-done((bf16[128,128]{1,0:T(8,128)(2,1)S(1)}, bf16[128,128]{1,0:T(8,128)(2,1)S(1)}, u32[]{:S(2)}, u32[]{:S(2)}) %collective-permute-start.12) | collective-permute-done | bytes 32800 | tf_op jit(solution)/shard_map/ppermute | solution.py:296
  74.0 2.3 %collective-permute-start.14 = (bf16[32,128,128]{2,1,0:T(8,128)(2,1)S(1)}, bf16[32,128,128]{2,1,0:T(8,128)(2,1)S(1)}, u32[]{:S(2)}, u32[]{:S(2)}) collective-permute-start(bf16[32,128,128]{2,1,0:T(8,128)(2,1)S(1)} %bitcast.7), channel_id=1, source_target_pairs={{0,1},{1,0},{2,3},{3,2},{4,5},{5,4},{6,7},{7,6},{8,9},{9,8},{10,11... | collective-permute-start | bytes 3145736 | tf_op jit(solution)/shard_map/ppermute | solution.py:291
  76.3 1.5 %collective-permute-start.15 = (bf16[128,128]{1,0:T(8,128)(2,1)S(1)}, bf16[128,128]{1,0:T(8,128)(2,1)S(1)}, u32[]{:S(2)}, u32[]{:S(2)}) collective-permute-start(bf16[128,128]{1,0:T(8,128)(2,1)S(1)} %add_convert_fusion.1.refs_0_), channel_id=1, source_target_pairs={{0,2},{2,0},{4,6},{6,4},{1,3},{3,1},{5,7},{7,5},{8,10},{10,8},{12,... | collective-permute-start | bytes 98312 | tf_op jit(solution)/shard_map/ppermute | solution.py:291
  77.8 4.7 %backward_first.1 = (f32[16,128,128]{2,1,0:T(8,128)S(1)}, bf16[320,128,128]{2,1,0:T(8,128)(2,1)S(1)}) custom-call(s32[1,512]{1,0:T(1,128)S(1)} %get-tuple-element.24.words, s32[1,1]{1,0:T(1,128)S(6)} %copy.10.count, bf16[1,1,320,128,128]{4,3,2,1,0:T(8,128)(2,1)} %stored.1, bf16[32,128,128]{2,1,0:T(8,128)(2,1)S(1)} %bitcast.8), custom_call_target="tpu_custom_call" | custom-call | flops 671088640 | bytes 5242880 | tf_op jit(solution)/shard_map/backward_first/pallas_call | solution.py:380
  82.5 2.9 %backward_second.1 = bf16[8,256,128]{2,1,0:T(8,128)(2,1)} custom-call(s32[1,512]{1,0:T(1,128)S(1)} %get-tuple-element.24.words, bf16[320,128,128]{2,1,0:T(8,128)(2,1)S(1)} %get-tuple-element.29.tiles, bf16[32,128,128]{2,1,0:T(8,128)(2,1)S(1)} %collective-permute-done.14.grads, f32[16,128,128]{2,1,0:T(8,128)S(1)} %get-tuple-element.30.start), custom_call_target="tpu_custom_call" | custom-call | flops 671088640 | bytes 5242880 | tf_op jit(solution)/shard_map/backward_second/pallas_call | solution.py:390
  85.5 6.6 %all-to-all-start.2 = ((bf16[8,256,128]{2,1,0:T(8,128)(2,1)}), bf16[8,256,128]{2,1,0:T(8,128)(2,1)S(1)}, u32[]{:S(2)}, u32[]{:S(2)}) async-start(bf16[8,256,128]{2,1,0:T(8,128)(2,1)} %backward_second.1), calls=%async_computation.2 | async-start | bytes 1048576 | tf_op jit(solution)/shard_map/all_to_all | solution.py:401
  92.1 1.4 %collective-permute-start.16 = (bf16[128,128]{1,0:T(8,128)(2,1)S(1)}, bf16[128,128]{1,0:T(8,128)(2,1)S(1)}, u32[]{:S(2)}, u32[]{:S(2)}) collective-permute-start(bf16[128,128]{1,0:T(8,128)(2,1)S(1)} %add.33.refs_0_), channel_id=1, source_target_pairs={{0,4},{2,6},{4,0},{6,2},{1,5},{3,7},{5,1},{7,3},{8,12},{10,14},{12... | collective-permute-start | bytes 98312 | tf_op jit(solution)/shard_map/ppermute | solution.py:291
  93.5 3.3 %collective-permute-done.16.refs_1_ = bf16[128,128]{1,0:T(8,128)(2,1)S(1)} collective-permute-done((bf16[128,128]{1,0:T(8,128)(2,1)S(1)}, bf16[128,128]{1,0:T(8,128)(2,1)S(1)}, u32[]{:S(2)}, u32[]{:S(2)}) %collective-permute-start.16) | collective-permute-done | bytes 32800 | tf_op jit(solution)/shard_map/ppermute | solution.py:291
  96.8 0.7 collective-permute-start.17
  97.5 2.4 %collective-permute-start.18 = (bf16[128,128]{1,0:T(8,128)(2,1)S(1)}, bf16[128,128]{1,0:T(8,128)(2,1)S(1)}, u32[]{:S(2)}, u32[]{:S(2)}) collective-permute-start(bf16[128,128]{1,0:T(8,128)(2,1)S(1)} %add.34.refs_0_), channel_id=1, source_target_pairs={{0,8},{8,16},{16,24},{24,0},{1,9},{9,17},{17,25},{25,1},{2,10},{10... | collective-permute-start | bytes 98312 | tf_op jit(solution)/shard_map/ppermute | solution.py:296
  99.9 1.2 %collective-permute-start.19 = (bf16[128,128]{1,0:T(8,128)(2,1)S(1)}, bf16[128,128]{1,0:T(8,128)(2,1)S(1)}, u32[]{:S(2)}, u32[]{:S(2)}) collective-permute-start(bf16[128,128]{1,0:T(8,128)(2,1)S(1)} %add.34.refs_0_), channel_id=1, source_target_pairs={{0,24},{8,0},{16,8},{24,16},{1,25},{9,1},{17,9},{25,17},{2,26},{10... | collective-permute-start | bytes 98312 | tf_op jit(solution)/shard_map/ppermute | solution.py:296
  101.1 0.0 collective-permute-done.17.refs_1_
  101.1 1.3 %collective-permute-done.18.refs_2_ = bf16[128,128]{1,0:T(8,128)(2,1)S(1)} collective-permute-done((bf16[128,128]{1,0:T(8,128)(2,1)S(1)}, bf16[128,128]{1,0:T(8,128)(2,1)S(1)}, u32[]{:S(2)}, u32[]{:S(2)}) %collective-permute-start.18) | collective-permute-done | bytes 32800 | tf_op jit(solution)/shard_map/ppermute | solution.py:296
  102.4 0.3 collective-permute-done.19.refs_3_
  102.7 3.0 %collective-permute-start.20 = (bf16[128,128]{1,0:T(8,128)(2,1)S(1)}, bf16[128,128]{1,0:T(8,128)(2,1)S(1)}, u32[]{:S(2)}, u32[]{:S(2)}) collective-permute-start(bf16[128,128]{1,0:T(8,128)(2,1)S(1)} %add.35.refs_1_), channel_id=1, source_target_pairs={{0,1},{1,0},{2,3},{3,2},{4,5},{5,4},{6,7},{7,6},{8,9},{9,8},{10,11... | collective-permute-start | bytes 98312 | tf_op jit(solution)/shard_map/ppermute | solution.py:291
  105.7 0.9 collective-permute-done.20.refs_2_
  106.5 1.5 %all-to-all-done.2.refs_0_ = bf16[8,256,128]{2,1,0:T(8,128)(2,1)S(1)} async-done(((bf16[8,256,128]{2,1,0:T(8,128)(2,1)}), bf16[8,256,128]{2,1,0:T(8,128)(2,1)S(1)}, u32[]{:S(2)}, u32[]{:S(2)}) %all-to-all-start.2) | async-done | bytes 524320 | tf_op jit(solution)/shard_map/all_to_all | solution.py:401
  108.0 0.7 finish.1
  (28 shorter events, 0.1 us)
Async XLA Ops:
  0.6 10.4 %collective-permute-start.2 = (bf16[256,128]{1,0:T(8,128)(2,1)}, bf16[256,128]{1,0:T(8,128)(2,1)S(1)}, u32[]{:S(2)}, u32[]{:S(2)}) collective-permute-start(bf16[256,128]{1,0:T(8,128)(2,1)} %refs_0_.1), channel_id=1, source_target_pairs={{0,64},{32,96},{64,128},{96,160},{128,192},{160,224},{192,0},{224,... | collective-permute-start | bytes 196616 | tf_op jit(solution)/shard_map/ppermute | solution.py:296
  4.5 7.2 %collective-permute-start.3 = (bf16[256,128]{1,0:T(8,128)(2,1)}, bf16[256,128]{1,0:T(8,128)(2,1)S(1)}, u32[]{:S(2)}, u32[]{:S(2)}) collective-permute-start(bf16[256,128]{1,0:T(8,128)(2,1)} %refs_0_.1), channel_id=1, source_target_pairs={{0,192},{32,224},{64,0},{96,32},{128,64},{160,96},{192,128},{224,1... | collective-permute-start | bytes 196616 | tf_op jit(solution)/shard_map/ppermute | solution.py:296
  7.6 8.1 %collective-permute-start = (bf16[256,128]{1,0:T(8,128)(2,1)}, bf16[256,128]{1,0:T(8,128)(2,1)S(1)}, u32[]{:S(2)}, u32[]{:S(2)}) collective-permute-start(bf16[256,128]{1,0:T(8,128)(2,1)} %refs_0_.1), channel_id=1, source_target_pairs={{0,32},{32,64},{64,96},{96,128},{128,160},{160,192},{192,224},{224... | collective-permute-start | bytes 196616 | tf_op jit(solution)/shard_map/ppermute | solution.py:296
  8.4 11.6 %collective-permute-start.1 = (bf16[256,128]{1,0:T(8,128)(2,1)}, bf16[256,128]{1,0:T(8,128)(2,1)S(1)}, u32[]{:S(2)}, u32[]{:S(2)}) collective-permute-start(bf16[256,128]{1,0:T(8,128)(2,1)} %refs_0_.1), channel_id=1, source_target_pairs={{0,224},{32,0},{64,32},{96,64},{128,96},{160,128},{192,160},{224,1... | collective-permute-start | bytes 196616 | tf_op jit(solution)/shard_map/ppermute | solution.py:296
  11.0 9.0 %collective-permute-start.6 = (bf16[128,128]{1,0:T(8,128)(2,1)S(1)}, bf16[128,128]{1,0:T(8,128)(2,1)S(1)}, u32[]{:S(2)}, u32[]{:S(2)}) collective-permute-start(bf16[128,128]{1,0:T(8,128)(2,1)S(1)} %slice.8), channel_id=1, source_target_pairs={{0,64},{32,96},{64,128},{96,160},{128,192},{160,224},{192,0},{224,... | collective-permute-start | bytes 98312 | tf_op jit(solution)/shard_map/ppermute | solution.py:296
  11.8 8.3 %slice-start = ((s8[10485760]{0:T(1024)(128)(4,1)}), s8[4194304]{0:T(1024)(128)(4,1)S(1)}, s32[]{:S(2)}) async-start(s8[10485760]{0:T(1024)(128)(4,1)} %bitcast.3), calls=%async_computation.3 | async-start | bytes 8388608
  11.8 8.3 %slice-start.1 = ((s8[10485760]{0:T(1024)(128)(4,1)}), s8[4194304]{0:T(1024)(128)(4,1)S(1)}, s32[]{:S(2)}) async-start(s8[10485760]{0:T(1024)(128)(4,1)} %bitcast.3), calls=%async_computation.4 | async-start | bytes 8388608
  11.8 8.3 %slice-start.2 = ((s8[10485760]{0:T(1024)(128)(4,1)}), s8[2097152]{0:T(1024)(128)(4,1)S(1)}, s32[]{:S(2)}) async-start(s8[10485760]{0:T(1024)(128)(4,1)} %bitcast.3), calls=%async_computation.5 | async-start | bytes 4194304
  11.8 8.3 %copy-start.1 = (bf16[256,128]{1,0:T(8,128)(2,1)S(1)}, bf16[256,128]{1,0:T(8,128)(2,1)}, u32[]{:S(2)}) copy-start(bf16[256,128]{1,0:T(8,128)(2,1)} %refs_0_.1) | copy-start | bytes 196612
  11.8 8.3 %collective-permute-start.7 = (bf16[128,128]{1,0:T(8,128)(2,1)S(1)}, bf16[128,128]{1,0:T(8,128)(2,1)S(1)}, u32[]{:S(2)}, u32[]{:S(2)}) collective-permute-start(bf16[128,128]{1,0:T(8,128)(2,1)S(1)} %slice.9), channel_id=1, source_target_pairs={{0,192},{32,224},{64,0},{96,32},{128,64},{160,96},{192,128},{224,1... | collective-permute-start | bytes 98312 | tf_op jit(solution)/shard_map/ppermute | solution.py:296
  14.8 5.3 %collective-permute-start.4 = (bf16[256,128]{1,0:T(8,128)(2,1)S(1)}, bf16[256,128]{1,0:T(8,128)(2,1)S(1)}, u32[]{:S(2)}, u32[]{:S(2)}) collective-permute-start(bf16[256,128]{1,0:T(8,128)(2,1)S(1)} %collective-permute-done.2.refs_3_), channel_id=1, source_target_pairs={{0,32},{32,64},{64,96},{96,128},{128,160},{160,192},{192,224},{224... | collective-permute-start | bytes 196616 | tf_op jit(solution)/shard_map/ppermute | solution.py:296
  15.8 4.3 %collective-permute-start.5 = (bf16[256,128]{1,0:T(8,128)(2,1)S(1)}, bf16[256,128]{1,0:T(8,128)(2,1)S(1)}, u32[]{:S(2)}, u32[]{:S(2)}) collective-permute-start(bf16[256,128]{1,0:T(8,128)(2,1)S(1)} %collective-permute-done.3.refs_4_), channel_id=1, source_target_pairs={{0,224},{32,0},{64,32},{96,64},{128,96},{160,128},{192,160},{224,1... | collective-permute-start | bytes 196616 | tf_op jit(solution)/shard_map/ppermute | solution.py:296
  22.8 4.3 %collective-permute-start.8 = (bf16[32,128,128]{2,1,0:T(8,128)(2,1)S(1)}, bf16[32,128,128]{2,1,0:T(8,128)(2,1)S(1)}, u32[]{:S(2)}, u32[]{:S(2)}) collective-permute-start(bf16[32,128,128]{2,1,0:T(8,128)(2,1)S(1)} %get-tuple-element.22), channel_id=1, source_target_pairs={{0,1},{1,0},{2,3},{3,2},{4,5},{5,4},{6,7},{7,6},{8,9},{9,8},{10,11... | collective-permute-start | bytes 3145736 | tf_op jit(solution)/shard_map/ppermute | solution.py:291
  27.5 23.9 %copy-start = (bf16[256,256]{1,0:T(8,128)(2,1)S(1)}, bf16[256,256]{1,0:T(8,128)(2,1)}, u32[]{:S(2)}) copy-start(bf16[256,256]{1,0:T(8,128)(2,1)} %cotangent.1) | copy-start | bytes 393220
  27.5 23.9 %copy-start.2 = (bf16[128,256]{1,0:T(8,128)(2,1)S(1)}, bf16[128,256]{1,0:T(8,128)(2,1)}, u32[]{:S(2)}) copy-start(bf16[128,256]{1,0:T(8,128)(2,1)} %weight.1) | copy-start | bytes 196612
  53.2 20.8 %all-to-all-start.1 = ((bf16[16,256,128]{2,1,0:T(8,128)(2,1)}), bf16[16,256,128]{2,1,0:T(8,128)(2,1)S(1)}, u32[]{:S(2)}, u32[]{:S(2)}) async-start(bf16[16,256,128]{2,1,0:T(8,128)(2,1)} %get-tuple-element.25), calls=%async_computation.1 | async-start | bytes 2097152 | tf_op jit(solution)/shard_map/all_to_all | solution.py:376
  56.9 2.7 %collective-permute-start.9 = (bf16[128,128]{1,0:T(8,128)(2,1)S(1)}, bf16[128,128]{1,0:T(8,128)(2,1)S(1)}, u32[]{:S(2)}, u32[]{:S(2)}) collective-permute-start(bf16[128,128]{1,0:T(8,128)(2,1)S(1)} %get-tuple-element.27), channel_id=1, source_target_pairs={{0,1},{1,0},{2,3},{3,2},{4,5},{5,4},{6,7},{7,6},{8,9},{9,8},{10,11... | collective-permute-start | bytes 98312 | tf_op jit(solution)/shard_map/ppermute | solution.py:291
  59.6 2.9 %collective-permute-start.10 = (bf16[128,128]{1,0:T(8,128)(2,1)S(1)}, bf16[128,128]{1,0:T(8,128)(2,1)S(1)}, u32[]{:S(2)}, u32[]{:S(2)}) collective-permute-start(bf16[128,128]{1,0:T(8,128)(2,1)S(1)} %add_convert_fusion.3), channel_id=1, source_target_pairs={{0,32},{32,0},{64,96},{96,64},{128,160},{160,128},{192,224},{224,1... | collective-permute-start | bytes 98312 | tf_op jit(solution)/shard_map/ppermute | solution.py:291
  62.5 9.6 %collective-permute-start.11 = (bf16[128,128]{1,0:T(8,128)(2,1)S(1)}, bf16[128,128]{1,0:T(8,128)(2,1)S(1)}, u32[]{:S(2)}, u32[]{:S(2)}) collective-permute-start(bf16[128,128]{1,0:T(8,128)(2,1)S(1)} %add_convert_fusion.2), channel_id=1, source_target_pairs={{0,128},{32,160},{64,192},{96,224},{128,0},{160,32},{192,64},{224,... | collective-permute-start | bytes 98312 | tf_op jit(solution)/shard_map/ppermute | solution.py:296
  68.5 5.5 %collective-permute-start.12 = (bf16[128,128]{1,0:T(8,128)(2,1)S(1)}, bf16[128,128]{1,0:T(8,128)(2,1)S(1)}, u32[]{:S(2)}, u32[]{:S(2)}) collective-permute-start(bf16[128,128]{1,0:T(8,128)(2,1)S(1)} %add_convert_fusion.2), channel_id=1, source_target_pairs={{0,64},{32,96},{64,128},{96,160},{128,192},{160,224},{192,0},{224,... | collective-permute-start | bytes 98312 | tf_op jit(solution)/shard_map/ppermute | solution.py:296
  68.5 5.5 %collective-permute-start.13 = (bf16[128,128]{1,0:T(8,128)(2,1)S(1)}, bf16[128,128]{1,0:T(8,128)(2,1)S(1)}, u32[]{:S(2)}, u32[]{:S(2)}) collective-permute-start(bf16[128,128]{1,0:T(8,128)(2,1)S(1)} %add_convert_fusion.2), channel_id=1, source_target_pairs={{0,192},{32,224},{64,0},{96,32},{128,64},{160,96},{192,128},{224,1... | collective-permute-start | bytes 98312 | tf_op jit(solution)/shard_map/ppermute | solution.py:296
  74.0 8.5 %collective-permute-start.14 = (bf16[32,128,128]{2,1,0:T(8,128)(2,1)S(1)}, bf16[32,128,128]{2,1,0:T(8,128)(2,1)S(1)}, u32[]{:S(2)}, u32[]{:S(2)}) collective-permute-start(bf16[32,128,128]{2,1,0:T(8,128)(2,1)S(1)} %bitcast.7), channel_id=1, source_target_pairs={{0,1},{1,0},{2,3},{3,2},{4,5},{5,4},{6,7},{7,6},{8,9},{9,8},{10,11... | collective-permute-start | bytes 3145736 | tf_op jit(solution)/shard_map/ppermute | solution.py:291
  76.3 9.1 %collective-permute-start.15 = (bf16[128,128]{1,0:T(8,128)(2,1)S(1)}, bf16[128,128]{1,0:T(8,128)(2,1)S(1)}, u32[]{:S(2)}, u32[]{:S(2)}) collective-permute-start(bf16[128,128]{1,0:T(8,128)(2,1)S(1)} %add_convert_fusion.1.refs_0_), channel_id=1, source_target_pairs={{0,2},{2,0},{4,6},{6,4},{1,3},{3,1},{5,7},{7,5},{8,10},{10,8},{12,... | collective-permute-start | bytes 98312 | tf_op jit(solution)/shard_map/ppermute | solution.py:291
  85.5 22.5 %all-to-all-start.2 = ((bf16[8,256,128]{2,1,0:T(8,128)(2,1)}), bf16[8,256,128]{2,1,0:T(8,128)(2,1)S(1)}, u32[]{:S(2)}, u32[]{:S(2)}) async-start(bf16[8,256,128]{2,1,0:T(8,128)(2,1)} %backward_second.1), calls=%async_computation.2 | async-start | bytes 1048576 | tf_op jit(solution)/shard_map/all_to_all | solution.py:401
  92.1 4.7 %collective-permute-start.16 = (bf16[128,128]{1,0:T(8,128)(2,1)S(1)}, bf16[128,128]{1,0:T(8,128)(2,1)S(1)}, u32[]{:S(2)}, u32[]{:S(2)}) collective-permute-start(bf16[128,128]{1,0:T(8,128)(2,1)S(1)} %add.33.refs_0_), channel_id=1, source_target_pairs={{0,4},{2,6},{4,0},{6,2},{1,5},{3,7},{5,1},{7,3},{8,12},{10,14},{12... | collective-permute-start | bytes 98312 | tf_op jit(solution)/shard_map/ppermute | solution.py:291
  96.8 4.4 %collective-permute-start.17 = (bf16[128,128]{1,0:T(8,128)(2,1)S(1)}, bf16[128,128]{1,0:T(8,128)(2,1)S(1)}, u32[]{:S(2)}, u32[]{:S(2)}) collective-permute-start(bf16[128,128]{1,0:T(8,128)(2,1)S(1)} %add.34.refs_0_), channel_id=1, source_target_pairs={{0,16},{8,24},{16,0},{24,8},{1,17},{9,25},{17,1},{25,9},{2,18},{10... | collective-permute-start | bytes 98312 | tf_op jit(solution)/shard_map/ppermute | solution.py:296
  97.5 4.9 %collective-permute-start.18 = (bf16[128,128]{1,0:T(8,128)(2,1)S(1)}, bf16[128,128]{1,0:T(8,128)(2,1)S(1)}, u32[]{:S(2)}, u32[]{:S(2)}) collective-permute-start(bf16[128,128]{1,0:T(8,128)(2,1)S(1)} %add.34.refs_0_), channel_id=1, source_target_pairs={{0,8},{8,16},{16,24},{24,0},{1,9},{9,17},{17,25},{25,1},{2,10},{10... | collective-permute-start | bytes 98312 | tf_op jit(solution)/shard_map/ppermute | solution.py:296
  99.9 2.8 %collective-permute-start.19 = (bf16[128,128]{1,0:T(8,128)(2,1)S(1)}, bf16[128,128]{1,0:T(8,128)(2,1)S(1)}, u32[]{:S(2)}, u32[]{:S(2)}) collective-permute-start(bf16[128,128]{1,0:T(8,128)(2,1)S(1)} %add.34.refs_0_), channel_id=1, source_target_pairs={{0,24},{8,0},{16,8},{24,16},{1,25},{9,1},{17,9},{25,17},{2,26},{10... | collective-permute-start | bytes 98312 | tf_op jit(solution)/shard_map/ppermute | solution.py:296
  102.7 3.8 %collective-permute-start.20 = (bf16[128,128]{1,0:T(8,128)(2,1)S(1)}, bf16[128,128]{1,0:T(8,128)(2,1)S(1)}, u32[]{:S(2)}, u32[]{:S(2)}) collective-permute-start(bf16[128,128]{1,0:T(8,128)(2,1)S(1)} %add.35.refs_1_), channel_id=1, source_target_pairs={{0,1},{1,0},{2,3},{3,2},{4,5},{5,4},{6,7},{7,6},{8,9},{9,8},{10,11... | collective-permute-start | bytes 98312 | tf_op jit(solution)/shard_map/ppermute | solution.py:291

commit v5 on v4

--- a/solution.py
+++ b/solution.py
@@ -6,13 +6,12 @@
 from jax.sharding import Mesh, PartitionSpec as P
 
 F32, BF16, I32 = jnp.float32, jnp.bfloat16, jnp.int32
-HIGHEST = lax.Precision.HIGHEST
 UNROLL = 16
 LIST = 240
 WORDS = 512
 CHUNKS = 8
 AHEAD = 8
-NEAR = (1, 7, 2, 6, 3, 5)
+NEAR = (1, 7, 2, 6, 3, 5, 4)
 SMEM = pl.BlockSpec(memory_space=pltpu.SMEM)
 VMEM = pl.BlockSpec(memory_space=pltpu.VMEM)
 HBM = pl.BlockSpec(memory_space=pltpu.HBM)
@@ -188,16 +187,13 @@
 
 
 def forward_send_kernel(words, tiles, *refs):
-    *blocks, low, high, send, panel, acc = refs
+    *blocks, send, panel, acc = refs
     here, rows = lax.axis_index("row"), lax.axis_size("row")
     size = panel.shape[1]
     for distance, block in zip((0, *NEAR), blocks):
         owner = lax.rem(here - distance + rows, rows)
         for part in range(block.shape[0] // size):
             panel[2 * owner + part] = block[pl.ds(part * size, size)]
-    opposite = lax.rem(here + rows // 2, rows)
-    panel[2 * opposite] = low[...]
-    panel[2 * opposite + 1] = high[...]
     acc[...] = jnp.zeros_like(acc)
     tile_pass(0, words, tiles, forward_product(panel), acc)
     send[...] = acc[...].astype(BF16)
@@ -214,8 +210,11 @@
     agg = parts[0].astype(F32)
     for peer in range(1, peers):
         agg += parts[peer].astype(F32)
-    wide = weight[...].astype(F32)
-    pre = jnp.dot(agg, wide, precision=HIGHEST, preferred_element_type=F32)
+    high = agg.astype(BF16)
+    rest = agg - high.astype(F32)
+    low = rest.astype(BF16)
+    lowest = (rest - low.astype(F32)).astype(BF16)
+    pre = sum(jnp.dot(term, weight[...], preferred_element_type=F32) for term in (lowest, low, high))
     slope, cubic = 0.7978845608028654, 0.044715
     square = pre * pre
     curve = jnp.tanh(slope * pre * (1.0 + cubic * square))
@@ -229,7 +228,7 @@
     for peer in range(peers):
         payload[peer] = grad
     share = lax.dot_general(
-        agg, act, (((0,), (0,)), ((), ())), precision=HIGHEST, preferred_element_type=F32
+        high, act.astype(BF16), (((0,), (0,)), ((), ())), preferred_element_type=F32
     ).astype(BF16)
     first = lax.axis_index("core") == 0
     keep[...] = jnp.where(first, share[:, :feat], share[:, feat:])
@@ -327,8 +326,8 @@
     )
     after, before, after2, before2 = [shifted(features, "row", way) for way in NEAR[:4]]
     after3, before3 = shifted(after2, "row", 1), shifted(before2, "row", 7)
-    low, high = shifted(after2[:size], "row", 2), shifted(before2[size:], "row", 6)
-    blocks = (features, after, before, after2, before2, after3, before3)
+    opposite = shifted(after2, "row", 2)
+    blocks = (features, after, before, after2, before2, after3, before3, opposite)
     flops = slots * size * size * feat
     tile_cost = pl.CostEstimate(flops=flops, bytes_accessed=adj_tiles.size, transcendentals=0)
     send, panel = pl.pallas_call(
@@ -337,13 +336,13 @@
             jax.ShapeDtypeStruct((half_rows, size, feat), BF16),
             jax.ShapeDtypeStruct((col_tiles, size, feat), BF16),
         ],
-        in_specs=[SMEM, VMEM, *([VMEM] * (n_row + 1))],
+        in_specs=[SMEM, VMEM, *([VMEM] * n_row)],
         out_specs=[VMEM, VMEM],
         scratch_shapes=[pltpu.VMEM((half_rows, size, feat), F32)],
         compiler_params=params(16),
         cost_estimate=tile_cost,
         name="forward_send",
-    )(forward_words, resident, *blocks, low, high)
+    )(forward_words, resident, *blocks)
     got = swapped(send, "core", 1)
     keep = pl.pallas_call(
         forward_keep_kernel,

time: 110 us -> 107 us (0.973)
  waiting for transfers between devices: 12.9 us -> 10.3 us
  starting transfers between devices: 52 us -> 50.9 us
    ppermute x7, starting transfers between devices: 12.3 us -> 15 us  [swapped(): lax.ppermute(value, axis, [(i, i ^ step) for i in range(lax.axis_size(axi...]
    ppermute x7, waiting for transfers between devices: 7.39 us -> 4.69 us  [swapped(): lax.ppermute(value, axis, [(i, i ^ step) for i in range(lax.axis_size(axi...]
    ppermute x14 -> x13, starting transfers between devices: 29.4 us -> 27.4 us  [shifted(): lax.ppermute(value, axis, [(i, (i + step) % size) for i in range(size)])]
    all_to_all x1, starting transfers between devices: 6.59 us -> 4.78 us  [per_device(): shares = lax.all_to_all(col_partial, 'row', 0, 0, tiled=True)]
    ppermute x14 -> x13, waiting for transfers between devices: 4.07 us -> 4.66 us  [shifted(): lax.ppermute(value, axis, [(i, (i + step) % size) for i in range(size)])]
  transfers between devices with their start and end apart: 23 -> 22, of which waited for: 9 -> 9; matrix products, arithmetic and copies ran while one was open for 0% -> 0% of each run, Pallas kernels for 12% -> 12%
where the time goes in v5:
time: 107 us; the launch traced here: 105 us
  starting transfers between devices  50.9 us (48%)
  blocking collectives  24.3 us (23%)
  Pallas kernels  17.9 us (17%)
  waiting for transfers between devices  10.3 us (10%)
  between operations  1.64 us (2%)
    ppermute x13, starting transfers between devices, shifted(): lax.ppermute(value, axis, [(i, (i + step) % size) for i in range(size)])  27.4 us
    all_to_all x1, blocking collectives, per_device(): parts = lax.all_to_all(paired, yx, 0, 0, tiled=True)  24.3 us
    ppermute x7, starting transfers between devices, swapped(): lax.ppermute(value, axis, [(i, i ^ step) for i in range(lax.axis_size(axi...  15 us
    pallas_call x1, Pallas kernels, per_device(): pl.pallas_call(backward_first_kernel, out_shape=[jax.ShapeDtypeStruct((co...  4.85 us
    all_to_all x1, starting transfers between devices, per_device(): shares = lax.all_to_all(col_partial, 'row', 0, 0, tiled=True)  4.78 us
    ppermute x7, waiting for transfers between devices, swapped(): lax.ppermute(value, axis, [(i, i ^ step) for i in range(lax.axis_size(axi...  4.69 us
    ppermute x13, waiting for transfers between devices, shifted(): lax.ppermute(value, axis, [(i, (i + step) % size) for i in range(size)])  4.66 us
    all_to_all x1, starting transfers between devices, per_device(): lax.all_to_all(payload, yx, 0, 0, tiled=True).reshape(half_rows, size, feat)  3.65 us
  transfers between devices with their start and end apart: 22, of which 9 were waited for; matrix products, arithmetic and copies ran while one was open for 0% of the time, Pallas kernels for 12%

profile of v5, /device:TPU:1, one launch (start us, length us, event | category | flops | bytes accessed | tf_op | source)
XLA Modules:
  0.0 105.5 jit_solution(17192565584890351565)
XLA Ops:
  0.6 3.9 %collective-permute-start.2 = (bf16[256,128]{1,0:T(8,128)(2,1)}, bf16[256,128]{1,0:T(8,128)(2,1)S(1)}, u32[]{:S(2)}, u32[]{:S(2)}) collective-permute-start(bf16[256,128]{1,0:T(8,128)(2,1)} %refs_0_.1), channel_id=1, source_target_pairs={{0,64},{32,96},{64,128},{96,160},{128,192},{160,224},{192,0},{224,... | collective-permute-start | bytes 196616 | tf_op jit(solution)/shard_map/ppermute | solution.py:295
  4.5 3.1 %collective-permute-start.3 = (bf16[256,128]{1,0:T(8,128)(2,1)}, bf16[256,128]{1,0:T(8,128)(2,1)S(1)}, u32[]{:S(2)}, u32[]{:S(2)}) collective-permute-start(bf16[256,128]{1,0:T(8,128)(2,1)} %refs_0_.1), channel_id=1, source_target_pairs={{0,192},{32,224},{64,0},{96,32},{128,64},{160,96},{192,128},{224,1... | collective-permute-start | bytes 196616 | tf_op jit(solution)/shard_map/ppermute | solution.py:295
  7.6 0.7 collective-permute-start
  8.4 1.9 %collective-permute-start.1 = (bf16[256,128]{1,0:T(8,128)(2,1)}, bf16[256,128]{1,0:T(8,128)(2,1)S(1)}, u32[]{:S(2)}, u32[]{:S(2)}) collective-permute-start(bf16[256,128]{1,0:T(8,128)(2,1)} %refs_0_.1), channel_id=1, source_target_pairs={{0,224},{32,0},{64,32},{96,64},{128,96},{160,128},{192,160},{224,1... | collective-permute-start | bytes 196616 | tf_op jit(solution)/shard_map/ppermute | solution.py:295
  11.1 0.0 slice-start.2
  11.2 0.9 collective-permute-start.4
  12.0 1.5 %collective-permute-start.6 = (bf16[256,128]{1,0:T(8,128)(2,1)S(1)}, bf16[256,128]{1,0:T(8,128)(2,1)S(1)}, u32[]{:S(2)}, u32[]{:S(2)}) collective-permute-start(bf16[256,128]{1,0:T(8,128)(2,1)S(1)} %collective-permute-done.2.refs_3_), channel_id=1, source_target_pairs={{0,64},{32,96},{64,128},{96,160},{128,192},{160,224},{192,0},{224,... | collective-permute-start | bytes 196616 | tf_op jit(solution)/shard_map/ppermute | solution.py:295
  13.5 0.0 collective-permute-done.3.refs_4_
  13.5 0.9 collective-permute-start.5
  14.4 2.6 %prepare.1 = (s32[1,512]{1,0:T(1,128)S(1)}, s32[1,512]{1,0:T(1,128)S(1)}) custom-call(s32[1,1,320]{2,1,0:T(1,128)} %rows.1, s32[1,1,320]{2,1,0:T(1,128)} %cols.1, s32[1,1]{1,0:T(1,128)S(6)} %copy.10.count), custom_call_target="tpu_custom_call" | custom-call | flops 10000000000 | tf_op jit(solution)/shard_map/prepare/pallas_call | solution.py:311
  17.0 0.0 collective-permute-done.refs_1_
  17.0 0.0 collective-permute-done.4.refs_5_
  17.0 1.1 %collective-permute-done.6.refs_7_ = bf16[256,128]{1,0:T(8,128)(2,1)S(1)} collective-permute-done((bf16[256,128]{1,0:T(8,128)(2,1)S(1)}, bf16[256,128]{1,0:T(8,128)(2,1)S(1)}, u32[]{:S(2)}, u32[]{:S(2)}) %collective-permute-start.6) | collective-permute-done | bytes 65568 | tf_op jit(solution)/shard_map/ppermute | solution.py:295
  18.1 0.0 collective-permute-done.5.refs_6_
  18.2 2.7 %forward_send.1 = (bf16[32,128,128]{2,1,0:T(8,128)(2,1)S(1)}, bf16[16,128,128]{2,1,0:T(8,128)(2,1)S(1)}) custom-call(s32[1,512]{1,0:T(1,128)S(1)} %get-tuple-element.20.words, bf16[320,128,128]{2,1,0:T(8,128)(2,1)S(1)} %bitcast.5, bf16[256,128]{1,0:T(8,128)(2,1)S(1)} %copy-done.1, bf16[256,128]{1,0:T(8,128)(2,1)S(1)} %collective-permute-done.refs_1_, ...), custom_call_target="tpu_custom_call" | custom-call | flops 671088640 | bytes 5242880 | tf_op jit(solution)/shard_map/forward_send/pallas_call | solution.py:333
  20.8 1.7 %collective-permute-start.7 = (bf16[32,128,128]{2,1,0:T(8,128)(2,1)S(1)}, bf16[32,128,128]{2,1,0:T(8,128)(2,1)S(1)}, u32[]{:S(2)}, u32[]{:S(2)}) collective-permute-start(bf16[32,128,128]{2,1,0:T(8,128)(2,1)S(1)} %get-tuple-element.22), channel_id=1, source_target_pairs={{0,1},{1,0},{2,3},{3,2},{4,5},{5,4},{6,7},{7,6},{8,9},{9,8},{10,11... | collective-permute-start | bytes 3145736 | tf_op jit(solution)/shard_map/ppermute | solution.py:290
  22.5 2.5 %forward_keep.1 = f32[32,128,128]{2,1,0:T(8,128)S(1)} custom-call(s32[1,512]{1,0:T(1,128)S(1)} %get-tuple-element.20.words, bf16[320,128,128]{2,1,0:T(8,128)(2,1)S(1)} %bitcast.6, bf16[16,128,128]{2,1,0:T(8,128)(2,1)S(1)} %get-tuple-element.21.panel), custom_call_target="tpu_custom_call" | custom-call | flops 671088640 | bytes 5242880 | tf_op jit(solution)/shard_map/forward_keep/pallas_call | solution.py:347
  25.0 0.3 add_convert_fusion
  25.4 0.0 copy-start
  25.4 0.0 copy-start.2
  25.4 24.3 %all_to_all.15.parts = bf16[16,256,128]{2,1,0:T(8,128)(2,1)S(1)} all-to-all(bf16[16,256,128]{2,1,0:T(8,128)(2,1)S(1)} %bitcast.9), channel_id=1, replica_groups=mesh['row'=8,'y'=4,'x'=4,'core'=2] {'y','x'}, dimensions={0} | all-to-all | bytes 2097152 | tf_op jit(solution)/shard_map/all_to_all | solution.py:357
  49.7 1.6 %middle.1 = (bf16[256,256]{1,0:T(8,128)(2,1)}, bf16[16,256,128]{2,1,0:T(8,128)(2,1)}, bf16[128,128]{1,0:T(8,128)(2,1)S(1)}, bf16[128,128]{1,0:T(8,128)(2,1)S(1)}) custom-call(bf16[16,256,128]{2,1,0:T(8,128)(2,1)S(1)} %all_to_all.15.parts, bf16[128,256]{1,0:T(8,128)(2,1)S(1)} %copy-done.2, bf16[256,256]{1,0:T(8,128)(2,1)S(1)} %copy-done), custom_call_target="tpu_custom_call" | custom-call | tf_op jit(solution)/shard_map/middle/pallas_call | solution.py:358
  51.3 3.7 %all-to-all-start.1 = ((bf16[16,256,128]{2,1,0:T(8,128)(2,1)}), bf16[16,256,128]{2,1,0:T(8,128)(2,1)S(1)}, u32[]{:S(2)}, u32[]{:S(2)}) async-start(bf16[16,256,128]{2,1,0:T(8,128)(2,1)} %get-tuple-element.25), calls=%async_computation.1 | async-start | bytes 2097152 | tf_op jit(solution)/shard_map/all_to_all | solution.py:375
  54.9 2.4 %collective-permute-start.8 = (bf16[128,128]{1,0:T(8,128)(2,1)S(1)}, bf16[128,128]{1,0:T(8,128)(2,1)S(1)}, u32[]{:S(2)}, u32[]{:S(2)}) collective-permute-start(bf16[128,128]{1,0:T(8,128)(2,1)S(1)} %get-tuple-element.27), channel_id=1, source_target_pairs={{0,1},{1,0},{2,3},{3,2},{4,5},{5,4},{6,7},{7,6},{8,9},{9,8},{10,11... | collective-permute-start | bytes 98312 | tf_op jit(solution)/shard_map/ppermute | solution.py:290
  57.3 0.9 collective-permute-done.8
  58.2 2.3 %collective-permute-start.9 = (bf16[128,128]{1,0:T(8,128)(2,1)S(1)}, bf16[128,128]{1,0:T(8,128)(2,1)S(1)}, u32[]{:S(2)}, u32[]{:S(2)}) collective-permute-start(bf16[128,128]{1,0:T(8,128)(2,1)S(1)} %add_convert_fusion.3), channel_id=1, source_target_pairs={{0,32},{32,0},{64,96},{96,64},{128,160},{160,128},{192,224},{224,1... | collective-permute-start | bytes 98312 | tf_op jit(solution)/shard_map/ppermute | solution.py:290
  60.5 1.6 %collective-permute-done.9 = bf16[128,128]{1,0:T(8,128)(2,1)S(1)} collective-permute-done((bf16[128,128]{1,0:T(8,128)(2,1)S(1)}, bf16[128,128]{1,0:T(8,128)(2,1)S(1)}, u32[]{:S(2)}, u32[]{:S(2)}) %collective-permute-start.9) | collective-permute-done | bytes 32800 | tf_op jit(solution)/shard_map/ppermute | solution.py:290
  62.1 2.6 %collective-permute-start.10 = (bf16[128,128]{1,0:T(8,128)(2,1)S(1)}, bf16[128,128]{1,0:T(8,128)(2,1)S(1)}, u32[]{:S(2)}, u32[]{:S(2)}) collective-permute-start(bf16[128,128]{1,0:T(8,128)(2,1)S(1)} %add_convert_fusion.2), channel_id=1, source_target_pairs={{0,128},{32,160},{64,192},{96,224},{128,0},{160,32},{192,64},{224,... | collective-permute-start | bytes 98312 | tf_op jit(solution)/shard_map/ppermute | solution.py:295
  64.8 0.0 collective-permute-start.11
  64.8 3.6 %collective-permute-start.12 = (bf16[128,128]{1,0:T(8,128)(2,1)S(1)}, bf16[128,128]{1,0:T(8,128)(2,1)S(1)}, u32[]{:S(2)}, u32[]{:S(2)}) collective-permute-start(bf16[128,128]{1,0:T(8,128)(2,1)S(1)} %add_convert_fusion.2), channel_id=1, source_target_pairs={{0,192},{32,224},{64,0},{96,32},{128,64},{160,96},{192,128},{224,1... | collective-permute-start | bytes 98312 | tf_op jit(solution)/shard_map/ppermute | solution.py:295
  68.3 1.0 collective-permute-done.10
  69.3 1.2 %collective-permute-done.11 = bf16[128,128]{1,0:T(8,128)(2,1)S(1)} collective-permute-done((bf16[128,128]{1,0:T(8,128)(2,1)S(1)}, bf16[128,128]{1,0:T(8,128)(2,1)S(1)}, u32[]{:S(2)}, u32[]{:S(2)}) %collective-permute-start.11) | collective-permute-done | bytes 32800 | tf_op jit(solution)/shard_map/ppermute | solution.py:295
  70.6 0.0 all-to-all-done.1
  70.6 2.8 %collective-permute-start.13 = (bf16[32,128,128]{2,1,0:T(8,128)(2,1)S(1)}, bf16[32,128,128]{2,1,0:T(8,128)(2,1)S(1)}, u32[]{:S(2)}, u32[]{:S(2)}) collective-permute-start(bf16[32,128,128]{2,1,0:T(8,128)(2,1)S(1)} %bitcast.7), channel_id=1, source_target_pairs={{0,1},{1,0},{2,3},{3,2},{4,5},{5,4},{6,7},{7,6},{8,9},{9,8},{10,11... | collective-permute-start | bytes 3145736 | tf_op jit(solution)/shard_map/ppermute | solution.py:290
  73.4 0.8 collective-permute-start.14
  74.1 4.8 %backward_first.1 = (f32[16,128,128]{2,1,0:T(8,128)S(1)}, bf16[320,128,128]{2,1,0:T(8,128)(2,1)S(1)}) custom-call(s32[1,512]{1,0:T(1,128)S(1)} %get-tuple-element.24.words, s32[1,1]{1,0:T(1,128)S(6)} %copy.10.count, bf16[1,1,320,128,128]{4,3,2,1,0:T(8,128)(2,1)} %stored.1, bf16[32,128,128]{2,1,0:T(8,128)(2,1)S(1)} %bitcast.8), custom_call_target="tpu_custom_call" | custom-call | flops 671088640 | bytes 5242880 | tf_op jit(solution)/shard_map/backward_first/pallas_call | solution.py:379
  79.0 0.0 collective-permute-done.13.grads
  79.0 2.9 %backward_second.1 = bf16[8,256,128]{2,1,0:T(8,128)(2,1)} custom-call(s32[1,512]{1,0:T(1,128)S(1)} %get-tuple-element.24.words, bf16[320,128,128]{2,1,0:T(8,128)(2,1)S(1)} %get-tuple-element.29.tiles, bf16[32,128,128]{2,1,0:T(8,128)(2,1)S(1)} %collective-permute-done.13.grads, f32[16,128,128]{2,1,0:T(8,128)S(1)} %get-tuple-element.30.start), custom_call_target="tpu_custom_call" | custom-call | flops 671088640 | bytes 5242880 | tf_op jit(solution)/shard_map/backward_second/pallas_call | solution.py:389
  82.0 4.8 %all-to-all-start.2 = ((bf16[8,256,128]{2,1,0:T(8,128)(2,1)}), bf16[8,256,128]{2,1,0:T(8,128)(2,1)S(1)}, u32[]{:S(2)}, u32[]{:S(2)}) async-start(bf16[8,256,128]{2,1,0:T(8,128)(2,1)} %backward_second.1), calls=%async_computation.2 | async-start | bytes 1048576 | tf_op jit(solution)/shard_map/all_to_all | solution.py:400
  86.8 3.0 %collective-permute-start.15 = (bf16[128,128]{1,0:T(8,128)(2,1)S(1)}, bf16[128,128]{1,0:T(8,128)(2,1)S(1)}, u32[]{:S(2)}, u32[]{:S(2)}) collective-permute-start(bf16[128,128]{1,0:T(8,128)(2,1)S(1)} %add.33.refs_0_), channel_id=1, source_target_pairs={{0,4},{2,6},{4,0},{6,2},{1,5},{3,7},{5,1},{7,3},{8,12},{10,14},{12... | collective-permute-start | bytes 98312 | tf_op jit(solution)/shard_map/ppermute | solution.py:290
  89.7 1.4 %collective-permute-done.15.refs_1_ = bf16[128,128]{1,0:T(8,128)(2,1)S(1)} collective-permute-done((bf16[128,128]{1,0:T(8,128)(2,1)S(1)}, bf16[128,128]{1,0:T(8,128)(2,1)S(1)}, u32[]{:S(2)}, u32[]{:S(2)}) %collective-permute-start.15) | collective-permute-done | bytes 32800 | tf_op jit(solution)/shard_map/ppermute | solution.py:290
  91.1 5.6 %collective-permute-start.16 = (bf16[128,128]{1,0:T(8,128)(2,1)S(1)}, bf16[128,128]{1,0:T(8,128)(2,1)S(1)}, u32[]{:S(2)}, u32[]{:S(2)}) collective-permute-start(bf16[128,128]{1,0:T(8,128)(2,1)S(1)} %add.34.refs_0_), channel_id=1, source_target_pairs={{0,16},{8,24},{16,0},{24,8},{1,17},{9,25},{17,1},{25,9},{2,18},{10... | collective-permute-start | bytes 98312 | tf_op jit(solution)/shard_map/ppermute | solution.py:295
  96.7 2.7 %collective-permute-start.18 = (bf16[128,128]{1,0:T(8,128)(2,1)S(1)}, bf16[128,128]{1,0:T(8,128)(2,1)S(1)}, u32[]{:S(2)}, u32[]{:S(2)}) collective-permute-start(bf16[128,128]{1,0:T(8,128)(2,1)S(1)} %add.34.refs_0_), channel_id=1, source_target_pairs={{0,24},{8,0},{16,8},{24,16},{1,25},{9,1},{17,9},{25,17},{2,26},{10... | collective-permute-start | bytes 98312 | tf_op jit(solution)/shard_map/ppermute | solution.py:295
  99.4 1.3 %collective-permute-done.17.refs_2_ = bf16[128,128]{1,0:T(8,128)(2,1)S(1)} collective-permute-done((bf16[128,128]{1,0:T(8,128)(2,1)S(1)}, bf16[128,128]{1,0:T(8,128)(2,1)S(1)}, u32[]{:S(2)}, u32[]{:S(2)}) %collective-permute-start.17) | collective-permute-done | bytes 32800 | tf_op jit(solution)/shard_map/ppermute | solution.py:295
  100.7 2.1 %collective-permute-start.19 = (bf16[128,128]{1,0:T(8,128)(2,1)S(1)}, bf16[128,128]{1,0:T(8,128)(2,1)S(1)}, u32[]{:S(2)}, u32[]{:S(2)}) collective-permute-start(bf16[128,128]{1,0:T(8,128)(2,1)S(1)} %add.35.refs_1_), channel_id=1, source_target_pairs={{0,1},{1,0},{2,3},{3,2},{4,5},{5,4},{6,7},{7,6},{8,9},{9,8},{10,11... | collective-permute-start | bytes 98312 | tf_op jit(solution)/shard_map/ppermute | solution.py:290
  102.9 0.9 collective-permute-done.19.refs_2_
  103.7 1.0 all-to-all-done.2.refs_0_
  104.7 0.7 finish.1
  (24 shorter events, 0.1 us)
Async XLA Ops:
  0.6 10.5 %collective-permute-start.2 = (bf16[256,128]{1,0:T(8,128)(2,1)}, bf16[256,128]{1,0:T(8,128)(2,1)S(1)}, u32[]{:S(2)}, u32[]{:S(2)}) collective-permute-start(bf16[256,128]{1,0:T(8,128)(2,1)} %refs_0_.1), channel_id=1, source_target_pairs={{0,64},{32,96},{64,128},{96,160},{128,192},{160,224},{192,0},{224,... | collective-permute-start | bytes 196616 | tf_op jit(solution)/shard_map/ppermute | solution.py:295
  4.5 9.0 %collective-permute-start.3 = (bf16[256,128]{1,0:T(8,128)(2,1)}, bf16[256,128]{1,0:T(8,128)(2,1)S(1)}, u32[]{:S(2)}, u32[]{:S(2)}) collective-permute-start(bf16[256,128]{1,0:T(8,128)(2,1)} %refs_0_.1), channel_id=1, source_target_pairs={{0,192},{32,224},{64,0},{96,32},{128,64},{160,96},{192,128},{224,1... | collective-permute-start | bytes 196616 | tf_op jit(solution)/shard_map/ppermute | solution.py:295
  7.6 9.4 %collective-permute-start = (bf16[256,128]{1,0:T(8,128)(2,1)}, bf16[256,128]{1,0:T(8,128)(2,1)S(1)}, u32[]{:S(2)}, u32[]{:S(2)}) collective-permute-start(bf16[256,128]{1,0:T(8,128)(2,1)} %refs_0_.1), channel_id=1, source_target_pairs={{0,32},{32,64},{64,96},{96,128},{128,160},{160,192},{192,224},{224... | collective-permute-start | bytes 196616 | tf_op jit(solution)/shard_map/ppermute | solution.py:295
  8.4 8.6 %collective-permute-start.1 = (bf16[256,128]{1,0:T(8,128)(2,1)}, bf16[256,128]{1,0:T(8,128)(2,1)S(1)}, u32[]{:S(2)}, u32[]{:S(2)}) collective-permute-start(bf16[256,128]{1,0:T(8,128)(2,1)} %refs_0_.1), channel_id=1, source_target_pairs={{0,224},{32,0},{64,32},{96,64},{128,96},{160,128},{192,160},{224,1... | collective-permute-start | bytes 196616 | tf_op jit(solution)/shard_map/ppermute | solution.py:295
  10.3 7.8 %slice-start = ((s8[10485760]{0:T(1024)(128)(4,1)}), s8[4194304]{0:T(1024)(128)(4,1)S(1)}, s32[]{:S(2)}) async-start(s8[10485760]{0:T(1024)(128)(4,1)} %bitcast.3), calls=%async_computation.3 | async-start | bytes 8388608
  11.1 7.0 %slice-start.1 = ((s8[10485760]{0:T(1024)(128)(4,1)}), s8[4194304]{0:T(1024)(128)(4,1)S(1)}, s32[]{:S(2)}) async-start(s8[10485760]{0:T(1024)(128)(4,1)} %bitcast.3), calls=%async_computation.4 | async-start | bytes 8388608
  11.1 7.0 %slice-start.2 = ((s8[10485760]{0:T(1024)(128)(4,1)}), s8[2097152]{0:T(1024)(128)(4,1)S(1)}, s32[]{:S(2)}) async-start(s8[10485760]{0:T(1024)(128)(4,1)} %bitcast.3), calls=%async_computation.5 | async-start | bytes 4194304
  11.2 7.0 %copy-start.1 = (bf16[256,128]{1,0:T(8,128)(2,1)S(1)}, bf16[256,128]{1,0:T(8,128)(2,1)}, u32[]{:S(2)}) copy-start(bf16[256,128]{1,0:T(8,128)(2,1)} %refs_0_.1) | copy-start | bytes 196612
  11.2 5.9 %collective-permute-start.4 = (bf16[256,128]{1,0:T(8,128)(2,1)S(1)}, bf16[256,128]{1,0:T(8,128)(2,1)S(1)}, u32[]{:S(2)}, u32[]{:S(2)}) collective-permute-start(bf16[256,128]{1,0:T(8,128)(2,1)S(1)} %collective-permute-done.2.refs_3_), channel_id=1, source_target_pairs={{0,32},{32,64},{64,96},{96,128},{128,160},{160,192},{192,224},{224... | collective-permute-start | bytes 196616 | tf_op jit(solution)/shard_map/ppermute | solution.py:295
  12.0 6.1 %collective-permute-start.6 = (bf16[256,128]{1,0:T(8,128)(2,1)S(1)}, bf16[256,128]{1,0:T(8,128)(2,1)S(1)}, u32[]{:S(2)}, u32[]{:S(2)}) collective-permute-start(bf16[256,128]{1,0:T(8,128)(2,1)S(1)} %collective-permute-done.2.refs_3_), channel_id=1, source_target_pairs={{0,64},{32,96},{64,128},{96,160},{128,192},{160,224},{192,0},{224,... | collective-permute-start | bytes 196616 | tf_op jit(solution)/shard_map/ppermute | solution.py:295
  13.5 4.6 %collective-permute-start.5 = (bf16[256,128]{1,0:T(8,128)(2,1)S(1)}, bf16[256,128]{1,0:T(8,128)(2,1)S(1)}, u32[]{:S(2)}, u32[]{:S(2)}) collective-permute-start(bf16[256,128]{1,0:T(8,128)(2,1)S(1)} %collective-permute-done.3.refs_4_), channel_id=1, source_target_pairs={{0,224},{32,0},{64,32},{96,64},{128,96},{160,128},{192,160},{224,1... | collective-permute-start | bytes 196616 | tf_op jit(solution)/shard_map/ppermute | solution.py:295
  20.8 4.2 %collective-permute-start.7 = (bf16[32,128,128]{2,1,0:T(8,128)(2,1)S(1)}, bf16[32,128,128]{2,1,0:T(8,128)(2,1)S(1)}, u32[]{:S(2)}, u32[]{:S(2)}) collective-permute-start(bf16[32,128,128]{2,1,0:T(8,128)(2,1)S(1)} %get-tuple-element.22), channel_id=1, source_target_pairs={{0,1},{1,0},{2,3},{3,2},{4,5},{5,4},{6,7},{7,6},{8,9},{9,8},{10,11... | collective-permute-start | bytes 3145736 | tf_op jit(solution)/shard_map/ppermute | solution.py:290
  25.4 24.3 %copy-start = (bf16[256,256]{1,0:T(8,128)(2,1)S(1)}, bf16[256,256]{1,0:T(8,128)(2,1)}, u32[]{:S(2)}) copy-start(bf16[256,256]{1,0:T(8,128)(2,1)} %cotangent.1) | copy-start | bytes 393220
  25.4 24.3 %copy-start.2 = (bf16[128,256]{1,0:T(8,128)(2,1)S(1)}, bf16[128,256]{1,0:T(8,128)(2,1)}, u32[]{:S(2)}) copy-start(bf16[128,256]{1,0:T(8,128)(2,1)} %weight.1) | copy-start | bytes 196612
  51.3 19.3 %all-to-all-start.1 = ((bf16[16,256,128]{2,1,0:T(8,128)(2,1)}), bf16[16,256,128]{2,1,0:T(8,128)(2,1)S(1)}, u32[]{:S(2)}, u32[]{:S(2)}) async-start(bf16[16,256,128]{2,1,0:T(8,128)(2,1)} %get-tuple-element.25), calls=%async_computation.1 | async-start | bytes 2097152 | tf_op jit(solution)/shard_map/all_to_all | solution.py:375
  54.9 3.2 %collective-permute-start.8 = (bf16[128,128]{1,0:T(8,128)(2,1)S(1)}, bf16[128,128]{1,0:T(8,128)(2,1)S(1)}, u32[]{:S(2)}, u32[]{:S(2)}) collective-permute-start(bf16[128,128]{1,0:T(8,128)(2,1)S(1)} %get-tuple-element.27), channel_id=1, source_target_pairs={{0,1},{1,0},{2,3},{3,2},{4,5},{5,4},{6,7},{7,6},{8,9},{9,8},{10,11... | collective-permute-start | bytes 98312 | tf_op jit(solution)/shard_map/ppermute | solution.py:290
  58.2 3.9 %collective-permute-start.9 = (bf16[128,128]{1,0:T(8,128)(2,1)S(1)}, bf16[128,128]{1,0:T(8,128)(2,1)S(1)}, u32[]{:S(2)}, u32[]{:S(2)}) collective-permute-start(bf16[128,128]{1,0:T(8,128)(2,1)S(1)} %add_convert_fusion.3), channel_id=1, source_target_pairs={{0,32},{32,0},{64,96},{96,64},{128,160},{160,128},{192,224},{224,1... | collective-permute-start | bytes 98312 | tf_op jit(solution)/shard_map/ppermute | solution.py:290
  62.1 7.2 %collective-permute-start.10 = (bf16[128,128]{1,0:T(8,128)(2,1)S(1)}, bf16[128,128]{1,0:T(8,128)(2,1)S(1)}, u32[]{:S(2)}, u32[]{:S(2)}) collective-permute-start(bf16[128,128]{1,0:T(8,128)(2,1)S(1)} %add_convert_fusion.2), channel_id=1, source_target_pairs={{0,128},{32,160},{64,192},{96,224},{128,0},{160,32},{192,64},{224,... | collective-permute-start | bytes 98312 | tf_op jit(solution)/shard_map/ppermute | solution.py:295
  64.8 5.8 %collective-permute-start.11 = (bf16[128,128]{1,0:T(8,128)(2,1)S(1)}, bf16[128,128]{1,0:T(8,128)(2,1)S(1)}, u32[]{:S(2)}, u32[]{:S(2)}) collective-permute-start(bf16[128,128]{1,0:T(8,128)(2,1)S(1)} %add_convert_fusion.2), channel_id=1, source_target_pairs={{0,64},{32,96},{64,128},{96,160},{128,192},{160,224},{192,0},{224,... | collective-permute-start | bytes 98312 | tf_op jit(solution)/shard_map/ppermute | solution.py:295
  64.8 5.8 %collective-permute-start.12 = (bf16[128,128]{1,0:T(8,128)(2,1)S(1)}, bf16[128,128]{1,0:T(8,128)(2,1)S(1)}, u32[]{:S(2)}, u32[]{:S(2)}) collective-permute-start(bf16[128,128]{1,0:T(8,128)(2,1)S(1)} %add_convert_fusion.2), channel_id=1, source_target_pairs={{0,192},{32,224},{64,0},{96,32},{128,64},{160,96},{192,128},{224,1... | collective-permute-start | bytes 98312 | tf_op jit(solution)/shard_map/ppermute | solution.py:295
  70.6 8.4 %collective-permute-start.13 = (bf16[32,128,128]{2,1,0:T(8,128)(2,1)S(1)}, bf16[32,128,128]{2,1,0:T(8,128)(2,1)S(1)}, u32[]{:S(2)}, u32[]{:S(2)}) collective-permute-start(bf16[32,128,128]{2,1,0:T(8,128)(2,1)S(1)} %bitcast.7), channel_id=1, source_target_pairs={{0,1},{1,0},{2,3},{3,2},{4,5},{5,4},{6,7},{7,6},{8,9},{9,8},{10,11... | collective-permute-start | bytes 3145736 | tf_op jit(solution)/shard_map/ppermute | solution.py:290
  73.4 8.6 %collective-permute-start.14 = (bf16[128,128]{1,0:T(8,128)(2,1)S(1)}, bf16[128,128]{1,0:T(8,128)(2,1)S(1)}, u32[]{:S(2)}, u32[]{:S(2)}) collective-permute-start(bf16[128,128]{1,0:T(8,128)(2,1)S(1)} %add_convert_fusion.1.refs_0_), channel_id=1, source_target_pairs={{0,2},{2,0},{4,6},{6,4},{1,3},{3,1},{5,7},{7,5},{8,10},{10,8},{12,... | collective-permute-start | bytes 98312 | tf_op jit(solution)/shard_map/ppermute | solution.py:290
  82.0 22.8 %all-to-all-start.2 = ((bf16[8,256,128]{2,1,0:T(8,128)(2,1)}), bf16[8,256,128]{2,1,0:T(8,128)(2,1)S(1)}, u32[]{:S(2)}, u32[]{:S(2)}) async-start(bf16[8,256,128]{2,1,0:T(8,128)(2,1)} %backward_second.1), calls=%async_computation.2 | async-start | bytes 1048576 | tf_op jit(solution)/shard_map/all_to_all | solution.py:400
  86.8 4.4 %collective-permute-start.15 = (bf16[128,128]{1,0:T(8,128)(2,1)S(1)}, bf16[128,128]{1,0:T(8,128)(2,1)S(1)}, u32[]{:S(2)}, u32[]{:S(2)}) collective-permute-start(bf16[128,128]{1,0:T(8,128)(2,1)S(1)} %add.33.refs_0_), channel_id=1, source_target_pairs={{0,4},{2,6},{4,0},{6,2},{1,5},{3,7},{5,1},{7,3},{8,12},{10,14},{12... | collective-permute-start | bytes 98312 | tf_op jit(solution)/shard_map/ppermute | solution.py:290
  91.1 8.3 %collective-permute-start.16 = (bf16[128,128]{1,0:T(8,128)(2,1)S(1)}, bf16[128,128]{1,0:T(8,128)(2,1)S(1)}, u32[]{:S(2)}, u32[]{:S(2)}) collective-permute-start(bf16[128,128]{1,0:T(8,128)(2,1)S(1)} %add.34.refs_0_), channel_id=1, source_target_pairs={{0,16},{8,24},{16,0},{24,8},{1,17},{9,25},{17,1},{25,9},{2,18},{10... | collective-permute-start | bytes 98312 | tf_op jit(solution)/shard_map/ppermute | solution.py:295
  96.7 4.0 %collective-permute-start.17 = (bf16[128,128]{1,0:T(8,128)(2,1)S(1)}, bf16[128,128]{1,0:T(8,128)(2,1)S(1)}, u32[]{:S(2)}, u32[]{:S(2)}) collective-permute-start(bf16[128,128]{1,0:T(8,128)(2,1)S(1)} %add.34.refs_0_), channel_id=1, source_target_pairs={{0,8},{8,16},{16,24},{24,0},{1,9},{9,17},{17,25},{25,1},{2,10},{10... | collective-permute-start | bytes 98312 | tf_op jit(solution)/shard_map/ppermute | solution.py:295
  96.7 4.0 %collective-permute-start.18 = (bf16[128,128]{1,0:T(8,128)(2,1)S(1)}, bf16[128,128]{1,0:T(8,128)(2,1)S(1)}, u32[]{:S(2)}, u32[]{:S(2)}) collective-permute-start(bf16[128,128]{1,0:T(8,128)(2,1)S(1)} %add.34.refs_0_), channel_id=1, source_target_pairs={{0,24},{8,0},{16,8},{24,16},{1,25},{9,1},{17,9},{25,17},{2,26},{10... | collective-permute-start | bytes 98312 | tf_op jit(solution)/shard_map/ppermute | solution.py:295
  100.7 3.0 %collective-permute-start.19 = (bf16[128,128]{1,0:T(8,128)(2,1)S(1)}, bf16[128,128]{1,0:T(8,128)(2,1)S(1)}, u32[]{:S(2)}, u32[]{:S(2)}) collective-permute-start(bf16[128,128]{1,0:T(8,128)(2,1)S(1)} %add.35.refs_1_), channel_id=1, source_target_pairs={{0,1},{1,0},{2,3},{3,2},{4,5},{5,4},{6,7},{7,6},{8,9},{9,8},{10,11... | collective-permute-start | bytes 98312 | tf_op jit(solution)/shard_map/ppermute | solution.py:290

commit v6 on v5

--- a/solution.py
+++ b/solution.py
@@ -9,8 +9,8 @@
 UNROLL = 16
 LIST = 240
 WORDS = 512
-CHUNKS = 8
-AHEAD = 8
+CHUNKS = 16
+AHEAD = 16
 NEAR = (1, 7, 2, 6, 3, 5, 4)
 SMEM = pl.BlockSpec(memory_space=pltpu.SMEM)
 VMEM = pl.BlockSpec(memory_space=pltpu.VMEM)
@@ -83,18 +83,27 @@
     words[...] = word
 
 
-def prepare_kernel(rows, cols, count, forward_words, backward_words, padded):
+def prepare_kernel(rows, cols, count, forward_words, backward_words, padded, *scratch):
+    row_block, col_block, row_sem, col_sem = scratch
+    loads = [
+        pltpu.make_async_copy(rows, row_block, row_sem),
+        pltpu.make_async_copy(cols, col_block, col_sem),
+    ]
+    for load in loads:
+        load.start()
     core = lax.axis_index("core")
+    width = forward_words.shape[1]
+    earlier = ones_where(
+        lax.broadcasted_iota(I32, (width, width), 0) < lax.broadcasted_iota(I32, (width, width), 1)
+    )
     padded[...] = jnp.zeros_like(padded)
-    padded[0:1, : rows.shape[2]] = rows[0]
-    padded[1:2, : rows.shape[2]] = cols[0]
+    for load in loads:
+        load.wait()
+    padded[0:1, : rows.shape[2]] = row_block[0]
+    padded[1:2, : rows.shape[2]] = col_block[0]
     row, col = padded[0:1], padded[1:2]
     slot = lax.broadcasted_iota(I32, row.shape, 1)
     valid = slot < count[0, 0]
-    width = forward_words.shape[1]
-    earlier = ones_where(
-        lax.broadcasted_iota(I32, (width, width), 0) < lax.broadcasted_iota(I32, (width, width), 1)
-    )
     own = jnp.where(((row >> 1) & 1) == core, 1, 0)
     local = ((row >> 2) << 1) + (row & 1)
     shared = (slot, valid, earlier)
@@ -311,9 +320,15 @@
     forward_words, backward_words = pl.pallas_call(
         prepare_kernel,
         out_shape=[list_shape, list_shape],
-        in_specs=[VMEM, VMEM, SMEM],
+        in_specs=[HBM, HBM, SMEM],
         out_specs=[VMEM, VMEM],
-        scratch_shapes=[pltpu.VMEM((8, -(-slots // 128) * 128), I32)],
+        scratch_shapes=[
+            pltpu.VMEM((8, -(-slots // 128) * 128), I32),
+            pltpu.VMEM(tile_rows.shape, I32),
+            pltpu.VMEM(tile_cols.shape, I32),
+            pltpu.SemaphoreType.DMA(()),
+            pltpu.SemaphoreType.DMA(()),
+        ],
         compiler_params=params(16),
         cost_estimate=pl.CostEstimate(flops=10**10, bytes_accessed=0, transcendentals=0),
         name="prepare",

time: 107 us -> 106 us (level); the launches traced: 105 us -> 107 us
  waiting for transfers between devices: 10.3 us -> 14.1 us
  Pallas kernels: 17.9 us -> 14.4 us
    all_to_all x1, starting transfers between devices: 4.78 us -> 7.82 us  [per_device(): shares = lax.all_to_all(col_partial, 'row', 0, 0, tiled=True)]
    ppermute x13, starting transfers between devices: 27.4 us -> 24.9 us  [shifted(): lax.ppermute(value, axis, [(i, (i + step) % size) for i in range(size)])]
    all_to_all x1, waiting for transfers between devices: 0.96 us -> 2.97 us  [per_device(): shares = lax.all_to_all(col_partial, 'row', 0, 0, tiled=True)]
    pallas_call x1, Pallas kernels: 4.85 us -> 3.62 us  [per_device(): pl.pallas_call(backward_first_kernel, out_shape=[jax.ShapeDtypeStruct((co...]
  transfers between devices with their start and end apart: 22 -> 22, of which waited for: 9 -> 11; matrix products, arithmetic and copies ran while one was open for 0% -> 0% of each run, Pallas kernels for 12% -> 10%
where the time goes in v6:
time: 106 us; the launch traced here: 107 us
  starting transfers between devices  51.3 us (48%)
  blocking collectives  24.7 us (23%)
  Pallas kernels  14.4 us (14%)
  waiting for transfers between devices  14.1 us (13%)
  between operations  1.63 us (2%)
    ppermute x13, starting transfers between devices, shifted(): lax.ppermute(value, axis, [(i, (i + step) % size) for i in range(size)])  24.9 us
    all_to_all x1, blocking collectives, per_device(): parts = lax.all_to_all(paired, yx, 0, 0, tiled=True)  24.7 us
    ppermute x7, starting transfers between devices, swapped(): lax.ppermute(value, axis, [(i, i ^ step) for i in range(lax.axis_size(axi...  14.9 us
    all_to_all x1, starting transfers between devices, per_device(): shares = lax.all_to_all(col_partial, 'row', 0, 0, tiled=True)  7.82 us
    ppermute x13, waiting for transfers between devices, shifted(): lax.ppermute(value, axis, [(i, (i + step) % size) for i in range(size)])  5.29 us
    ppermute x7, waiting for transfers between devices, swapped(): lax.ppermute(value, axis, [(i, i ^ step) for i in range(lax.axis_size(axi...  5.11 us
    all_to_all x1, starting transfers between devices, per_device(): lax.all_to_all(payload, yx, 0, 0, tiled=True).reshape(half_rows, size, feat)  3.65 us
    pallas_call x1, Pallas kernels, per_device(): pl.pallas_call(backward_first_kernel, out_shape=[jax.ShapeDtypeStruct((co...  3.62 us
  transfers between devices with their start and end apart: 22, of which 11 were waited for; matrix products, arithmetic and copies ran while one was open for 0% of the time, Pallas kernels for 10%

profile of v6, /device:TPU:1, one launch (start us, length us, event | category | flops | bytes accessed | tf_op | source)
XLA Modules:
  0.0 106.5 jit_solution(284319798424201116)
XLA Ops:
  0.6 3.9 %collective-permute-start.2 = (bf16[256,128]{1,0:T(8,128)(2,1)}, bf16[256,128]{1,0:T(8,128)(2,1)S(1)}, u32[]{:S(2)}, u32[]{:S(2)}) collective-permute-start(bf16[256,128]{1,0:T(8,128)(2,1)} %refs_0_.1), channel_id=1, source_target_pairs={{0,64},{32,96},{64,128},{96,160},{128,192},{160,224},{192,0},{224,... | collective-permute-start | bytes 196616 | tf_op jit(solution)/shard_map/ppermute | solution.py:304
  4.5 3.1 %collective-permute-start.3 = (bf16[256,128]{1,0:T(8,128)(2,1)}, bf16[256,128]{1,0:T(8,128)(2,1)S(1)}, u32[]{:S(2)}, u32[]{:S(2)}) collective-permute-start(bf16[256,128]{1,0:T(8,128)(2,1)} %refs_0_.1), channel_id=1, source_target_pairs={{0,192},{32,224},{64,0},{96,32},{128,64},{160,96},{192,128},{224,1... | collective-permute-start | bytes 196616 | tf_op jit(solution)/shard_map/ppermute | solution.py:304
  7.6 0.7 collective-permute-start
  8.4 1.9 %collective-permute-start.1 = (bf16[256,128]{1,0:T(8,128)(2,1)}, bf16[256,128]{1,0:T(8,128)(2,1)S(1)}, u32[]{:S(2)}, u32[]{:S(2)}) collective-permute-start(bf16[256,128]{1,0:T(8,128)(2,1)} %refs_0_.1), channel_id=1, source_target_pairs={{0,224},{32,0},{64,32},{96,64},{128,96},{160,128},{192,160},{224,1... | collective-permute-start | bytes 196616 | tf_op jit(solution)/shard_map/ppermute | solution.py:304
  11.1 0.0 slice-start.1
  11.1 0.0 slice-start.2
  11.2 0.9 collective-permute-start.4
  12.0 1.5 %collective-permute-start.6 = (bf16[256,128]{1,0:T(8,128)(2,1)S(1)}, bf16[256,128]{1,0:T(8,128)(2,1)S(1)}, u32[]{:S(2)}, u32[]{:S(2)}) collective-permute-start(bf16[256,128]{1,0:T(8,128)(2,1)S(1)} %collective-permute-done.2.refs_3_), channel_id=1, source_target_pairs={{0,64},{32,96},{64,128},{96,160},{128,192},{160,224},{192,0},{224,... | collective-permute-start | bytes 196616 | tf_op jit(solution)/shard_map/ppermute | solution.py:304
  13.5 0.0 collective-permute-done.3.refs_4_
  13.5 0.9 collective-permute-start.5
  14.4 2.6 %prepare.1 = (s32[1,512]{1,0:T(1,128)S(1)}, s32[1,512]{1,0:T(1,128)S(1)}) custom-call(s32[1,1,320]{2,1,0:T(1,128)} %rows.1, s32[1,1,320]{2,1,0:T(1,128)} %cols.1, s32[1,1]{1,0:T(1,128)S(6)} %copy.10.count), custom_call_target="tpu_custom_call" | custom-call | flops 10000000000 | tf_op jit(solution)/shard_map/prepare/pallas_call | solution.py:320
  17.0 0.0 collective-permute-done.refs_1_
  17.0 0.0 collective-permute-done.4.refs_5_
  17.1 1.1 %collective-permute-done.6.refs_7_ = bf16[256,128]{1,0:T(8,128)(2,1)S(1)} collective-permute-done((bf16[256,128]{1,0:T(8,128)(2,1)S(1)}, bf16[256,128]{1,0:T(8,128)(2,1)S(1)}, u32[]{:S(2)}, u32[]{:S(2)}) %collective-permute-start.6) | collective-permute-done | bytes 65568 | tf_op jit(solution)/shard_map/ppermute | solution.py:304
  18.1 0.0 collective-permute-done.5.refs_6_
  18.2 1.8 %forward_send.1 = (bf16[32,128,128]{2,1,0:T(8,128)(2,1)S(1)}, bf16[16,128,128]{2,1,0:T(8,128)(2,1)S(1)}) custom-call(s32[1,512]{1,0:T(1,128)S(1)} %get-tuple-element.20.words, bf16[320,128,128]{2,1,0:T(8,128)(2,1)S(1)} %bitcast.5, bf16[256,128]{1,0:T(8,128)(2,1)S(1)} %copy-done.1, bf16[256,128]{1,0:T(8,128)(2,1)S(1)} %collective-permute-done.refs_1_, ...), custom_call_target="tpu_custom_call" | custom-call | flops 671088640 | bytes 5242880 | tf_op jit(solution)/shard_map/forward_send/pallas_call | solution.py:348
  19.9 3.0 %collective-permute-start.7 = (bf16[32,128,128]{2,1,0:T(8,128)(2,1)S(1)}, bf16[32,128,128]{2,1,0:T(8,128)(2,1)S(1)}, u32[]{:S(2)}, u32[]{:S(2)}) collective-permute-start(bf16[32,128,128]{2,1,0:T(8,128)(2,1)S(1)} %get-tuple-element.22), channel_id=1, source_target_pairs={{0,1},{1,0},{2,3},{3,2},{4,5},{5,4},{6,7},{7,6},{8,9},{9,8},{10,11... | collective-permute-start | bytes 3145736 | tf_op jit(solution)/shard_map/ppermute | solution.py:299
  23.0 1.6 %forward_keep.1 = f32[32,128,128]{2,1,0:T(8,128)S(1)} custom-call(s32[1,512]{1,0:T(1,128)S(1)} %get-tuple-element.20.words, bf16[320,128,128]{2,1,0:T(8,128)(2,1)S(1)} %bitcast.6, bf16[16,128,128]{2,1,0:T(8,128)(2,1)S(1)} %get-tuple-element.21.panel), custom_call_target="tpu_custom_call" | custom-call | flops 671088640 | bytes 5242880 | tf_op jit(solution)/shard_map/forward_keep/pallas_call | solution.py:362
  24.6 0.7 collective-permute-done.7
  25.2 0.3 add_convert_fusion
  25.6 0.0 copy-start
  25.6 0.0 copy-start.2
  25.6 24.7 %all_to_all.15.parts = bf16[16,256,128]{2,1,0:T(8,128)(2,1)S(1)} all-to-all(bf16[16,256,128]{2,1,0:T(8,128)(2,1)S(1)} %bitcast.9), channel_id=1, replica_groups=mesh['row'=8,'y'=4,'x'=4,'core'=2] {'y','x'}, dimensions={0} | all-to-all | bytes 2097152 | tf_op jit(solution)/shard_map/all_to_all | solution.py:372
  50.3 1.6 %middle.1 = (bf16[256,256]{1,0:T(8,128)(2,1)}, bf16[16,256,128]{2,1,0:T(8,128)(2,1)}, bf16[128,128]{1,0:T(8,128)(2,1)S(1)}, bf16[128,128]{1,0:T(8,128)(2,1)S(1)}) custom-call(bf16[16,256,128]{2,1,0:T(8,128)(2,1)S(1)} %all_to_all.15.parts, bf16[128,256]{1,0:T(8,128)(2,1)S(1)} %copy-done.2, bf16[256,256]{1,0:T(8,128)(2,1)S(1)} %copy-done), custom_call_target="tpu_custom_call" | custom-call | tf_op jit(solution)/shard_map/middle/pallas_call | solution.py:373
  51.9 3.7 %all-to-all-start.1 = ((bf16[16,256,128]{2,1,0:T(8,128)(2,1)}), bf16[16,256,128]{2,1,0:T(8,128)(2,1)S(1)}, u32[]{:S(2)}, u32[]{:S(2)}) async-start(bf16[16,256,128]{2,1,0:T(8,128)(2,1)} %get-tuple-element.25), calls=%async_computation.1 | async-start | bytes 2097152 | tf_op jit(solution)/shard_map/all_to_all | solution.py:390
  55.5 1.7 %collective-permute-start.8 = (bf16[128,128]{1,0:T(8,128)(2,1)S(1)}, bf16[128,128]{1,0:T(8,128)(2,1)S(1)}, u32[]{:S(2)}, u32[]{:S(2)}) collective-permute-start(bf16[128,128]{1,0:T(8,128)(2,1)S(1)} %get-tuple-element.27), channel_id=1, source_target_pairs={{0,1},{1,0},{2,3},{3,2},{4,5},{5,4},{6,7},{7,6},{8,9},{9,8},{10,11... | collective-permute-start | bytes 98312 | tf_op jit(solution)/shard_map/ppermute | solution.py:299
  57.2 0.9 collective-permute-done.8
  58.1 1.8 %collective-permute-start.9 = (bf16[128,128]{1,0:T(8,128)(2,1)S(1)}, bf16[128,128]{1,0:T(8,128)(2,1)S(1)}, u32[]{:S(2)}, u32[]{:S(2)}) collective-permute-start(bf16[128,128]{1,0:T(8,128)(2,1)S(1)} %add_convert_fusion.3), channel_id=1, source_target_pairs={{0,32},{32,0},{64,96},{96,64},{128,160},{160,128},{192,224},{224,1... | collective-permute-start | bytes 98312 | tf_op jit(solution)/shard_map/ppermute | solution.py:299
  59.8 1.3 %collective-permute-done.9 = bf16[128,128]{1,0:T(8,128)(2,1)S(1)} collective-permute-done((bf16[128,128]{1,0:T(8,128)(2,1)S(1)}, bf16[128,128]{1,0:T(8,128)(2,1)S(1)}, u32[]{:S(2)}, u32[]{:S(2)}) %collective-permute-start.9) | collective-permute-done | bytes 32800 | tf_op jit(solution)/shard_map/ppermute | solution.py:299
  61.1 3.1 %collective-permute-start.10 = (bf16[128,128]{1,0:T(8,128)(2,1)S(1)}, bf16[128,128]{1,0:T(8,128)(2,1)S(1)}, u32[]{:S(2)}, u32[]{:S(2)}) collective-permute-start(bf16[128,128]{1,0:T(8,128)(2,1)S(1)} %add_convert_fusion.2), channel_id=1, source_target_pairs={{0,128},{32,160},{64,192},{96,224},{128,0},{160,32},{192,64},{224,... | collective-permute-start | bytes 98312 | tf_op jit(solution)/shard_map/ppermute | solution.py:304
  64.3 0.2 collective-permute-start.11
  64.4 3.4 %collective-permute-start.12 = (bf16[128,128]{1,0:T(8,128)(2,1)S(1)}, bf16[128,128]{1,0:T(8,128)(2,1)S(1)}, u32[]{:S(2)}, u32[]{:S(2)}) collective-permute-start(bf16[128,128]{1,0:T(8,128)(2,1)S(1)} %add_convert_fusion.2), channel_id=1, source_target_pairs={{0,192},{32,224},{64,0},{96,32},{128,64},{160,96},{192,128},{224,1... | collective-permute-start | bytes 98312 | tf_op jit(solution)/shard_map/ppermute | solution.py:304
  67.8 0.3 collective-permute-done.10
  68.2 1.9 %collective-permute-done.11 = bf16[128,128]{1,0:T(8,128)(2,1)S(1)} collective-permute-done((bf16[128,128]{1,0:T(8,128)(2,1)S(1)}, bf16[128,128]{1,0:T(8,128)(2,1)S(1)}, u32[]{:S(2)}, u32[]{:S(2)}) %collective-permute-start.11) | collective-permute-done | bytes 32800 | tf_op jit(solution)/shard_map/ppermute | solution.py:304
  70.1 0.7 all-to-all-done.1
  70.9 3.0 %collective-permute-start.13 = (bf16[32,128,128]{2,1,0:T(8,128)(2,1)S(1)}, bf16[32,128,128]{2,1,0:T(8,128)(2,1)S(1)}, u32[]{:S(2)}, u32[]{:S(2)}) collective-permute-start(bf16[32,128,128]{2,1,0:T(8,128)(2,1)S(1)} %bitcast.7), channel_id=1, source_target_pairs={{0,1},{1,0},{2,3},{3,2},{4,5},{5,4},{6,7},{7,6},{8,9},{9,8},{10,11... | collective-permute-start | bytes 3145736 | tf_op jit(solution)/shard_map/ppermute | solution.py:299
  73.9 3.6 %backward_first.1 = (f32[16,128,128]{2,1,0:T(8,128)S(1)}, bf16[320,128,128]{2,1,0:T(8,128)(2,1)S(1)}) custom-call(s32[1,512]{1,0:T(1,128)S(1)} %get-tuple-element.24.words, s32[1,1]{1,0:T(1,128)S(6)} %copy.10.count, bf16[1,1,320,128,128]{4,3,2,1,0:T(8,128)(2,1)} %stored.1, bf16[32,128,128]{2,1,0:T(8,128)(2,1)S(1)} %bitcast.8), custom_call_target="tpu_custom_call" | custom-call | flops 671088640 | bytes 5242880 | tf_op jit(solution)/shard_map/backward_first/pallas_call | solution.py:394
  77.5 2.5 %backward_second.1 = bf16[8,256,128]{2,1,0:T(8,128)(2,1)} custom-call(s32[1,512]{1,0:T(1,128)S(1)} %get-tuple-element.24.words, bf16[320,128,128]{2,1,0:T(8,128)(2,1)S(1)} %get-tuple-element.29.tiles, bf16[32,128,128]{2,1,0:T(8,128)(2,1)S(1)} %collective-permute-done.13.grads, f32[16,128,128]{2,1,0:T(8,128)S(1)} %get-tuple-element.30.start), custom_call_target="tpu_custom_call" | custom-call | flops 671088640 | bytes 5242880 | tf_op jit(solution)/shard_map/backward_second/pallas_call | solution.py:404
  80.0 7.8 %all-to-all-start.2 = ((bf16[8,256,128]{2,1,0:T(8,128)(2,1)}), bf16[8,256,128]{2,1,0:T(8,128)(2,1)S(1)}, u32[]{:S(2)}, u32[]{:S(2)}) async-start(bf16[8,256,128]{2,1,0:T(8,128)(2,1)} %backward_second.1), calls=%async_computation.2 | async-start | bytes 1048576 | tf_op jit(solution)/shard_map/all_to_all | solution.py:415
  87.8 3.0 %collective-permute-start.15 = (bf16[128,128]{1,0:T(8,128)(2,1)S(1)}, bf16[128,128]{1,0:T(8,128)(2,1)S(1)}, u32[]{:S(2)}, u32[]{:S(2)}) collective-permute-start(bf16[128,128]{1,0:T(8,128)(2,1)S(1)} %add.33.refs_0_), channel_id=1, source_target_pairs={{0,4},{2,6},{4,0},{6,2},{1,5},{3,7},{5,1},{7,3},{8,12},{10,14},{12... | collective-permute-start | bytes 98312 | tf_op jit(solution)/shard_map/ppermute | solution.py:299
  90.8 1.4 %collective-permute-done.15.refs_1_ = bf16[128,128]{1,0:T(8,128)(2,1)S(1)} collective-permute-done((bf16[128,128]{1,0:T(8,128)(2,1)S(1)}, bf16[128,128]{1,0:T(8,128)(2,1)S(1)}, u32[]{:S(2)}, u32[]{:S(2)}) %collective-permute-start.15) | collective-permute-done | bytes 32800 | tf_op jit(solution)/shard_map/ppermute | solution.py:299
  92.2 2.6 %collective-permute-start.16 = (bf16[128,128]{1,0:T(8,128)(2,1)S(1)}, bf16[128,128]{1,0:T(8,128)(2,1)S(1)}, u32[]{:S(2)}, u32[]{:S(2)}) collective-permute-start(bf16[128,128]{1,0:T(8,128)(2,1)S(1)} %add.34.refs_0_), channel_id=1, source_target_pairs={{0,16},{8,24},{16,0},{24,8},{1,17},{9,25},{17,1},{25,9},{2,18},{10... | collective-permute-start | bytes 98312 | tf_op jit(solution)/shard_map/ppermute | solution.py:304
  94.8 2.7 %collective-permute-start.18 = (bf16[128,128]{1,0:T(8,128)(2,1)S(1)}, bf16[128,128]{1,0:T(8,128)(2,1)S(1)}, u32[]{:S(2)}, u32[]{:S(2)}) collective-permute-start(bf16[128,128]{1,0:T(8,128)(2,1)S(1)} %add.34.refs_0_), channel_id=1, source_target_pairs={{0,24},{8,0},{16,8},{24,16},{1,25},{9,1},{17,9},{25,17},{2,26},{10... | collective-permute-start | bytes 98312 | tf_op jit(solution)/shard_map/ppermute | solution.py:304
  97.5 1.9 %collective-permute-done.17.refs_2_ = bf16[128,128]{1,0:T(8,128)(2,1)S(1)} collective-permute-done((bf16[128,128]{1,0:T(8,128)(2,1)S(1)}, bf16[128,128]{1,0:T(8,128)(2,1)S(1)}, u32[]{:S(2)}, u32[]{:S(2)}) %collective-permute-start.17) | collective-permute-done | bytes 32800 | tf_op jit(solution)/shard_map/ppermute | solution.py:304
  99.4 2.5 %collective-permute-start.19 = (bf16[128,128]{1,0:T(8,128)(2,1)S(1)}, bf16[128,128]{1,0:T(8,128)(2,1)S(1)}, u32[]{:S(2)}, u32[]{:S(2)}) collective-permute-start(bf16[128,128]{1,0:T(8,128)(2,1)S(1)} %add.35.refs_1_), channel_id=1, source_target_pairs={{0,1},{1,0},{2,3},{3,2},{4,5},{5,4},{6,7},{7,6},{8,9},{9,8},{10,11... | collective-permute-start | bytes 98312 | tf_op jit(solution)/shard_map/ppermute | solution.py:299
  101.9 0.9 collective-permute-done.19.refs_2_
  102.8 3.0 %all-to-all-done.2.refs_0_ = bf16[8,256,128]{2,1,0:T(8,128)(2,1)S(1)} async-done(((bf16[8,256,128]{2,1,0:T(8,128)(2,1)}), bf16[8,256,128]{2,1,0:T(8,128)(2,1)S(1)}, u32[]{:S(2)}, u32[]{:S(2)}) %all-to-all-start.2) | async-done | bytes 524320 | tf_op jit(solution)/shard_map/all_to_all | solution.py:415
  105.8 0.7 finish.1
  (24 shorter events, 0.1 us)
Async XLA Ops:
  0.6 10.5 %collective-permute-start.2 = (bf16[256,128]{1,0:T(8,128)(2,1)}, bf16[256,128]{1,0:T(8,128)(2,1)S(1)}, u32[]{:S(2)}, u32[]{:S(2)}) collective-permute-start(bf16[256,128]{1,0:T(8,128)(2,1)} %refs_0_.1), channel_id=1, source_target_pairs={{0,64},{32,96},{64,128},{96,160},{128,192},{160,224},{192,0},{224,... | collective-permute-start | bytes 196616 | tf_op jit(solution)/shard_map/ppermute | solution.py:304
  4.5 9.0 %collective-permute-start.3 = (bf16[256,128]{1,0:T(8,128)(2,1)}, bf16[256,128]{1,0:T(8,128)(2,1)S(1)}, u32[]{:S(2)}, u32[]{:S(2)}) collective-permute-start(bf16[256,128]{1,0:T(8,128)(2,1)} %refs_0_.1), channel_id=1, source_target_pairs={{0,192},{32,224},{64,0},{96,32},{128,64},{160,96},{192,128},{224,1... | collective-permute-start | bytes 196616 | tf_op jit(solution)/shard_map/ppermute | solution.py:304
  7.6 9.4 %collective-permute-start = (bf16[256,128]{1,0:T(8,128)(2,1)}, bf16[256,128]{1,0:T(8,128)(2,1)S(1)}, u32[]{:S(2)}, u32[]{:S(2)}) collective-permute-start(bf16[256,128]{1,0:T(8,128)(2,1)} %refs_0_.1), channel_id=1, source_target_pairs={{0,32},{32,64},{64,96},{96,128},{128,160},{160,192},{192,224},{224... | collective-permute-start | bytes 196616 | tf_op jit(solution)/shard_map/ppermute | solution.py:304
  8.4 8.6 %collective-permute-start.1 = (bf16[256,128]{1,0:T(8,128)(2,1)}, bf16[256,128]{1,0:T(8,128)(2,1)S(1)}, u32[]{:S(2)}, u32[]{:S(2)}) collective-permute-start(bf16[256,128]{1,0:T(8,128)(2,1)} %refs_0_.1), channel_id=1, source_target_pairs={{0,224},{32,0},{64,32},{96,64},{128,96},{160,128},{192,160},{224,1... | collective-permute-start | bytes 196616 | tf_op jit(solution)/shard_map/ppermute | solution.py:304
  10.3 7.8 %slice-start = ((s8[10485760]{0:T(1024)(128)(4,1)}), s8[4194304]{0:T(1024)(128)(4,1)S(1)}, s32[]{:S(2)}) async-start(s8[10485760]{0:T(1024)(128)(4,1)} %bitcast.3), calls=%async_computation.3 | async-start | bytes 8388608
  11.1 7.0 %slice-start.1 = ((s8[10485760]{0:T(1024)(128)(4,1)}), s8[4194304]{0:T(1024)(128)(4,1)S(1)}, s32[]{:S(2)}) async-start(s8[10485760]{0:T(1024)(128)(4,1)} %bitcast.3), calls=%async_computation.4 | async-start | bytes 8388608
  11.1 7.0 %slice-start.2 = ((s8[10485760]{0:T(1024)(128)(4,1)}), s8[2097152]{0:T(1024)(128)(4,1)S(1)}, s32[]{:S(2)}) async-start(s8[10485760]{0:T(1024)(128)(4,1)} %bitcast.3), calls=%async_computation.5 | async-start | bytes 4194304
  11.2 7.0 %copy-start.1 = (bf16[256,128]{1,0:T(8,128)(2,1)S(1)}, bf16[256,128]{1,0:T(8,128)(2,1)}, u32[]{:S(2)}) copy-start(bf16[256,128]{1,0:T(8,128)(2,1)} %refs_0_.1) | copy-start | bytes 196612
  11.2 5.9 %collective-permute-start.4 = (bf16[256,128]{1,0:T(8,128)(2,1)S(1)}, bf16[256,128]{1,0:T(8,128)(2,1)S(1)}, u32[]{:S(2)}, u32[]{:S(2)}) collective-permute-start(bf16[256,128]{1,0:T(8,128)(2,1)S(1)} %collective-permute-done.2.refs_3_), channel_id=1, source_target_pairs={{0,32},{32,64},{64,96},{96,128},{128,160},{160,192},{192,224},{224... | collective-permute-start | bytes 196616 | tf_op jit(solution)/shard_map/ppermute | solution.py:304
  12.0 6.1 %collective-permute-start.6 = (bf16[256,128]{1,0:T(8,128)(2,1)S(1)}, bf16[256,128]{1,0:T(8,128)(2,1)S(1)}, u32[]{:S(2)}, u32[]{:S(2)}) collective-permute-start(bf16[256,128]{1,0:T(8,128)(2,1)S(1)} %collective-permute-done.2.refs_3_), channel_id=1, source_target_pairs={{0,64},{32,96},{64,128},{96,160},{128,192},{160,224},{192,0},{224,... | collective-permute-start | bytes 196616 | tf_op jit(solution)/shard_map/ppermute | solution.py:304
  13.5 4.6 %collective-permute-start.5 = (bf16[256,128]{1,0:T(8,128)(2,1)S(1)}, bf16[256,128]{1,0:T(8,128)(2,1)S(1)}, u32[]{:S(2)}, u32[]{:S(2)}) collective-permute-start(bf16[256,128]{1,0:T(8,128)(2,1)S(1)} %collective-permute-done.3.refs_4_), channel_id=1, source_target_pairs={{0,224},{32,0},{64,32},{96,64},{128,96},{160,128},{192,160},{224,1... | collective-permute-start | bytes 196616 | tf_op jit(solution)/shard_map/ppermute | solution.py:304
  19.9 5.3 %collective-permute-start.7 = (bf16[32,128,128]{2,1,0:T(8,128)(2,1)S(1)}, bf16[32,128,128]{2,1,0:T(8,128)(2,1)S(1)}, u32[]{:S(2)}, u32[]{:S(2)}) collective-permute-start(bf16[32,128,128]{2,1,0:T(8,128)(2,1)S(1)} %get-tuple-element.22), channel_id=1, source_target_pairs={{0,1},{1,0},{2,3},{3,2},{4,5},{5,4},{6,7},{7,6},{8,9},{9,8},{10,11... | collective-permute-start | bytes 3145736 | tf_op jit(solution)/shard_map/ppermute | solution.py:299
  25.6 24.7 %copy-start = (bf16[256,256]{1,0:T(8,128)(2,1)S(1)}, bf16[256,256]{1,0:T(8,128)(2,1)}, u32[]{:S(2)}) copy-start(bf16[256,256]{1,0:T(8,128)(2,1)} %cotangent.1) | copy-start | bytes 393220
  25.6 24.7 %copy-start.2 = (bf16[128,256]{1,0:T(8,128)(2,1)S(1)}, bf16[128,256]{1,0:T(8,128)(2,1)}, u32[]{:S(2)}) copy-start(bf16[128,256]{1,0:T(8,128)(2,1)} %weight.1) | copy-start | bytes 196612
  51.9 19.0 %all-to-all-start.1 = ((bf16[16,256,128]{2,1,0:T(8,128)(2,1)}), bf16[16,256,128]{2,1,0:T(8,128)(2,1)S(1)}, u32[]{:S(2)}, u32[]{:S(2)}) async-start(bf16[16,256,128]{2,1,0:T(8,128)(2,1)} %get-tuple-element.25), calls=%async_computation.1 | async-start | bytes 2097152 | tf_op jit(solution)/shard_map/all_to_all | solution.py:390
  55.5 2.5 %collective-permute-start.8 = (bf16[128,128]{1,0:T(8,128)(2,1)S(1)}, bf16[128,128]{1,0:T(8,128)(2,1)S(1)}, u32[]{:S(2)}, u32[]{:S(2)}) collective-permute-start(bf16[128,128]{1,0:T(8,128)(2,1)S(1)} %get-tuple-element.27), channel_id=1, source_target_pairs={{0,1},{1,0},{2,3},{3,2},{4,5},{5,4},{6,7},{7,6},{8,9},{9,8},{10,11... | collective-permute-start | bytes 98312 | tf_op jit(solution)/shard_map/ppermute | solution.py:299
  58.1 3.1 %collective-permute-start.9 = (bf16[128,128]{1,0:T(8,128)(2,1)S(1)}, bf16[128,128]{1,0:T(8,128)(2,1)S(1)}, u32[]{:S(2)}, u32[]{:S(2)}) collective-permute-start(bf16[128,128]{1,0:T(8,128)(2,1)S(1)} %add_convert_fusion.3), channel_id=1, source_target_pairs={{0,32},{32,0},{64,96},{96,64},{128,160},{160,128},{192,224},{224,1... | collective-permute-start | bytes 98312 | tf_op jit(solution)/shard_map/ppermute | solution.py:299
  61.1 7.1 %collective-permute-start.10 = (bf16[128,128]{1,0:T(8,128)(2,1)S(1)}, bf16[128,128]{1,0:T(8,128)(2,1)S(1)}, u32[]{:S(2)}, u32[]{:S(2)}) collective-permute-start(bf16[128,128]{1,0:T(8,128)(2,1)S(1)} %add_convert_fusion.2), channel_id=1, source_target_pairs={{0,128},{32,160},{64,192},{96,224},{128,0},{160,32},{192,64},{224,... | collective-permute-start | bytes 98312 | tf_op jit(solution)/shard_map/ppermute | solution.py:304
  64.3 5.8 %collective-permute-start.11 = (bf16[128,128]{1,0:T(8,128)(2,1)S(1)}, bf16[128,128]{1,0:T(8,128)(2,1)S(1)}, u32[]{:S(2)}, u32[]{:S(2)}) collective-permute-start(bf16[128,128]{1,0:T(8,128)(2,1)S(1)} %add_convert_fusion.2), channel_id=1, source_target_pairs={{0,64},{32,96},{64,128},{96,160},{128,192},{160,224},{192,0},{224,... | collective-permute-start | bytes 98312 | tf_op jit(solution)/shard_map/ppermute | solution.py:304
  64.4 5.6 %collective-permute-start.12 = (bf16[128,128]{1,0:T(8,128)(2,1)S(1)}, bf16[128,128]{1,0:T(8,128)(2,1)S(1)}, u32[]{:S(2)}, u32[]{:S(2)}) collective-permute-start(bf16[128,128]{1,0:T(8,128)(2,1)S(1)} %add_convert_fusion.2), channel_id=1, source_target_pairs={{0,192},{32,224},{64,0},{96,32},{128,64},{160,96},{192,128},{224,1... | collective-permute-start | bytes 98312 | tf_op jit(solution)/shard_map/ppermute | solution.py:304
  70.9 6.7 %collective-permute-start.13 = (bf16[32,128,128]{2,1,0:T(8,128)(2,1)S(1)}, bf16[32,128,128]{2,1,0:T(8,128)(2,1)S(1)}, u32[]{:S(2)}, u32[]{:S(2)}) collective-permute-start(bf16[32,128,128]{2,1,0:T(8,128)(2,1)S(1)} %bitcast.7), channel_id=1, source_target_pairs={{0,1},{1,0},{2,3},{3,2},{4,5},{5,4},{6,7},{7,6},{8,9},{9,8},{10,11... | collective-permute-start | bytes 3145736 | tf_op jit(solution)/shard_map/ppermute | solution.py:299
  73.9 6.1 %collective-permute-start.14 = (bf16[128,128]{1,0:T(8,128)(2,1)S(1)}, bf16[128,128]{1,0:T(8,128)(2,1)S(1)}, u32[]{:S(2)}, u32[]{:S(2)}) collective-permute-start(bf16[128,128]{1,0:T(8,128)(2,1)S(1)} %add_convert_fusion.1.refs_0_), channel_id=1, source_target_pairs={{0,2},{2,0},{4,6},{6,4},{1,3},{3,1},{5,7},{7,5},{8,10},{10,8},{12,... | collective-permute-start | bytes 98312 | tf_op jit(solution)/shard_map/ppermute | solution.py:299
  80.0 25.8 %all-to-all-start.2 = ((bf16[8,256,128]{2,1,0:T(8,128)(2,1)}), bf16[8,256,128]{2,1,0:T(8,128)(2,1)S(1)}, u32[]{:S(2)}, u32[]{:S(2)}) async-start(bf16[8,256,128]{2,1,0:T(8,128)(2,1)} %backward_second.1), calls=%async_computation.2 | async-start | bytes 1048576 | tf_op jit(solution)/shard_map/all_to_all | solution.py:415
  87.8 4.4 %collective-permute-start.15 = (bf16[128,128]{1,0:T(8,128)(2,1)S(1)}, bf16[128,128]{1,0:T(8,128)(2,1)S(1)}, u32[]{:S(2)}, u32[]{:S(2)}) collective-permute-start(bf16[128,128]{1,0:T(8,128)(2,1)S(1)} %add.33.refs_0_), channel_id=1, source_target_pairs={{0,4},{2,6},{4,0},{6,2},{1,5},{3,7},{5,1},{7,3},{8,12},{10,14},{12... | collective-permute-start | bytes 98312 | tf_op jit(solution)/shard_map/ppermute | solution.py:299
  92.2 5.3 %collective-permute-start.16 = (bf16[128,128]{1,0:T(8,128)(2,1)S(1)}, bf16[128,128]{1,0:T(8,128)(2,1)S(1)}, u32[]{:S(2)}, u32[]{:S(2)}) collective-permute-start(bf16[128,128]{1,0:T(8,128)(2,1)S(1)} %add.34.refs_0_), channel_id=1, source_target_pairs={{0,16},{8,24},{16,0},{24,8},{1,17},{9,25},{17,1},{25,9},{2,18},{10... | collective-permute-start | bytes 98312 | tf_op jit(solution)/shard_map/ppermute | solution.py:304
  94.8 4.6 %collective-permute-start.17 = (bf16[128,128]{1,0:T(8,128)(2,1)S(1)}, bf16[128,128]{1,0:T(8,128)(2,1)S(1)}, u32[]{:S(2)}, u32[]{:S(2)}) collective-permute-start(bf16[128,128]{1,0:T(8,128)(2,1)S(1)} %add.34.refs_0_), channel_id=1, source_target_pairs={{0,8},{8,16},{16,24},{24,0},{1,9},{9,17},{17,25},{25,1},{2,10},{10... | collective-permute-start | bytes 98312 | tf_op jit(solution)/shard_map/ppermute | solution.py:304
  94.8 4.6 %collective-permute-start.18 = (bf16[128,128]{1,0:T(8,128)(2,1)S(1)}, bf16[128,128]{1,0:T(8,128)(2,1)S(1)}, u32[]{:S(2)}, u32[]{:S(2)}) collective-permute-start(bf16[128,128]{1,0:T(8,128)(2,1)S(1)} %add.34.refs_0_), channel_id=1, source_target_pairs={{0,24},{8,0},{16,8},{24,16},{1,25},{9,1},{17,9},{25,17},{2,26},{10... | collective-permute-start | bytes 98312 | tf_op jit(solution)/shard_map/ppermute | solution.py:304
  99.4 3.4 %collective-permute-start.19 = (bf16[128,128]{1,0:T(8,128)(2,1)S(1)}, bf16[128,128]{1,0:T(8,128)(2,1)S(1)}, u32[]{:S(2)}, u32[]{:S(2)}) collective-permute-start(bf16[128,128]{1,0:T(8,128)(2,1)S(1)} %add.35.refs_1_), channel_id=1, source_target_pairs={{0,1},{1,0},{2,3},{3,2},{4,5},{5,4},{6,7},{7,6},{8,9},{9,8},{10,11... | collective-permute-start | bytes 98312 | tf_op jit(solution)/shard_map/ppermute | solution.py:299
